TPU v7x, 256 devices: a whole 4x4x8 slice. The times are simulated.
256 devices in a mesh: side: 2 (over core), grp: 32 (over z, x), tp: 4 (over y).
Axes of the slice: x: 4, y: 4, z: 8, core: 2. Of those that a mesh axis runs over, the one named last changes fastest.
Arguments:
- queries: bfloat16 [128, 32, 128], P('grp', ('side', 'tp')), may hold values from -6 to 6
- new_keys: bfloat16 [128, 32, 128], P('grp', ('side', 'tp')), may hold values from -0.5 to 0.5
- new_values: bfloat16 [128, 32, 128], P('grp', ('side', 'tp')), may hold values from -6 to 6
- kv_memory: float32 [128, 32, 128, 128], P('grp', ('side', 'tp')), may hold values from -0.5 to 0.5
- decay_rate: float32 [32], P(('side', 'tp')), may hold values from 0.3 to 1
- attn_gain: float32 [32, 128], P(('side', 'tp')), may hold values from 0.1 to 1.9
- w_out: bfloat16 [4096, 6144], P(('side', 'tp'), 'grp'), may hold values from -0.09375 to 0.09375
- residual: bfloat16 [128, 6144], P(('side', 'tp'), 'grp'), may hold values from -6 to 6
- moe_gain: float32 [6144], P('grp'), may hold values from 0.1 to 1.9
- w_gate: bfloat16 [32, 6144, 2304], P('grp', None, ('side', 'tp')), may hold values from -0.078125 to 0.078125
- w_up: bfloat16 [32, 6144, 2304], P('grp', None, ('side', 'tp')), may hold values from -0.078125 to 0.078125
- w_down: bfloat16 [32, 2304, 6144], P('grp', ('side', 'tp')), may hold values from -0.09375 to 0.09375
- routes: int32 [128, 2], P(('side', 'tp')), may hold values from 0 to 15, all different within a row; in each aligned block of 16 rows (0 to 15, 16 to 31, ...) at most 4 rows name the same one
- route_weights: float32 [128, 2], P(('side', 'tp')), may hold values from 0.1 to 0.9
Outputs:
- layer_out: bfloat16 [128, 6144], P(('side', 'tp'), 'grp')
Inputs may be any that keep to these rules, and one draw needn't show every extreme that they name: `routes`: each row names two different experts; in each aligned block of 16 rows no expert is named by more than 4 rows.
All inputs are finite; a program needn't handle non-finite values.
Results may differ from a plain program's by a relative error of at most 0.0049.
Values may be sent and summed in bfloat16 or wider, within the bound.
No kernel may reach another device: no remote copies, remote signals or barrier semaphores. Data moves between devices by JAX's collectives and lax.ppermute only.
A program may use at most 64 MiB of HBM per device.

v0:
```python
import jax
import jax.numpy as jnp
from jax import lax
from jax.sharding import PartitionSpec as P

D = 6144
HEADS = 32
HEAD_DIM = 128


epsilon = 1e-06
slot_limit = 4


def routing_tables(routes, route_weights, experts, capacity):
    chosen = routes.reshape(-1)
    labels = jnp.arange(experts, dtype=jnp.int32)
    one_hot = (chosen[:, None] == labels[None, :]).astype(jnp.int32)
    running = jnp.cumsum(one_hot, axis=0) - 1
    slot_of = jnp.sum(one_hot * running, axis=1)
    position = (chosen * capacity + slot_of).reshape(routes.shape)
    ordered = (slot_of * experts + chosen).reshape(routes.shape)
    places = jnp.arange(experts * capacity, dtype=jnp.int32)
    dispatcher = jnp.sum(
        (position[None, :, :] == places[:, None, None]).astype(jnp.float32), axis=2
    )
    combiner = jnp.sum(
        jnp.where(ordered[:, :, None] == places[None, None, :], route_weights[:, :, None], 0.0),
        axis=1,
    )
    return (dispatcher, combiner)


def body(
    queries,
    new_keys,
    new_values,
    kv_memory,
    decay_rate,
    attn_gain,
    w_out,
    residual,
    moe_gain,
    w_gate,
    w_up,
    w_down,
    routes,
    route_weights,
):
    query_f = queries.astype(jnp.float32)
    from_memory = jnp.einsum("shj,shji->shi", query_f, kv_memory, precision=lax.Precision.HIGHEST)
    dot_keys = jnp.sum(query_f * new_keys.astype(jnp.float32), axis=2)
    attended = decay_rate[None, :, None] * from_memory + dot_keys[:, :, None] * new_values.astype(
        jnp.float32
    )
    squares = lax.psum(jnp.sum(attended * attended, axis=(1, 2)), ("side", "tp"))
    inverse_rms = lax.rsqrt(squares / (HEADS * HEAD_DIM) + epsilon)
    head_out = (attended * inverse_rms[:, None, None] * attn_gain[None]).astype(jnp.bfloat16)
    head_out = head_out.reshape(head_out.shape[0], -1)
    projected = jnp.dot(
        lax.all_gather(head_out, "grp", axis=0, tiled=True),
        w_out,
        preferred_element_type=jnp.float32,
    )
    attn_sum = lax.psum_scatter(projected, ("side", "tp"), scatter_dimension=0, tiled=True)
    hidden_state = residual.astype(jnp.float32) + attn_sum
    feature_sq = lax.psum(jnp.sum(hidden_state * hidden_state, axis=1), "grp")
    normed = (
        hidden_state * lax.rsqrt(feature_sq / D + epsilon)[:, None] * moe_gain[None, :]
    ).astype(jnp.bfloat16)
    groups = lax.axis_size("grp")
    experts = groups // 2
    capacity = min(slot_limit, routes.shape[0])
    slice_width = normed.shape[1]
    dispatcher, combiner = routing_tables(routes, route_weights, experts, capacity)
    grouped = jnp.dot(
        dispatcher.astype(jnp.bfloat16), normed, preferred_element_type=jnp.float32
    ).astype(jnp.bfloat16)
    outbox = jnp.repeat(grouped.reshape(experts, capacity, slice_width), 2, axis=0)
    token_rows = lax.all_to_all(outbox, "grp", split_axis=0, concat_axis=2, tiled=True)[0]
    gate_local = w_gate[0]
    up_local = w_up[0]
    down_local = w_down[0]
    block_rows = lax.all_gather(token_rows, ("side", "tp"), axis=0, tiled=True)
    gate_act = jnp.dot(block_rows, gate_local, preferred_element_type=jnp.float32)
    up_act = jnp.dot(block_rows, up_local, preferred_element_type=jnp.float32)
    hidden = (jax.nn.silu(gate_act) * up_act).astype(jnp.bfloat16)
    partial_out = jnp.dot(hidden, down_local, preferred_element_type=jnp.float32)
    expert_sum = lax.psum_scatter(partial_out, ("side", "tp"), scatter_dimension=0, tiled=True)
    returned = lax.all_to_all(
        expert_sum.reshape(capacity, groups, slice_width),
        "grp",
        split_axis=1,
        concat_axis=1,
        tiled=True,
    )
    returned = jnp.sum(returned.reshape(capacity, experts, 2, slice_width), axis=2)
    mixture = jnp.dot(
        combiner, returned.reshape(capacity * experts, slice_width), precision=lax.Precision.HIGHEST
    )
    return (hidden_state + mixture).astype(jnp.bfloat16)


def solution(mesh):
    placed = (
        P("grp", ("side", "tp"), None),
        P("grp", ("side", "tp"), None),
        P("grp", ("side", "tp"), None),
        P("grp", ("side", "tp"), None, None),
        P(("side", "tp")),
        P(("side", "tp"), None),
        P(("side", "tp"), "grp"),
        P(("side", "tp"), "grp"),
        P("grp"),
        P("grp", None, ("side", "tp")),
        P("grp", None, ("side", "tp")),
        P("grp", ("side", "tp"), None),
        P(("side", "tp"), None),
        P(("side", "tp"), None),
    )
    return jax.shard_map(
        body, mesh=mesh, in_specs=placed, out_specs=P(("side", "tp"), "grp"), check_vma=False
    )
```

profile of v0, /device:TPU:1, one launch (start us, length us, event | category | flops | bytes accessed | tf_op | source)
XLA Modules:
  0.0 332.8 jit_solution(12777516439727036931)
XLA Ops:
  6.5 2.0 fusion.25
  9.4 16.6 %psum.14 = f32[4]{0:T(128)S(1)} all-reduce(f32[4]{0:T(128)S(1)} %get-tuple-element.7), channel_id=1, replica_groups=mesh['side'=2,'grp'=32,'tp'=4] {'side','tp'}, use_global_device_ids=true, to_apply=%region_2.0 | all-reduce | flops 4 | bytes 32 | tf_op jit(solution)/shard_map/psum | solution.py:56
  26.8 39.5 %all-gather = bf16[32,4,512]{2,1,0:T(4,128)(2,1)} all-gather(bf16[1,4,512]{2,1,0:T(4,128)(2,1)S(1)} %reshape.46), channel_id=1, replica_groups=mesh['side'=2,'grp'=32,'tp'=4] {'grp'}, dimensions={0}, use_global_device_ids=true | all-gather | bytes 135168 | tf_op jit(solution)/shard_map/all_gather | solution.py:61
  66.2 1.6 reshape.47
  67.8 1.8 fusion.32
  72.5 1.3 select_reduce_fusion.1
  75.9 33.5 %reduce-scatter.2.cloned.1.call-done = f32[16,192]{1,0:T(8,128)} async-done(((f32[128,192]{1,0:T(8,128)}), f32[16,192]{1,0:T(8,128)}) %reduce-scatter.2.cloned.1.call-update) | async-done | bytes 12304 | tf_op jit(solution)/shard_map/reduce_scatter | solution.py:65
  110.3 61.1 %psum.15 = f32[16]{0:T(128)S(1)} all-reduce(f32[16]{0:T(128)S(1)} %multiply_reduce_fusion), channel_id=1, replica_groups=mesh['side'=2,'grp'=32,'tp'=4] {'grp'}, use_global_device_ids=true, to_apply=%region_9.10 | all-reduce | flops 16 | bytes 128 | tf_op jit(solution)/shard_map/psum | solution.py:67
  171.4 1.5 convolution_convert_fusion
  173.0 1.4 reshape.41
  175.1 13.1 %all_to_all.20 = bf16[32,4,192]{2,1,0:T(4,128)(2,1)S(1)} all-to-all(bf16[32,4,192]{2,1,0:T(4,128)(2,1)S(1)} %bitcast.36), channel_id=1, replica_groups=mesh['side'=2,'grp'=32,'tp'=4] {'grp'}, dimensions={0} | all-to-all | bytes 98304 | tf_op jit(solution)/shard_map/all_to_all | solution.py:80
  188.8 1.6 reshape.48
  190.4 39.6 %all-gather.1 = bf16[8,4,6144]{2,1,0:T(4,128)(2,1)} all-gather(bf16[1,4,6144]{2,1,0:T(4,128)(2,1)} %reshape.48), channel_id=1, replica_groups=mesh['side'=2,'grp'=32,'tp'=4] {'side','tp'}, dimensions={0}, use_global_device_ids=true | all-gather | bytes 442368 | tf_op jit(solution)/shard_map/all_gather | solution.py:84
  230.0 1.8 reshape.49
  231.8 3.9 %fusion.5 = f32[32,288]{1,0:T(8,128)} fusion(bf16[32,6144]{1,0:T(8,128)(2,1)} %reshape.49, bf16[1,6144,288]{1,2,0:T(8,128)(2,1)} %param.23), kind=kOutput, calls=%fused_computation.5 | convolution fusion | flops 113246208 | bytes 3969024 | tf_op jit(solution)/shard_map/dot_general | solution.py:85
  235.7 5.7 %fusion.1 = f32[32,6144]{1,0:T(8,128)} fusion(bf16[1,288,6144]{2,1,0:T(8,128)(2,1)S(1)} %copy-done, bf16[32,6144]{1,0:T(8,128)(2,1)} %reshape.49, bf16[1,6144,288]{1,2,0:T(8,128)(2,1)} %param.24, f32[32,288]{1,0:T(8,128)} %fusion.5), kind=kOutput, calls=%fused_computation.1 | convolution fusion | flops 226547712 | bytes 8294400 | tf_op jit(solution)/shard_map/dot_general | solution.py:88
  243.4 56.1 %all-reduce.3.cloned.1.call-done = f32[32,6144]{1,0:T(8,128)} async-done(((f32[32,6144]{1,0:T(8,128)}), f32[32,6144]{1,0:T(8,128)}) %all-reduce.3.cloned.1.call-update) | async-done | bytes 786448
  299.6 1.6 constant_dynamic-slice_fusion
  301.1 1.7 reshape.43
  302.8 1.6 copy.61
  304.4 9.7 %all-to-all-start.1 = ((f32[4,32,192]{2,0,1:T(4,128)}), f32[4,32,192]{2,0,1:T(4,128)}, u32[]{:S(2)}, u32[]{:S(2)}) async-start(f32[4,32,192]{2,0,1:T(4,128)} %copy.61), calls=%async_computation.2 | async-start | bytes 262144 | tf_op jit(solution)/shard_map/all_to_all | solution.py:90
  314.1 1.4 select_reduce_fusion
  315.5 8.1 %all-to-all-done.1 = f32[4,32,192]{2,0,1:T(4,128)} async-done(((f32[4,32,192]{2,0,1:T(4,128)}), f32[4,32,192]{2,0,1:T(4,128)}, u32[]{:S(2)}, u32[]{:S(2)}) %all-to-all-start.1) | async-done | bytes 98336 | tf_op jit(solution)/shard_map/all_to_all | solution.py:90
  324.5 1.5 fusion.13
  (29 shorter events, 11.2 us)
Async XLA Ops:
  6.5 229.2 %copy-start = (bf16[1,288,6144]{2,1,0:T(8,128)(2,1)S(1)}, bf16[1,288,6144]{2,1,0:T(8,128)(2,1)}, u32[]{:S(2)}) copy-start(bf16[1,288,6144]{2,1,0:T(8,128)(2,1)} %param.25) | copy-start | bytes 10616836
  6.5 102.9 %reduce-scatter.2.cloned.1.call-start = ((), (), s32[]{:S(2)}) async-start(), calls=%async_computation.3 | async-start | bytes 147456 | tf_op jit(solution)/shard_map/reduce_scatter | solution.py:65
  69.7 229.9 %all-reduce.3.cloned.1.call-start = ((), (), s32[]{:S(2)}) async-start(), calls=%async_computation.4 | async-start | bytes 1572864
  70.6 0.5 copy-start.2
  235.7 88.8 %copy-start.1 = (f32[16,192]{1,0:T(8,128)S(1)}, f32[16,192]{1,0:T(8,128)}, u32[]{:S(2)}) copy-start(f32[16,192]{1,0:T(8,128)} %reduce-scatter.2.cloned.1.call-done) | copy-start | bytes 36868
  304.4 19.1 %all-to-all-start.1 = ((f32[4,32,192]{2,0,1:T(4,128)}), f32[4,32,192]{2,0,1:T(4,128)}, u32[]{:S(2)}, u32[]{:S(2)}) async-start(f32[4,32,192]{2,0,1:T(4,128)} %copy.61), calls=%async_computation.2 | async-start | bytes 262144 | tf_op jit(solution)/shard_map/all_to_all | solution.py:90
Sparse Core Ops, SparseCore 0:
  69.8 39.5 reduce-scatter.1
  241.6 57.9 all-reduce.2
where the time goes:
time: 335 us; the launch traced here: 333 us
  blocking collectives  170 us (51%)
  waiting for transfers between devices  97.8 us (29%)
  matrix products  16.4 us (5%)
  local copies, waits for them, and re-layouts  16.1 us (5%)
  between operations  14.1 us (4%)
  starting transfers between devices  9.71 us (3%)
  other arithmetic  8.95 us (3%)
    psum x1, blocking collectives, body(): feature_sq = lax.psum(jnp.sum(hidden_state * hidden_state, axis=1), 'grp')  61.1 us
    unnamed x3, waiting for transfers between devices  56.2 us
    all_gather x1, blocking collectives, body(): block_rows = lax.all_gather(token_rows, ('side', 'tp'), axis=0, tiled=True)  39.6 us
    all_gather x1, blocking collectives, body(): lax.all_gather(head_out, 'grp', axis=0, tiled=True)  39.5 us
    reduce_scatter x1, waiting for transfers between devices, body(): lax.psum_scatter(projected, ('side', 'tp'), scatter_dimension=0, tiled=True)  33.5 us
    psum x1, blocking collectives, body(): lax.psum(jnp.sum(attended * attended, axis=(1, 2)), ('side', 'tp'))  16.6 us
    all_to_all x1, blocking collectives, body(): lax.all_to_all(outbox, 'grp', split_axis=0, concat_axis=2, tiled=True)[0]  13.1 us
    all_to_all x1, starting transfers between devices, body(): lax.all_to_all(expert_sum.reshape(capacity, groups, slice_width), 'grp',...  9.66 us
  transfers between devices with their start and end apart: 3, of which 3 were waited for; matrix products, arithmetic and copies ran while one was open for 3% of the time, Pallas kernels for 0%

commit v1 on v0

v1 whole, which is shorter than its diff:
```python
import jax
import jax.numpy as jnp
from jax import lax
from jax.sharding import PartitionSpec as P

D = 6144
HEADS = 32
HEAD_DIM = 128
EXPERTS = 16
CAP = 4
RB = 16
LANES = 256

epsilon = 1e-06
BLOCK = ("side", "tp")


def slots(routes):
    one_hot = (routes[..., None] == jnp.arange(EXPERTS, dtype=jnp.int32)).astype(jnp.float32)
    per_row = jnp.sum(one_hot, axis=2)
    rows = jnp.arange(RB)
    earlier = (rows[:, None] > rows[None, :]).astype(jnp.float32)
    counts = jnp.einsum("rq,bqe->bre", earlier, per_row)
    slot = jnp.sum(one_hot * counts[:, :, None, :], axis=3).astype(jnp.int32)
    return one_hot, slot


def halves(value):
    high = lax.reduce_precision(value, 8, 7)
    return high.astype(jnp.bfloat16), (value - high).astype(jnp.bfloat16)


def body(
    queries,
    new_keys,
    new_values,
    kv_memory,
    decay_rate,
    attn_gain,
    w_out,
    residual,
    moe_gain,
    w_gate,
    w_up,
    w_down,
    routes,
    route_weights,
):
    f32, bf16 = jnp.float32, jnp.bfloat16
    groups = lax.axis_size("grp")
    side = lax.axis_index("side")
    tp = lax.axis_index("tp")
    width = residual.shape[1]

    query_f = queries.astype(f32)
    from_memory = jnp.einsum("shj,shji->shi", query_f, kv_memory, precision=lax.Precision.HIGHEST)
    dot_keys = jnp.sum(query_f * new_keys.astype(f32), axis=2)
    attended = decay_rate[None, :, None] * from_memory + dot_keys[:, :, None] * new_values.astype(f32)
    heads = (attended * attn_gain[None]).astype(bf16).reshape(attended.shape[0], -1)

    sent = jnp.broadcast_to(heads[None], (groups,) + heads.shape)
    every = lax.all_to_all(sent, "grp", 0, 0, tiled=True).reshape(-1, heads.shape[1])

    projected = jnp.dot(every, w_out, preferred_element_type=f32)
    plain = every.astype(f32) / attn_gain.reshape(1, -1)
    high, low = halves(jnp.sum(plain * plain, axis=1, keepdims=True))
    spare = LANES - width - 2
    table = jnp.concatenate(
        [projected.astype(bf16), high, low, jnp.zeros((projected.shape[0], spare), bf16)], axis=1
    )
    half = table.shape[0] // 2
    table = jnp.broadcast_to(table.reshape(2, 1, half, LANES), (2, 4, half, LANES)).reshape(8, half, LANES)
    own = jnp.concatenate([residual, routes.astype(bf16), jnp.zeros((RB, spare), bf16)], axis=1)
    message = jnp.concatenate([table, jnp.broadcast_to(own[None], (8, RB, LANES))], axis=1)
    got = lax.all_to_all(message, BLOCK, 0, 0, tiled=True)
    summed = jnp.sum(got[:, :half].astype(f32), axis=0)
    rest = lax.dynamic_slice(got, (4 * side, half, 0), (4, RB, LANES)).reshape(half, LANES)
    inverse_rms = lax.rsqrt((summed[:, width] + summed[:, width + 1]) / (HEADS * HEAD_DIM) + epsilon)
    hidden_state = rest[:, :width].astype(f32) + inverse_rms[:, None] * summed[:, :width]
    feature_high, feature_low = halves(jnp.sum(hidden_state * hidden_state, axis=1, keepdims=True))
    scaled = (hidden_state * moe_gain[None, :]).astype(bf16)
    rows = jnp.concatenate([scaled, feature_high, feature_low, jnp.zeros((half, spare), bf16)], axis=1)

    side_routes = rest[:, width : width + 2].astype(jnp.int32).reshape(4, RB, 2)
    one_hot, slot = slots(side_routes)
    in_slot = (slot[..., None] == jnp.arange(CAP)).astype(f32)
    dispatcher = jnp.einsum("brke,brkc->becr", one_hot, in_slot).astype(bf16)
    grouped = jnp.einsum(
        "becr,brd->ebcd", dispatcher, rows.reshape(4, RB, LANES), preferred_element_type=f32
    ).astype(bf16)
    outbox = jnp.repeat(grouped.reshape(EXPERTS, 4 * CAP, LANES), 2, axis=0)
    inbox = lax.all_to_all(outbox, "grp", 0, 0, tiled=True)
    both = lax.all_gather(inbox, "side", axis=0)
    feature = jnp.sum(both[..., width : width + 2].astype(f32), axis=(1, 3)).reshape(-1, 1)
    scale = lax.rsqrt(feature / D + epsilon)
    tokens = jnp.transpose(both[..., :width], (0, 2, 1, 3)).reshape(-1, D)

    gate_act = scale * jnp.dot(tokens, w_gate[0], preferred_element_type=f32)
    up_act = scale * jnp.dot(tokens, w_up[0], preferred_element_type=f32)
    hidden = (jax.nn.silu(gate_act) * up_act).astype(bf16)
    partial_out = jnp.dot(hidden, w_down[0], preferred_element_type=f32).astype(bf16)
    parts = lax.all_to_all(partial_out.reshape(8, CAP, D), BLOCK, 0, 0, tiled=True)
    expert_sum = jnp.sum(parts.astype(f32), axis=0)
    back = jnp.transpose(expert_sum.reshape(CAP, groups, width), (1, 0, 2))
    returned = lax.all_to_all(back, "grp", 0, 0, tiled=True)

    own_hot, own_slot = slots(routes[None])
    own_in = (own_slot[..., None] == jnp.arange(CAP)).astype(f32)
    combiner = jnp.einsum("brke,brkc,rk->rec", own_hot, own_in, route_weights, precision=lax.Precision.HIGHEST)
    combiner = jnp.repeat(combiner, 2, axis=1).reshape(RB, -1)
    mixture = jnp.dot(combiner, returned.reshape(-1, width), precision=lax.Precision.HIGHEST)
    own_hidden = lax.dynamic_slice(hidden_state, (RB * tp, 0), (RB, width))
    return (own_hidden + mixture).astype(bf16)


def solution(mesh):
    placed = (
        P("grp", ("side", "tp"), None),
        P("grp", ("side", "tp"), None),
        P("grp", ("side", "tp"), None),
        P("grp", ("side", "tp"), None, None),
        P(("side", "tp")),
        P(("side", "tp"), None),
        P(("side", "tp"), "grp"),
        P(("side", "tp"), "grp"),
        P("grp"),
        P("grp", None, ("side", "tp")),
        P("grp", None, ("side", "tp")),
        P("grp", ("side", "tp"), None),
        P(("side", "tp"), None),
        P(("side", "tp"), None),
    )
    return jax.shard_map(
        body, mesh=mesh, in_specs=placed, out_specs=P(("side", "tp"), "grp"), check_vma=False
    )
```

time: 335 us -> 137 us (0.41)
  blocking collectives: 170 us -> 18.7 us
  waiting for transfers between devices: 97.8 us -> 26 us
  starting transfers between devices: 9.71 us -> 27.4 us
  between operations: 14.1 us -> 0.13 us
  local copies, waits for them, and re-layouts: 16.1 us -> 27.3 us
  other arithmetic: 8.95 us -> 15.7 us
  matrix products: 16.4 us -> 19.9 us
    psum x2 -> x0, blocking collectives: 77.7 us -> none  [the longest x1 61.1 us: body(): feature_sq = lax.psum(jnp.sum(hidden_state * hidden_state, axis=1), 'grp')]
    all_gather x2 -> x1, blocking collectives: 79.1 us -> 4.09 us  [body(): both = lax.all_gather(inbox, 'side', axis=0)]
    unnamed x3 -> x0, waiting for transfers between devices: 56.2 us -> none
    reduce_scatter x1 -> x0, waiting for transfers between devices: 33.5 us -> none  [body(): lax.psum_scatter(projected, ('side', 'tp'), scatter_dimension=0, tiled=True)]
    all_to_all x1 -> x4, waiting for transfers between devices: 8.06 us -> 26 us  [the longest x1 7.37 us: body(): got = lax.all_to_all(message, BLOCK, 0, 0, tiled=True)]
    all_to_all x1 -> x4, starting transfers between devices: 9.66 us -> 27.4 us  [the longest x1 12 us: body(): lax.all_to_all(sent, 'grp', 0, 0, tiled=True).reshape(-1, heads.shape[1])]
    unnamed x13 -> x11, local copies, waits for them, and re-layouts: 9.19 us -> 2.59 us
    convert_element_type x0 -> x7, local copies, waits for them, and re-layouts: none -> 5.25 us  [the longest x4 3.54 us: halves(): return (high.astype(jnp.bfloat16), (value - high).astype(jnp.bfloat16))]
  transfers between devices with their start and end apart: 3 -> 4, of which waited for: 3 -> 4; matrix products, arithmetic and copies ran while one was open for 3% -> 6% of each run, Pallas kernels for 0% -> 0%
where the time goes in v1:
time: 137 us; the launch traced here: 135 us
  starting transfers between devices  27.4 us (20%)
  local copies, waits for them, and re-layouts  27.3 us (20%)
  waiting for transfers between devices  26 us (19%)
  matrix products  19.9 us (15%)
  blocking collectives  18.7 us (14%)
  other arithmetic  15.7 us (11%)
    all_to_all x1, blocking collectives, body(): inbox = lax.all_to_all(outbox, 'grp', 0, 0, tiled=True)  14.6 us
    all_to_all x1, starting transfers between devices, body(): lax.all_to_all(sent, 'grp', 0, 0, tiled=True).reshape(-1, heads.shape[1])  12 us
    all_to_all x1, waiting for transfers between devices, body(): got = lax.all_to_all(message, BLOCK, 0, 0, tiled=True)  7.37 us
    all_to_all x1, waiting for transfers between devices, body(): returned = lax.all_to_all(back, 'grp', 0, 0, tiled=True)  6.7 us
    all_to_all x1, waiting for transfers between devices, body(): lax.all_to_all(sent, 'grp', 0, 0, tiled=True).reshape(-1, heads.shape[1])  6.56 us
    all_to_all x1, starting transfers between devices, body(): got = lax.all_to_all(message, BLOCK, 0, 0, tiled=True)  6.52 us
    dot_general x1, matrix products, body(): jnp.dot(hidden, w_down[0], preferred_element_type=f32).astype(bf16)  5.55 us
    all_to_all x1, waiting for transfers between devices, body(): lax.all_to_all(partial_out.reshape(8, CAP, D), BLOCK, 0, 0, tiled=True)  5.38 us
  transfers between devices with their start and end apart: 4, of which 4 were waited for; matrix products, arithmetic and copies ran while one was open for 6% of the time, Pallas kernels for 0%

profile of v1, /device:TPU:1, one launch (start us, length us, event | category | flops | bytes accessed | tf_op | source)
XLA Modules:
  0.0 135.2 jit_solution(5997559962275714157)
XLA Ops:
  0.0 2.0 %fusion.53 = f32[4,4,1,128]{3,2,1,0:T(1,128)S(1)} fusion(f32[4,4,128,128]{3,2,1,0:T(8,128)} %param.17, bf16[4,4,128,1]{2,1,0,3:T(4,128)(2,1)} %bitcast.87), kind=kOutput, calls=%fused_computation.71 | convolution fusion | flops 3145728 | bytes 1060864 | tf_op jit(solution)/shard_map/shj,shji->shi/dot_general | solution.py:56
  3.5 12.0 %all-to-all-start = ((bf16[32,4,512]{2,1,0:T(4,128)(2,1)}), bf16[32,4,512]{2,1,0:T(4,128)(2,1)}, u32[]{:S(2)}, u32[]{:S(2)}) async-start(bf16[32,4,512]{2,1,0:T(4,128)(2,1)} %broadcast_in_dim.21), calls=%async_computation | async-start | bytes 262144 | tf_op jit(solution)/shard_map/all_to_all | solution.py:62
  18.3 6.6 %all-to-all-done = bf16[32,4,512]{2,1,0:T(4,128)(2,1)} async-done(((bf16[32,4,512]{2,1,0:T(4,128)(2,1)}), bf16[32,4,512]{2,1,0:T(4,128)(2,1)}, u32[]{:S(2)}, u32[]{:S(2)}) %all-to-all-start) | async-done | bytes 131104 | tf_op jit(solution)/shard_map/all_to_all | solution.py:62
  24.8 1.6 %multiply_reduce_fusion = f32[32,4]{0,1:T(4,128)} fusion(bf16[32,4,512]{2,1,0:T(4,128)(2,1)} %all-to-all-done, f32[512]{0:T(512)} %bitcast.90), kind=kLoop, calls=%fused_computation.29 | loop fusion | flops 262016 | bytes 133632 | tf_op jit(solution)/shard_map/reduce_sum | solution.py:66
  28.5 1.6 %reshape.187 = bf16[128,512]{1,0:T(8,128)(2,1)} reshape(bf16[32,4,512]{2,1,0:T(4,128)(2,1)} %all-to-all-done) | data formatting | bytes 262144 | tf_op jit(solution)/shard_map/reshape | solution.py:62
  30.1 1.8 %convolution_convert_fusion.3 = bf16[128,192]{0,1:T(8,128)(2,1)} fusion(bf16[128,512]{1,0:T(8,128)(2,1)} %reshape.187, bf16[512,192]{0,1:T(8,128)(2,1)} %param.20), kind=kOutput, calls=%fused_computation.9 | convolution fusion | flops 25190400 | bytes 376832 | tf_op jit(solution)/shard_map/dot_general | solution.py:64
  37.3 6.5 %all-to-all-start.1 = ((bf16[8,80,256]{2,1,0:T(8,128)(2,1)}), bf16[8,80,256]{2,1,0:T(8,128)(2,1)}, u32[]{:S(2)}, u32[]{:S(2)}) async-start(bf16[8,80,256]{2,1,0:T(8,128)(2,1)} %pad_maximum_fusion), calls=%async_computation.1 | async-start | bytes 655360 | tf_op jit(solution)/shard_map/all_to_all | solution.py:75
  43.9 7.4 %all-to-all-done.1 = bf16[8,80,256]{2,1,0:T(8,128)(2,1)} async-done(((bf16[8,80,256]{2,1,0:T(8,128)(2,1)}), bf16[8,80,256]{2,1,0:T(8,128)(2,1)}, u32[]{:S(2)}, u32[]{:S(2)}) %all-to-all-start.1) | async-done | bytes 327712 | tf_op jit(solution)/shard_map/all_to_all | solution.py:75
  65.2 14.6 %all_to_all.25 = bf16[32,16,256]{2,1,0:T(8,128)(2,1)S(1)} all-to-all(bf16[32,16,256]{2,1,0:T(8,128)(2,1)S(1)} %bitcast.76), channel_id=1, replica_groups=mesh['side'=2,'grp'=32,'tp'=4] {'grp'}, dimensions={0} | all-to-all | bytes 524288 | tf_op jit(solution)/shard_map/all_to_all | solution.py:92
  79.9 4.1 %all-gather = bf16[64,16,256]{2,1,0:T(8,128)(2,1)S(1)} all-gather(bf16[32,16,256]{2,1,0:T(8,128)(2,1)S(1)} %all_to_all.25), channel_id=2, replica_groups=mesh['side'=2,'grp'=32,'tp'=4] {'side'}, dimensions={0}, use_global_device_ids=true | all-gather | bytes 786432 | tf_op jit(solution)/shard_map/all_gather | solution.py:93
  85.2 2.4 %reshape.192 = bf16[32,6144]{1,0:T(8,128)(2,1)} reshape(bf16[2,16,32,192]{3,2,1,0:T(8,128)(2,1)} %copy.184) | data formatting | bytes 786432 | tf_op jit(solution)/shard_map/reshape | solution.py:96
  87.7 3.9 %fusion.7 = f32[32,288]{1,0:T(8,128)} fusion(bf16[32,6144]{1,0:T(8,128)(2,1)} %reshape.192, bf16[1,6144,288]{1,2,0:T(8,128)(2,1)} %param.23, f32[32]{0:T(128)S(1)} %rsqrt.17), kind=kOutput, calls=%fused_computation.11 | convolution fusion | flops 113255424 | bytes 3969152 | tf_op jit(solution)/shard_map/dot_general | solution.py:98
  91.6 5.5 %convolution_convert_fusion = bf16[32,6144]{1,0:T(8,128)(2,1)} fusion(bf16[1,288,6144]{2,1,0:T(8,128)(2,1)S(1)} %copy-done, bf16[32,6144]{1,0:T(8,128)(2,1)} %reshape.192, bf16[1,6144,288]{1,2,0:T(8,128)(2,1)} %param.24, f32[32,288]{1,0:T(8,128)} %fusion.7, f32[32]{0:T(128)S(1)} %rsqrt.17), kind=kOutput, calls=%fused_computation.1 | convolution fusion | flops 226753536 | bytes 7901312 | tf_op jit(solution)/shard_map/dot_general | solution.py:101
  97.2 1.9 %reshape.193 = bf16[8,4,6144]{2,1,0:T(4,128)(2,1)} reshape(bf16[32,6144]{1,0:T(8,128)(2,1)} %convolution_convert_fusion) | data formatting | bytes 786432 | tf_op jit(solution)/shard_map/reshape | solution.py:102
  99.1 4.4 %all-to-all-start.3 = ((bf16[8,4,6144]{2,1,0:T(4,128)(2,1)}), bf16[8,4,6144]{2,1,0:T(4,128)(2,1)}, u32[]{:S(2)}, u32[]{:S(2)}) async-start(bf16[8,4,6144]{2,1,0:T(4,128)(2,1)} %reshape.193), calls=%async_computation.3 | async-start | bytes 786432 | tf_op jit(solution)/shard_map/all_to_all | solution.py:102
  106.1 5.4 %all-to-all-done.3 = bf16[8,4,6144]{2,1,0:T(4,128)(2,1)} async-done(((bf16[8,4,6144]{2,1,0:T(4,128)(2,1)}), bf16[8,4,6144]{2,1,0:T(4,128)(2,1)}, u32[]{:S(2)}, u32[]{:S(2)}) %all-to-all-start.3) | async-done | bytes 393248 | tf_op jit(solution)/shard_map/all_to_all | solution.py:102
  111.5 1.8 %convert_reduce_fusion = f32[4,6144]{1,0:T(4,128)} fusion(bf16[8,4,6144]{2,1,0:T(4,128)(2,1)} %all-to-all-done.3), kind=kLoop, calls=%fused_computation.24 | loop fusion | flops 368640 | bytes 491520 | tf_op jit(solution)/shard_map/reduce_sum | solution.py:103
  113.3 1.6 %reshape.194 = f32[4,32,192]{2,1,0:T(8,128)} reshape(f32[4,6144]{1,0:T(4,128)} %convert_reduce_fusion) | data formatting | bytes 196608 | tf_op jit(solution)/shard_map/reshape | solution.py:104
  115.0 1.6 %copy.185 = f32[32,4,192]{2,1,0:T(4,128)} copy(f32[32,4,192]{2,0,1:T(8,128)} %bitcast.77) | data formatting | bytes 196608 | tf_op jit(solution)/shard_map/transpose | solution.py:104
  116.6 4.6 %all-to-all-start.4 = ((f32[32,4,192]{2,1,0:T(4,128)}), f32[32,4,192]{2,1,0:T(4,128)}, u32[]{:S(2)}, u32[]{:S(2)}) async-start(f32[32,4,192]{2,1,0:T(4,128)} %copy.185), calls=%async_computation.4 | async-start | bytes 262144 | tf_op jit(solution)/shard_map/all_to_all | solution.py:105
  121.2 1.7 %fusion.47 = f32[16,16,4]{1,2,0:T(4,128)} fusion(f32[16,2]{1,0:T(8,128)S(1)} %copy.174, s32[16,2]{1,0:T(8,128)S(1)} %copy.173, s32[16,2]{1,0:T(8,128)} %copy.171), kind=kOutput, calls=%fused_computation.60 | convolution fusion | flops 25344 | bytes 4480 | tf_op jit(solution)/shard_map/brke,brkc,rk->rec/dot_general | solution.py:109
  124.3 6.7 %all-to-all-done.4 = f32[32,4,192]{2,1,0:T(4,128)} async-done(((f32[32,4,192]{2,1,0:T(4,128)}), f32[32,4,192]{2,1,0:T(4,128)}, u32[]{:S(2)}, u32[]{:S(2)}) %all-to-all-start.4) | async-done | bytes 98336 | tf_op jit(solution)/shard_map/all_to_all | solution.py:105
  131.0 1.6 %reshape.195 = f32[128,192]{1,0:T(8,128)} reshape(f32[32,4,192]{2,1,0:T(4,128)} %all-to-all-done.4) | data formatting | bytes 196608 | tf_op jit(solution)/shard_map/reshape | solution.py:111
  133.4 1.8 %fusion.19 = bf16[16,192]{1,0:T(8,128)(2,1)} fusion(f32[16,128]{0,1:T(8,128)S(1)} %bitcast.83, f32[128,192]{1,0:T(8,128)} %reshape.195, f32[64,192]{1,0:T(8,128)} %copy-done.1, s32[]{:T(128)S(6)} %select_n.7), kind=kOutput, calls=%fused_computation.17 | convolution fusion | flops 4724736 | bytes 124932 | tf_op jit(solution)/shard_map/dot_general | solution.py:111
  (60 shorter events, 31.9 us)
Async XLA Ops:
  0.0 91.6 %copy-start = (bf16[1,288,6144]{2,1,0:T(8,128)(2,1)S(1)}, bf16[1,288,6144]{2,1,0:T(8,128)(2,1)}, u32[]{:S(2)}) copy-start(bf16[1,288,6144]{2,1,0:T(8,128)(2,1)} %param.25) | copy-start | bytes 10616836
  3.5 21.3 %all-to-all-start = ((bf16[32,4,512]{2,1,0:T(4,128)(2,1)}), bf16[32,4,512]{2,1,0:T(4,128)(2,1)}, u32[]{:S(2)}, u32[]{:S(2)}) async-start(bf16[32,4,512]{2,1,0:T(4,128)(2,1)} %broadcast_in_dim.21), calls=%async_computation | async-start | bytes 262144 | tf_op jit(solution)/shard_map/all_to_all | solution.py:62
  16.4 0.5 copy-start.3
  37.3 13.9 %all-to-all-start.1 = ((bf16[8,80,256]{2,1,0:T(8,128)(2,1)}), bf16[8,80,256]{2,1,0:T(8,128)(2,1)}, u32[]{:S(2)}, u32[]{:S(2)}) async-start(bf16[8,80,256]{2,1,0:T(8,128)(2,1)} %pad_maximum_fusion), calls=%async_computation.1 | async-start | bytes 655360 | tf_op jit(solution)/shard_map/all_to_all | solution.py:75
  55.2 0.6 copy-start.1
  91.6 11.8 %copy-start.2 = (s32[16,2]{0,1:T(2,128)S(1)}, s32[16,2]{0,1:T(2,128)}, u32[]{:S(2)}) copy-start(s32[16,2]{0,1:T(2,128)} %param.26) | copy-start | bytes 388
  99.1 12.4 %all-to-all-start.3 = ((bf16[8,4,6144]{2,1,0:T(4,128)(2,1)}), bf16[8,4,6144]{2,1,0:T(4,128)(2,1)}, u32[]{:S(2)}, u32[]{:S(2)}) async-start(bf16[8,4,6144]{2,1,0:T(4,128)(2,1)} %reshape.193), calls=%async_computation.3 | async-start | bytes 786432 | tf_op jit(solution)/shard_map/all_to_all | solution.py:102
  116.6 14.4 %all-to-all-start.4 = ((f32[32,4,192]{2,1,0:T(4,128)}), f32[32,4,192]{2,1,0:T(4,128)}, u32[]{:S(2)}, u32[]{:S(2)}) async-start(f32[32,4,192]{2,1,0:T(4,128)} %copy.185), calls=%async_computation.4 | async-start | bytes 262144 | tf_op jit(solution)/shard_map/all_to_all | solution.py:105

commit v2 on v1

v2 whole, which is shorter than its diff:
```python
import functools
import jax
import jax.numpy as jnp
from jax import lax
from jax.experimental import pallas as pl
from jax.experimental.pallas import tpu as pltpu
from jax.sharding import PartitionSpec as P

D = 6144
HEADS = 32
HEAD_DIM = 128
EXPERTS = 16
CAP = 4
RB = 16
LANES = 256

epsilon = 1e-06
BLOCK = ("side", "tp")
f32, bf16 = jnp.float32, jnp.bfloat16
VM = pl.BlockSpec(memory_space=pltpu.VMEM)
SM = pl.BlockSpec(memory_space=pltpu.SMEM)
MINOR = (((1,), (1,)), ((), ()))


def iota(shape, dim):
    return lax.broadcasted_iota(jnp.int32, shape, dim)


def column(row, size):
    full = jnp.broadcast_to(row, (size, size))
    return jnp.sum(jnp.where(iota((size, size), 0) == iota((size, size), 1), full, 0.0), axis=1, keepdims=True)


def halves(value):
    high = value.astype(bf16).astype(f32)
    return high, value - high


def attention(q_ref, k_ref, v_ref, kv_ref, decay_ref, gain_ref, out_ref):
    sessions, heads = q_ref.shape[:2]
    query = jnp.concatenate([q_ref[s].astype(f32) for s in range(sessions)], axis=0)
    key = jnp.concatenate([k_ref[s].astype(f32) for s in range(sessions)], axis=0)
    value = jnp.concatenate([v_ref[s].astype(f32) for s in range(sessions)], axis=0)
    turned = jnp.transpose(query)
    dots = jnp.sum(query * key, axis=1, keepdims=True)
    rows = []
    for s in range(sessions):
        for h in range(heads):
            n = s * heads + h
            read = jnp.sum(turned[:, n : n + 1] * kv_ref[s, h], axis=0, keepdims=True)
            rows.append(decay_ref[h] * read)
    attended = jnp.concatenate(rows, axis=0) + dots * value
    gain = jnp.concatenate([gain_ref[...]] * sessions, axis=0)
    message = (attended * gain).astype(bf16)
    for g in range(out_ref.shape[0]):
        out_ref[g] = message


def project(x_ref, w_ref, gain_ref, residual_ref, routes_ref, out_ref, spread_ref):
    heads = gain_ref.shape[0]
    width = w_ref.shape[0]
    total = x_ref.shape[0] * x_ref.shape[1]
    sessions = total // heads
    half = sessions // 2
    spread_ref[...] = x_ref[...].reshape(total, HEAD_DIM).astype(f32)
    lane = iota((1, LANES), 1)
    squares = jnp.zeros((sessions, 1), f32)
    parts = []
    for h in range(heads):
        x = spread_ref[pl.ds(h, sessions, stride=heads), :]
        plain = x / gain_ref[h : h + 1, :]
        squares = squares + jnp.sum(plain * plain, axis=1, keepdims=True)
        parts.append(x.astype(bf16))
    projected = lax.dot_general(jnp.concatenate(parts, axis=1), w_ref[...], MINOR, preferred_element_type=f32)
    high, low = halves(squares)
    pad = jnp.zeros((sessions, LANES - width), f32)
    table = jnp.concatenate([projected, pad], axis=1)
    table = jnp.where(lane == width, high, jnp.where(lane == width + 1, low, table)).astype(bf16)
    routes = routes_ref[...].astype(f32)
    own = jnp.concatenate([residual_ref[...].astype(f32), pad[:RB]], axis=1)
    own = jnp.where(lane == width, column(routes[0:1], RB), jnp.where(lane == width + 1, column(routes[1:2], RB), own))
    own = own.astype(bf16)
    for b in range(8):
        out_ref[b, :half, :] = table[:half] if b < 4 else table[half:]
        out_ref[b, half:, :] = own


def dispatch(x_ref, gain_ref, out_ref, own_ref, scratch_ref):
    width = gain_ref.shape[1]
    half = x_ref.shape[1] - RB
    side, tp, odd = lax.axis_index("side"), lax.axis_index("tp"), lax.rem(lax.axis_index("grp"), 2)
    lane = iota((1, LANES), 1)
    summed = x_ref[0, :half, :].astype(f32)
    for b in range(1, 8):
        summed = summed + x_ref[b, :half, :].astype(f32)
    squares = jnp.sum(jnp.where((lane == width) | (lane == width + 1), summed, 0.0), axis=1, keepdims=True)
    rest = jnp.concatenate([x_ref[4 * side + i, half:, :].astype(f32) for i in range(4)], axis=0)
    hidden = jnp.where(lane < width, rest + lax.rsqrt(squares / (HEADS * HEAD_DIM) + epsilon) * summed, 0.0)
    scratch_ref[...] = hidden
    own_ref[...] = scratch_ref[pl.ds(pl.multiple_of(tp * RB, RB), RB), :]
    high, low = halves(jnp.sum(hidden * hidden, axis=1, keepdims=True))
    gain = jnp.concatenate([gain_ref[...], jnp.zeros((1, LANES - width), f32)], axis=1)
    rows = jnp.where(lane == width, high, jnp.where(lane == width + 1, low, hidden * gain))
    rows = jnp.where(odd == 1, pltpu.roll(rows, LANES - width, 1), rows).astype(bf16)

    first = jnp.sum(jnp.where(lane == width, rest, 0.0), axis=1, keepdims=True).astype(jnp.int32)
    second = jnp.sum(jnp.where(lane == width + 1, rest, 0.0), axis=1, keepdims=True).astype(jnp.int32)
    places = EXPERTS * 4 * CAP
    place = iota((1, places), 1)
    expert = place // (4 * CAP)
    chosen = jnp.where((first == expert) | (second == expert), 1.0, 0.0)
    r, c = iota((half, half), 0), iota((half, half), 1)
    earlier = jnp.where((r // RB == c // RB) & (c < r), 1.0, 0.0).astype(bf16)
    slot = jnp.dot(earlier, chosen.astype(bf16), preferred_element_type=f32)
    block = iota((half, 1), 0) // RB
    here = (slot == (place % CAP).astype(f32)) & (block == place // CAP % 4)
    table = jnp.transpose(jnp.where(here, chosen, 0.0)).astype(bf16)
    routed = jnp.dot(table, rows, preferred_element_type=f32).astype(bf16)
    for e in range(EXPERTS):
        piece = routed[e * 4 * CAP : (e + 1) * 4 * CAP]
        out_ref[2 * e] = piece
        out_ref[2 * e + 1] = piece


def experts(mine_ref, other_ref, gate_ref, up_ref, down_ref, out_ref, x_ref, feature_ref):
    groups, rows, _ = mine_ref.shape
    side = lax.axis_index("side")
    low_lane = iota((rows, 128), 1) < 64
    for ref, at in ((mine_ref, side), (other_ref, 1 - side)):
        start = pl.multiple_of(at * rows, rows)
        feature = jnp.zeros((rows, 128), f32)
        for i in range(groups // 2):
            b_even = ref[2 * i, :, 128:].astype(f32)
            b_odd = ref[2 * i + 1, :, :128].astype(f32)
            feature = feature + jnp.where(low_lane, b_odd, b_even)
            x_ref[pl.ds(start, rows), 384 * i : 384 * i + 128] = ref[2 * i, :, :128]
            x_ref[pl.ds(start, rows), 384 * i + 128 : 384 * i + 256] = jnp.where(low_lane, b_even, b_odd).astype(bf16)
            x_ref[pl.ds(start, rows), 384 * i + 256 : 384 * i + 384] = ref[2 * i + 1, :, 128:]
        feature_ref[pl.ds(start, rows), :] = feature
    scale = lax.rsqrt(jnp.sum(feature_ref[...], axis=1, keepdims=True) / D + epsilon)
    x = x_ref[...]
    gate = scale * lax.dot_general(x, gate_ref[...], MINOR, preferred_element_type=f32)
    up = scale * lax.dot_general(x, up_ref[...], MINOR, preferred_element_type=f32)
    hidden = (gate * jax.nn.sigmoid(gate) * up).astype(bf16)
    span = out_ref.shape[2]
    chunks = [
        jnp.dot(hidden, down_ref[:, q * span : (q + 1) * span], preferred_element_type=f32) for q in range(4)
    ]
    for b in range(8):
        piece = jnp.concatenate([chunk[b * CAP : (b + 1) * CAP] for chunk in chunks], axis=0)
        out_ref[b] = piece.astype(bf16)


def reduce_parts(x_ref, out_ref):
    total = x_ref[0].astype(f32)
    for b in range(1, 8):
        total = total + x_ref[b].astype(f32)
    for q in range(4):
        rows = total[q * CAP : (q + 1) * CAP]
        for i in range(4):
            a, b, c = (rows[:, 384 * i + 128 * n : 384 * i + 128 * (n + 1)] for n in range(3))
            out_ref[q * 8 + 2 * i] = jnp.concatenate([a, b], axis=0)
            out_ref[q * 8 + 2 * i + 1] = jnp.concatenate([b, c], axis=0)


def combiner(routes_ref, weights_ref, a_ref, b_ref):
    routes, weights = routes_ref[...].astype(f32), weights_ref[...]
    r0, r1 = column(routes[0:1], RB).astype(jnp.int32), column(routes[1:2], RB).astype(jnp.int32)
    w0, w1 = column(weights[0:1], RB), column(weights[1:2], RB)
    place = iota((1, 256), 1)
    expert = place // 16
    chosen = jnp.where((r0 == expert) | (r1 == expert), 1.0, 0.0)
    earlier = jnp.where(iota((RB, RB), 1) < iota((RB, RB), 0), 1.0, 0.0)
    slot = jnp.dot(earlier, chosen, preferred_element_type=f32)
    weight = jnp.where(r0 == expert, w0, 0.0) + jnp.where(r1 == expert, w1, 0.0)
    row = (place % 8).astype(f32)
    a_ref[...] = jnp.where(slot == row, weight, 0.0)
    b_ref[...] = jnp.where(slot + CAP == row, weight, 0.0)


def combine(x_ref, a_ref, b_ref, own_ref, out_ref):
    odd = lax.rem(lax.axis_index("grp"), 2)
    width = out_ref.shape[1]
    x = x_ref[...].reshape(-1, 128)
    table = jnp.concatenate([a_ref[...], b_ref[...]], axis=0)
    both = jnp.dot(table, x, precision=lax.Precision.HIGHEST, preferred_element_type=f32)
    mixture = jnp.concatenate([both[:RB], both[RB:]], axis=1)
    mixture = jnp.where(odd == 1, pltpu.roll(mixture, width, 1), mixture)
    out_ref[...] = (own_ref[...] + mixture)[:, :width].astype(bf16)


def call(kernel, outs, specs, args, scratch=(), flops=0, moved=0):
    single = not isinstance(outs, list)
    shapes = [outs] if single else outs
    made = pl.pallas_call(
        kernel,
        out_shape=outs if single else tuple(outs),
        in_specs=specs,
        out_specs=VM if single else tuple(VM for _ in shapes),
        scratch_shapes=list(scratch),
        compiler_params=pltpu.CompilerParams(vmem_limit_bytes=48 * 1024 * 1024),
        cost_estimate=pl.CostEstimate(flops=flops, bytes_accessed=moved, transcendentals=0),
    )
    return made(*args)


def shape(dims, dtype):
    return jax.ShapeDtypeStruct(dims, dtype)


def body(
    queries,
    new_keys,
    new_values,
    kv_memory,
    decay_rate,
    attn_gain,
    w_out,
    residual,
    moe_gain,
    w_gate,
    w_up,
    w_down,
    routes,
    route_weights,
):
    groups = lax.axis_size("grp")
    width = residual.shape[1]
    sessions, heads = queries.shape[:2]
    half = groups * sessions // 2
    turned_routes = routes.T

    comb_a, comb_b = call(
        combiner, [shape((RB, 256), f32)] * 2, [VM, VM], (turned_routes, route_weights.T), flops=10**6, moved=40000
    )
    sent = call(
        attention,
        shape((groups, sessions * heads, HEAD_DIM), bf16),
        [VM, VM, VM, VM, SM, VM],
        (queries, new_keys, new_values, kv_memory, decay_rate, attn_gain),
        flops=10**6,
        moved=1200000,
    )
    every = lax.all_to_all(sent, "grp", 0, 0, tiled=True)
    message = call(
        project,
        shape((8, half + RB, LANES), bf16),
        [VM] * 5,
        (every, w_out.T, attn_gain, residual, turned_routes),
        scratch=[pltpu.VMEM((groups * sessions * heads, HEAD_DIM), f32)],
        flops=25 * 10**6,
        moved=700000,
    )
    got = lax.all_to_all(message, BLOCK, 0, 0, tiled=True)
    outbox, own_hidden = call(
        dispatch,
        [shape((groups, 4 * CAP, LANES), bf16), shape((RB, LANES), f32)],
        [VM, VM],
        (got, moe_gain.reshape(1, -1)),
        scratch=[pltpu.VMEM((half, LANES), f32)],
        flops=10**7,
        moved=700000,
    )
    inbox = lax.all_to_all(outbox, "grp", 0, 0, tiled=True)
    other = lax.ppermute(inbox, "side", [(0, 1), (1, 0)])
    partial_out = call(
        experts,
        shape((8, 4 * CAP, D // 4), bf16),
        [VM] * 5,
        (inbox, other, w_gate[0].T, w_up[0].T, w_down[0]),
        scratch=[pltpu.VMEM((8 * CAP, D), bf16), pltpu.VMEM((8 * CAP, 128), f32)],
        flops=4 * 10**8,
        moved=11000000,
    )
    parts = lax.all_to_all(partial_out, BLOCK, 0, 0, tiled=True)
    back = call(reduce_parts, shape((groups, 2 * CAP, 128), f32), [VM], (parts,), flops=10**6, moved=600000)
    returned = lax.all_to_all(back, "grp", 0, 0, tiled=True)
    return call(
        combine,
        shape((RB, width), bf16),
        [VM] * 4,
        (returned, comb_a, comb_b, own_hidden),
        flops=10**7,
        moved=200000,
    )


def solution(mesh):
    placed = (
        P("grp", ("side", "tp"), None),
        P("grp", ("side", "tp"), None),
        P("grp", ("side", "tp"), None),
        P("grp", ("side", "tp"), None, None),
        P(("side", "tp")),
        P(("side", "tp"), None),
        P(("side", "tp"), "grp"),
        P(("side", "tp"), "grp"),
        P("grp"),
        P("grp", None, ("side", "tp")),
        P("grp", None, ("side", "tp")),
        P("grp", ("side", "tp"), None),
        P(("side", "tp"), None),
        P(("side", "tp"), None),
    )
    return jax.shard_map(
        body, mesh=mesh, in_specs=placed, out_specs=P(("side", "tp"), "grp"), check_vma=False
    )
```

time: 137 us -> 94.9 us (0.69)
  blocking collectives: 18.7 us -> 60.3 us
  starting transfers between devices: 27.4 us -> 6.18 us
  matrix products: 19.9 us -> 0 us
  local copies, waits for them, and re-layouts: 27.3 us -> 7.76 us
  other arithmetic: 15.7 us -> 0 us
  waiting for transfers between devices: 26 us -> 10.8 us
  Pallas kernels: 0 us -> 9.31 us
    all_to_all x0 -> x3, blocking collectives: none -> 45.7 us  [the longest x1 21 us: body(): every = lax.all_to_all(sent, 'grp', 0, 0, tiled=True)]
    all_to_all x3 -> x0, starting transfers between devices: 22.9 us -> none  [the longest x1 12 us: body(): lax.all_to_all(sent, 'grp', 0, 0, tiled=True).reshape(-1, heads.shape[1])]
    dot_general x10 -> x0, matrix products: 19.9 us -> none  [the longest x1 5.55 us: body(): jnp.dot(hidden, w_down[0], preferred_element_type=f32).astype(bf16)]
    all_to_all x3 -> x0, waiting for transfers between devices: 19.3 us -> none  [the longest x1 7.37 us: body(): got = lax.all_to_all(message, BLOCK, 0, 0, tiled=True)]
    pallas_call x0 -> x7, Pallas kernels: none -> 9.31 us  [call(): return made(*args)]
    reshape x6 -> x0, local copies, waits for them, and re-layouts: 9.21 us -> none  [the longest x1 2.44 us: body(): tokens = jnp.transpose(both[..., :width], (0, 2, 1, 3)).reshape(-1, D)]
    reduce_sum x9 -> x0, other arithmetic: 7.62 us -> none  [the longest x2 1.87 us: slots(): slot = jnp.sum(one_hot * counts[:, :, None, :], axis=3).astype(jnp.int32)]
    convert_element_type x7 -> x0, local copies, waits for them, and re-layouts: 5.25 us -> none  [the longest x4 3.54 us: halves(): return (high.astype(jnp.bfloat16), (value - high).astype(jnp.bfloat16))]
  transfers between devices with their start and end apart: 4 -> 2, of which waited for: 4 -> 2; matrix products, arithmetic and copies ran while one was open for 6% -> 0% of each run, Pallas kernels for 0% -> 0%
where the time goes in v2:
time: 94.9 us; the launch traced here: 94.4 us
  blocking collectives  60.3 us (64%)
  waiting for transfers between devices  10.8 us (11%)
  Pallas kernels  9.31 us (10%)
  local copies, waits for them, and re-layouts  7.76 us (8%)
  starting transfers between devices  6.18 us (7%)
    all_to_all x1, blocking collectives, body(): every = lax.all_to_all(sent, 'grp', 0, 0, tiled=True)  21 us
    all_to_all x1, blocking collectives, body(): inbox = lax.all_to_all(outbox, 'grp', 0, 0, tiled=True)  14.6 us
    all_to_all x1, blocking collectives, body(): got = lax.all_to_all(message, BLOCK, 0, 0, tiled=True)  13.9 us
    all_to_all x1, blocking collectives, body(): parts = lax.all_to_all(partial_out, BLOCK, 0, 0, tiled=True)  10.7 us
    all_to_all x1, waiting for transfers between devices, body(): returned = lax.all_to_all(back, 'grp', 0, 0, tiled=True)  9.61 us
    pallas_call x7, Pallas kernels, call(): return made(*args)  9.31 us
    unnamed x26, local copies, waits for them, and re-layouts  7.76 us
    all_to_all x1, starting transfers between devices, body(): returned = lax.all_to_all(back, 'grp', 0, 0, tiled=True)  3.85 us
  transfers between devices with their start and end apart: 2, of which 2 were waited for; matrix products, arithmetic and copies ran while one was open for 0% of the time, Pallas kernels for 0%

profile of v2, /device:TPU:1, one launch (start us, length us, event | category | flops | bytes accessed | tf_op | source)
XLA Modules:
  0.0 94.4 jit_solution(11736906538326781697)
XLA Ops:
  0.0 1.4 %copy-done.1 = f32[4,4,128,128]{3,2,1,0:T(8,128)S(1)} copy-done((f32[4,4,128,128]{3,2,1,0:T(8,128)S(1)}, f32[4,4,128,128]{3,2,1,0:T(8,128)}, u32[]{:S(2)}) %copy-start.1) | copy-done | bytes 1048600
  1.4 0.7 copy-done.3
  2.1 0.7 copy-done.5
  2.8 0.7 copy-done.6
  3.4 0.7 copy-done.7
  4.1 0.7 copy-done.11
  4.8 0.9 shard_map.136
  5.7 21.0 %all_to_all.25.x_ref = bf16[32,16,128]{2,1,0:T(8,128)(2,1)S(1)} all-to-all(bf16[32,16,128]{2,1,0:T(8,128)(2,1)S(1)} %shard_map.136), channel_id=1, replica_groups=mesh['side'=2,'grp'=32,'tp'=4] {'grp'}, dimensions={0} | all-to-all | bytes 262144 | tf_op jit(solution)/shard_map/all_to_all | solution.py:244
  26.7 0.9 copy-done.2
  27.6 0.7 copy-done.4
  28.3 0.7 copy-done.9
  29.0 0.2 shard_map.137
  29.2 13.9 %all_to_all.26.x_ref = bf16[8,80,256]{2,1,0:T(8,128)(2,1)S(1)} all-to-all(bf16[8,80,256]{2,1,0:T(8,128)(2,1)S(1)} %shard_map.137), channel_id=1, replica_groups=mesh['side'=2,'grp'=32,'tp'=4] {'side','tp'}, dimensions={0} | all-to-all | bytes 655360 | tf_op jit(solution)/shard_map/all_to_all | solution.py:254
  43.2 0.7 copy-done.8
  43.8 0.5 shard_map.138
  44.3 14.6 %all_to_all.27.mine_ref = bf16[32,16,256]{2,1,0:T(8,128)(2,1)S(1)} all-to-all(bf16[32,16,256]{2,1,0:T(8,128)(2,1)S(1)} %get-tuple-element.9), channel_id=1, replica_groups=mesh['side'=2,'grp'=32,'tp'=4] {'grp'}, dimensions={0} | all-to-all | bytes 524288 | tf_op jit(solution)/shard_map/all_to_all | solution.py:264
  58.9 2.3 %collective-permute-start = (bf16[32,16,256]{2,1,0:T(8,128)(2,1)S(1)}, bf16[32,16,256]{2,1,0:T(8,128)(2,1)S(1)}, u32[]{:S(2)}, u32[]{:S(2)}) collective-permute-start(bf16[32,16,256]{2,1,0:T(8,128)(2,1)S(1)} %all_to_all.27.mine_ref), channel_id=1, source_target_pairs={{0,128},{128,0},{1,129},{129,1},{2,130},{130,2},{3,131},{131,3},{4... | collective-permute-start | bytes 786440 | tf_op jit(solution)/shard_map/ppermute | solution.py:265
  61.3 1.2 %collective-permute-done.other_ref = bf16[32,16,256]{2,1,0:T(8,128)(2,1)S(1)} collective-permute-done((bf16[32,16,256]{2,1,0:T(8,128)(2,1)S(1)}, bf16[32,16,256]{2,1,0:T(8,128)(2,1)S(1)}, u32[]{:S(2)}, u32[]{:S(2)}) %collective-permute-start) | collective-permute-done | bytes 262176 | tf_op jit(solution)/shard_map/ppermute | solution.py:265
  62.4 5.9 %shard_map.139 = bf16[8,16,1536]{2,1,0:T(8,128)(2,1)S(1)} custom-call(bf16[32,16,256]{2,1,0:T(8,128)(2,1)S(1)} %all_to_all.27.mine_ref, bf16[32,16,256]{2,1,0:T(8,128)(2,1)S(1)} %collective-permute-done.other_ref, bf16[288,6144]{1,0:T(8,128)(2,1)S(1)} %bitcast.11, bf16[288,6144]{1,0:T(8,128)(2,1)} %bitcast.17, bf16[288,6144]{1,0:T(8,128)(2,1)} %bitcast.18), custom_call_target="tpu_custom_call" | custom-call | flops 400000000 | bytes 11000000 | tf_op jit(solution)/shard_map/pallas_call | solution.py:204
  68.4 10.7 %all_to_all.28.x_ref = bf16[8,16,1536]{2,1,0:T(8,128)(2,1)S(1)} all-to-all(bf16[8,16,1536]{2,1,0:T(8,128)(2,1)S(1)} %shard_map.139), channel_id=1, replica_groups=mesh['side'=2,'grp'=32,'tp'=4] {'side','tp'}, dimensions={0} | all-to-all | bytes 786432 | tf_op jit(solution)/shard_map/all_to_all | solution.py:275
  79.1 0.7 shard_map.140
  79.8 3.9 %all-to-all-start.4 = ((f32[32,8,128]{2,1,0:T(8,128)}), f32[32,8,128]{2,1,0:T(8,128)S(1)}, u32[]{:S(2)}, u32[]{:S(2)}) async-start(f32[32,8,128]{2,1,0:T(8,128)} %shard_map.140), calls=%async_computation.4 | async-start | bytes 262144 | tf_op jit(solution)/shard_map/all_to_all | solution.py:277
  83.9 9.6 %all-to-all-done.4.x_ref = f32[32,8,128]{2,1,0:T(8,128)S(1)} async-done(((f32[32,8,128]{2,1,0:T(8,128)}), f32[32,8,128]{2,1,0:T(8,128)S(1)}, u32[]{:S(2)}, u32[]{:S(2)}) %all-to-all-start.4) | async-done | bytes 131104 | tf_op jit(solution)/shard_map/all_to_all | solution.py:277
  93.5 0.9 shard_map.142
  (17 shorter events, 0.2 us)
Async XLA Ops:
  0.0 62.4 %copy-start = (bf16[1,6144,288]{1,2,0:T(8,128)(2,1)S(1)}, bf16[1,6144,288]{1,2,0:T(8,128)(2,1)}, u32[]{:S(2)}) copy-start(bf16[1,6144,288]{1,2,0:T(8,128)(2,1)} %param.23) | copy-start | bytes 10616836
  0.0 1.4 %copy-start.1 = (f32[4,4,128,128]{3,2,1,0:T(8,128)S(1)}, f32[4,4,128,128]{3,2,1,0:T(8,128)}, u32[]{:S(2)}) copy-start(f32[4,4,128,128]{3,2,1,0:T(8,128)} %kv_ref.1) | copy-start | bytes 3145732
  1.4 0.7 copy-start.3
  2.1 0.7 copy-start.5
  2.7 0.7 copy-start.6
  3.4 0.7 copy-start.7
  4.1 0.7 copy-start.11
  26.7 0.9 copy-start.2
  27.6 0.7 copy-start.4
  28.3 0.7 copy-start.9
  43.2 0.7 copy-start.8
  58.9 3.5 %collective-permute-start = (bf16[32,16,256]{2,1,0:T(8,128)(2,1)S(1)}, bf16[32,16,256]{2,1,0:T(8,128)(2,1)S(1)}, u32[]{:S(2)}, u32[]{:S(2)}) collective-permute-start(bf16[32,16,256]{2,1,0:T(8,128)(2,1)S(1)} %all_to_all.27.mine_ref), channel_id=1, source_target_pairs={{0,128},{128,0},{1,129},{129,1},{2,130},{130,2},{3,131},{131,3},{4... | collective-permute-start | bytes 786440 | tf_op jit(solution)/shard_map/ppermute | solution.py:265
  62.4 21.2 %copy-start.10 = (s32[16,2]{0,1:T(2,128)S(1)}, s32[16,2]{0,1:T(2,128)}, u32[]{:S(2)}) copy-start(s32[16,2]{0,1:T(2,128)} %param.26) | copy-start | bytes 388
  62.4 21.2 %copy-start.12 = (f32[16,2]{0,1:T(2,128)S(1)}, f32[16,2]{0,1:T(2,128)}, u32[]{:S(2)}) copy-start(f32[16,2]{0,1:T(2,128)} %param.27) | copy-start | bytes 388
  79.8 13.7 %all-to-all-start.4 = ((f32[32,8,128]{2,1,0:T(8,128)}), f32[32,8,128]{2,1,0:T(8,128)S(1)}, u32[]{:S(2)}, u32[]{:S(2)}) async-start(f32[32,8,128]{2,1,0:T(8,128)} %shard_map.140), calls=%async_computation.4 | async-start | bytes 262144 | tf_op jit(solution)/shard_map/all_to_all | solution.py:277

commit v3 on v2

v3 whole, which is shorter than its diff:
```python
import functools
import jax
import jax.numpy as jnp
from jax import lax
from jax.experimental import pallas as pl
from jax.experimental.pallas import tpu as pltpu
from jax.sharding import PartitionSpec as P

D = 6144
HEADS = 32
HEAD_DIM = 128
EXPERTS = 16
CAP = 4
RB = 16
LANES = 256
DEEP = 6
WIDE = 4

epsilon = 1e-06
BLOCK = ("side", "tp")
f32, bf16 = jnp.float32, jnp.bfloat16
VM = pl.BlockSpec(memory_space=pltpu.VMEM)
HB = pl.BlockSpec(memory_space=pltpu.HBM)
MINOR = (((1,), (1,)), ((), ()))


def iota(shape, dim):
    return lax.broadcasted_iota(jnp.int32, shape, dim)


def column(row, size):
    full = jnp.broadcast_to(row, (size, size))
    return jnp.sum(jnp.where(iota((size, size), 0) == iota((size, size), 1), full, 0.0), axis=1, keepdims=True)


def halves(value):
    high = value.astype(bf16).astype(f32)
    return high, value - high


def attention(
    q_hbm, k_hbm, v_hbm, kv_hbm, decay_hbm, gain_hbm, w_hbm, residual_hbm, moe_hbm, routes_hbm,
    out_ref, w_ref, gain_ref, own_ref, moe_ref,
    q_ref, k_ref, v_ref, kv_ref, decay_ref, residual_ref, routes_ref, narrow_ref, sems,
):
    sessions, heads = q_ref.shape[:2]
    width = residual_ref.shape[1]
    pairs = [(q_hbm, q_ref), (k_hbm, k_ref), (v_hbm, v_ref), (decay_hbm, decay_ref), (gain_hbm, gain_ref)]
    pairs += [(kv_hbm.at[s], kv_ref.at[s]) for s in range(sessions)]
    pairs += [(residual_hbm, residual_ref), (routes_hbm, routes_ref), (moe_hbm, narrow_ref), (w_hbm, w_ref)]
    copies = [pltpu.make_async_copy(source, target, sems.at[i]) for i, (source, target) in enumerate(pairs)]
    for copy in copies:
        copy.start()
    for copy in copies[:5]:
        copy.wait()
    query = jnp.concatenate([q_ref[s].astype(f32) for s in range(sessions)], axis=0)
    key = jnp.concatenate([k_ref[s].astype(f32) for s in range(sessions)], axis=0)
    value = jnp.concatenate([v_ref[s].astype(f32) for s in range(sessions)], axis=0)
    turned = jnp.transpose(query)
    dots = jnp.sum(query * key, axis=1, keepdims=True)
    rows = []
    for s in range(sessions):
        copies[5 + s].wait()
        for h in range(heads):
            n = s * heads + h
            read = jnp.sum(turned[:, n : n + 1] * kv_ref[s, h], axis=0, keepdims=True)
            rows.append(decay_ref[:, h : h + 1] * read)
    attended = jnp.concatenate(rows, axis=0) + dots * value
    gain = jnp.concatenate([gain_ref[...]] * sessions, axis=0)
    message = (attended * gain).astype(bf16)
    for g in range(out_ref.shape[0]):
        out_ref[g] = message

    for copy in copies[5 + sessions :]:
        copy.wait()
    lane = iota((1, LANES), 1)
    routes = routes_ref[...].astype(f32)
    own = jnp.concatenate([residual_ref[...].astype(f32), jnp.zeros((RB, LANES - width), f32)], axis=1)
    own = jnp.where(lane == width, column(routes[0:1], RB), jnp.where(lane == width + 1, column(routes[1:2], RB), own))
    own_ref[...] = own.astype(bf16)
    moe_ref[...] = jnp.concatenate([narrow_ref[...], jnp.zeros((1, LANES - width), f32)], axis=1)


def project(x_ref, w_ref, gain_ref, mine_ref, other_ref, spread_ref):
    heads = gain_ref.shape[0]
    width = w_ref.shape[0]
    total = x_ref.shape[0] * x_ref.shape[1]
    sessions = total // heads
    half = sessions // 2
    spread_ref[...] = x_ref[...].reshape(total, HEAD_DIM).astype(f32)
    lane = iota((1, LANES), 1)
    squares = jnp.zeros((sessions, 1), f32)
    parts = []
    for h in range(heads):
        x = spread_ref[pl.ds(h, sessions, stride=heads), :]
        plain = x / gain_ref[h : h + 1, :]
        squares = squares + jnp.sum(plain * plain, axis=1, keepdims=True)
        parts.append(x.astype(bf16))
    projected = lax.dot_general(jnp.concatenate(parts, axis=1), w_ref[...], MINOR, preferred_element_type=f32)
    table = jnp.concatenate([projected, jnp.zeros((sessions, LANES - width), f32)], axis=1)
    table = jnp.where(lane == width, squares, table)
    first = lax.axis_index("side") == 0
    mine_ref[...] = jnp.where(first, table[:half], table[half:])
    other_ref[...] = jnp.where(first, table[half:], table[:half])


def gather_side(width, mine_ref, other_ref, own_ref, out_ref):
    half = mine_ref.shape[0]
    lane = iota((1, LANES), 1)
    table = mine_ref[...] + other_ref[...]
    squares = jnp.sum(jnp.where(lane == width, table, 0.0), axis=1, keepdims=True)
    high, low = halves(squares)
    table = jnp.where(lane == width, high, jnp.where(lane == width + 1, low, table)).astype(bf16)
    for t in range(out_ref.shape[0]):
        out_ref[t, :half, :] = table
        out_ref[t, half:, :] = own_ref[...]


def dispatch(width, x_ref, gain_ref, out_ref, own_ref, scratch_ref):
    half = x_ref.shape[1] - RB
    tp, odd = lax.axis_index("tp"), lax.rem(lax.axis_index("grp"), 2)
    lane = iota((1, LANES), 1)
    summed = x_ref[0, :half, :].astype(f32)
    for t in range(1, 4):
        summed = summed + x_ref[t, :half, :].astype(f32)
    squares = jnp.sum(jnp.where((lane == width) | (lane == width + 1), summed, 0.0), axis=1, keepdims=True)
    rest = jnp.concatenate([x_ref[t, half:, :].astype(f32) for t in range(4)], axis=0)
    hidden = jnp.where(lane < width, rest + lax.rsqrt(squares / (HEADS * HEAD_DIM) + epsilon) * summed, 0.0)
    scratch_ref[...] = hidden
    own_ref[...] = scratch_ref[pl.ds(pl.multiple_of(tp * RB, RB), RB), :]
    high, low = halves(jnp.sum(hidden * hidden, axis=1, keepdims=True))
    rows = jnp.where(lane == width, high, jnp.where(lane == width + 1, low, hidden * gain_ref[...]))
    rows = jnp.where(odd == 1, pltpu.roll(rows, LANES - width, 1), rows).astype(bf16)

    first = jnp.sum(jnp.where(lane == width, rest, 0.0), axis=1, keepdims=True).astype(jnp.int32)
    second = jnp.sum(jnp.where(lane == width + 1, rest, 0.0), axis=1, keepdims=True).astype(jnp.int32)
    places = EXPERTS * 4 * CAP
    place = iota((1, places), 1)
    expert = place // (4 * CAP)
    chosen = jnp.where((first == expert) | (second == expert), 1.0, 0.0)
    r, c = iota((half, half), 0), iota((half, half), 1)
    earlier = jnp.where((r // RB == c // RB) & (c < r), 1.0, 0.0).astype(bf16)
    slot = jnp.dot(earlier, chosen.astype(bf16), preferred_element_type=f32)
    block = iota((half, 1), 0) // RB
    here = (slot == (place % CAP).astype(f32)) & (block == place // CAP % 4)
    table = jnp.transpose(jnp.where(here, chosen, 0.0)).astype(bf16)
    routed = jnp.dot(table, rows, preferred_element_type=f32).astype(bf16)
    for e in range(EXPERTS):
        piece = routed[e * 4 * CAP : (e + 1) * 4 * CAP]
        out_ref[2 * e] = piece
        out_ref[2 * e + 1] = piece


def experts(
    mine_ref, other_ref, gate_hbm, up_hbm, down_hbm, keep_ref, give_ref,
    x_ref, feature_ref, gate_ref, up_ref, down_ref, sems,
):
    groups, rows, _ = mine_ref.shape
    pairs = []
    for n in range(DEEP):
        part = pl.ds(n * D // DEEP, D // DEEP)
        pairs += [(gate_hbm.at[:, part], gate_ref.at[:, part]), (up_hbm.at[:, part], up_ref.at[:, part])]
    for n in range(WIDE):
        part = pl.ds(n * D // WIDE, D // WIDE)
        pairs.append((down_hbm.at[:, part], down_ref.at[:, part]))
    copies = [pltpu.make_async_copy(source, target, sems.at[i]) for i, (source, target) in enumerate(pairs)]
    for copy in copies:
        copy.start()
    side = lax.axis_index("side")
    low_lane = iota((rows, 128), 1) < 64
    for ref, at in ((mine_ref, side), (other_ref, 1 - side)):
        start = pl.multiple_of(at * rows, rows)
        feature = jnp.zeros((rows, 128), f32)
        for i in range(groups // 2):
            b_even = ref[2 * i, :, 128:].astype(f32)
            b_odd = ref[2 * i + 1, :, :128].astype(f32)
            feature = feature + jnp.where(low_lane, b_odd, b_even)
            x_ref[pl.ds(start, rows), 384 * i : 384 * i + 128] = ref[2 * i, :, :128]
            x_ref[pl.ds(start, rows), 384 * i + 128 : 384 * i + 256] = jnp.where(low_lane, b_even, b_odd).astype(bf16)
            x_ref[pl.ds(start, rows), 384 * i + 256 : 384 * i + 384] = ref[2 * i + 1, :, 128:]
        feature_ref[pl.ds(start, rows), :] = feature
    scale = lax.rsqrt(jnp.sum(feature_ref[...], axis=1, keepdims=True) / D + epsilon)
    gate = jnp.zeros((2 * rows, gate_ref.shape[0]), f32)
    up = gate
    for n in range(DEEP):
        part = slice(n * D // DEEP, (n + 1) * D // DEEP)
        x = x_ref[:, part]
        copies[2 * n].wait()
        gate = gate + lax.dot_general(x, gate_ref[:, part], MINOR, preferred_element_type=f32)
        copies[2 * n + 1].wait()
        up = up + lax.dot_general(x, up_ref[:, part], MINOR, preferred_element_type=f32)
    gate, up = scale * gate, scale * up
    hidden = (gate * jax.nn.sigmoid(gate) * up).astype(bf16)
    first = side == 0
    for n in range(WIDE):
        part = slice(n * D // WIDE, (n + 1) * D // WIDE)
        copies[2 * DEEP + n].wait()
        chunk = jnp.dot(hidden, down_ref[:, part], preferred_element_type=f32)
        keep_ref[:, part] = jnp.where(first, chunk[:rows], chunk[rows:])
        give_ref[:, part] = jnp.where(first, chunk[rows:], chunk[:rows]).astype(bf16)


def spread(keep_ref, other_ref, out_ref):
    for i in range(D // 384):
        a, b, c = (
            keep_ref[:, 128 * n : 128 * n + 128] + other_ref[:, 128 * n : 128 * n + 128].astype(f32)
            for n in range(3 * i, 3 * i + 3)
        )
        for t in range(4):
            rows = slice(t * CAP, (t + 1) * CAP)
            out_ref[(2 * i) * 4 + t] = jnp.concatenate([a[rows], b[rows]], axis=0).astype(bf16)
            out_ref[(2 * i + 1) * 4 + t] = jnp.concatenate([b[rows], c[rows]], axis=0).astype(bf16)


def combiner(routes_ref, weights_ref, out_ref):
    routes, weights = routes_ref[...].astype(f32), weights_ref[...]
    r0, r1 = column(routes[0:1], RB).astype(jnp.int32), column(routes[1:2], RB).astype(jnp.int32)
    w0, w1 = column(weights[0:1], RB), column(weights[1:2], RB)
    place = iota((1, out_ref.shape[1]), 1)
    expert = place // 64
    chosen = jnp.where((r0 == expert) | (r1 == expert), 1.0, 0.0)
    earlier = jnp.where(iota((RB, RB), 1) < iota((RB, RB), 0), 1.0, 0.0)
    slot = jnp.dot(earlier, chosen, preferred_element_type=f32)
    weight = jnp.where(r0 == expert, w0, 0.0) + jnp.where(r1 == expert, w1, 0.0)
    row = (place % 8).astype(f32)
    for part in range(2):
        value = jnp.where(slot + part * CAP == row, weight, 0.0)
        high, rest = halves(value)
        middle, low = halves(rest)
        for n, piece in enumerate((high, middle, low)):
            out_ref[(3 * part + n) * RB : (3 * part + n + 1) * RB, :] = piece.astype(bf16)


def combine(x_ref, table_ref, own_ref, out_ref):
    odd = lax.rem(lax.axis_index("grp"), 2)
    width = out_ref.shape[1]
    x = x_ref[...].reshape(-1, 128)
    both = jnp.dot(table_ref[...], x, preferred_element_type=f32)
    a = both[2 * RB : 3 * RB] + both[RB : 2 * RB] + both[:RB]
    b = both[5 * RB :] + both[4 * RB : 5 * RB] + both[3 * RB : 4 * RB]
    mixture = jnp.concatenate([a, b], axis=1)
    mixture = jnp.where(odd == 1, pltpu.roll(mixture, width, 1), mixture)
    out_ref[...] = (own_ref[...] + mixture)[:, :width].astype(bf16)


def far(x):
    return pltpu.with_memory_space_constraint(x, pltpu.HBM)


def call(kernel, outs, specs, args, scratch=(), flops=0, moved=0, limit=8):
    single = not isinstance(outs, list)
    made = pl.pallas_call(
        kernel,
        out_shape=outs if single else tuple(outs),
        in_specs=specs,
        out_specs=VM if single else tuple(VM for _ in outs),
        scratch_shapes=list(scratch),
        compiler_params=pltpu.CompilerParams(vmem_limit_bytes=limit * 1024 * 1024),
        cost_estimate=pl.CostEstimate(flops=flops, bytes_accessed=moved, transcendentals=0),
    )
    return made(*args)


def shape(dims, dtype):
    return jax.ShapeDtypeStruct(dims, dtype)


def body(
    queries,
    new_keys,
    new_values,
    kv_memory,
    decay_rate,
    attn_gain,
    w_out,
    residual,
    moe_gain,
    w_gate,
    w_up,
    w_down,
    routes,
    route_weights,
):
    groups = lax.axis_size("grp")
    width = residual.shape[1]
    sessions, heads = queries.shape[:2]
    half = groups * sessions // 2
    turned_routes = routes.T
    swap = [(0, 1), (1, 0)]

    table = call(
        combiner, shape((6 * RB, 1024), bf16), [VM, VM], (turned_routes, route_weights.T), flops=10**6, moved=200000
    )
    decay, narrow, w_turned = decay_rate.reshape(1, -1), moe_gain.reshape(1, -1), w_out.T
    taken = (queries, new_keys, new_values, kv_memory, decay, attn_gain, w_turned, residual, narrow, turned_routes)
    held = (queries, new_keys, new_values, kv_memory, decay, residual, turned_routes, narrow)
    taken = tuple(far(x) for x in taken)
    sent, w_near, gain_near, own_rows, moe_near = call(
        attention,
        [
            shape((groups, sessions * heads, HEAD_DIM), bf16),
            shape(w_turned.shape, bf16),
            shape(attn_gain.shape, f32),
            shape((RB, LANES), bf16),
            shape((1, LANES), f32),
        ],
        [HB] * len(taken),
        taken,
        scratch=[pltpu.VMEM(x.shape, x.dtype) for x in held] + [pltpu.SemaphoreType.DMA((9 + sessions,))],
        flops=10**6,
        moved=1200000,
    )
    every = lax.all_to_all(sent, "grp", 0, 0, tiled=True)
    mine, give = call(
        project,
        [shape((half, LANES), f32)] * 2,
        [VM] * 3,
        (every, w_near, gain_near),
        scratch=[pltpu.VMEM((groups * sessions * heads, HEAD_DIM), f32)],
        flops=25 * 10**6,
        moved=700000,
    )
    message = call(
        functools.partial(gather_side, width),
        shape((4, half + RB, LANES), bf16),
        [VM] * 3,
        (mine, lax.ppermute(give, "side", swap), own_rows),
        flops=10**6,
        moved=400000,
    )
    got = lax.all_to_all(message, "tp", 0, 0, tiled=True)
    outbox, own_hidden = call(
        functools.partial(dispatch, width),
        [shape((groups, 4 * CAP, LANES), bf16), shape((RB, LANES), f32)],
        [VM, VM],
        (got, moe_near),
        scratch=[pltpu.VMEM((half, LANES), f32)],
        flops=10**7,
        moved=700000,
    )
    inbox = lax.all_to_all(outbox, "grp", 0, 0, tiled=True)
    weights = [far(x) for x in (w_gate[0].T, w_up[0].T, w_down[0])]
    keep, give = call(
        experts,
        [shape((4 * CAP, D), f32), shape((4 * CAP, D), bf16)],
        [VM, VM, HB, HB, HB],
        (inbox, lax.ppermute(inbox, "side", swap), *weights),
        scratch=[pltpu.VMEM((8 * CAP, D), bf16), pltpu.VMEM((8 * CAP, 128), f32)]
        + [pltpu.VMEM(x.shape, bf16) for x in weights]
        + [pltpu.SemaphoreType.DMA((2 * DEEP + WIDE,))],
        flops=4 * 10**8,
        moved=11000000,
        limit=24,
    )
    back = call(
        spread,
        shape((groups * 4, 2 * CAP, 128), bf16),
        [VM, VM],
        (keep, lax.ppermute(give, "side", swap)),
        flops=10**6,
        moved=900000,
    )
    returned = lax.all_to_all(back, ("grp", "tp"), 0, 0, tiled=True)
    return call(
        combine,
        shape((RB, width), bf16),
        [VM] * 3,
        (returned, table, own_hidden),
        flops=3 * 10**7,
        moved=500000,
    )


def solution(mesh):
    placed = (
        P("grp", ("side", "tp"), None),
        P("grp", ("side", "tp"), None),
        P("grp", ("side", "tp"), None),
        P("grp", ("side", "tp"), None, None),
        P(("side", "tp")),
        P(("side", "tp"), None),
        P(("side", "tp"), "grp"),
        P(("side", "tp"), "grp"),
        P("grp"),
        P("grp", None, ("side", "tp")),
        P("grp", None, ("side", "tp")),
        P("grp", ("side", "tp"), None),
        P(("side", "tp"), None),
        P(("side", "tp"), None),
    )
    return jax.shard_map(
        body, mesh=mesh, in_specs=placed, out_specs=P(("side", "tp"), "grp"), check_vma=False
    )
```

time: 94.9 us -> 84.5 us (0.89)
  blocking collectives: 60.3 us -> 43.5 us
  local copies, waits for them, and re-layouts: 7.76 us -> 0.01 us
  starting transfers between devices: 6.18 us -> 12.5 us
  waiting for transfers between devices: 10.8 us -> 16.8 us
  Pallas kernels: 9.31 us -> 11.3 us
    all_to_all x2 -> x1, blocking collectives: 24.6 us -> 8.99 us  [body(): got = lax.all_to_all(message, 'tp', 0, 0, tiled=True)]
    unnamed x26 -> x4, local copies, waits for them, and re-layouts: 7.76 us -> 0.01 us
    all_to_all x1, waiting for transfers between devices: 9.61 us -> 13.7 us  [body(): returned = lax.all_to_all(back, ('grp', 'tp'), 0, 0, tiled=True)]
    ppermute x1 -> x3, starting transfers between devices: 2.33 us -> 6.37 us  [the longest x1 3.76 us: body(): lax.ppermute(inbox, 'side', swap)]
    all_to_all x1, starting transfers between devices: 3.85 us -> 6.16 us  [body(): returned = lax.all_to_all(back, ('grp', 'tp'), 0, 0, tiled=True)]
    pallas_call x7 -> x8, Pallas kernels: 9.31 us -> 11.3 us  [call(): return made(*args)]
    ppermute x1 -> x3, waiting for transfers between devices: 1.16 us -> 3.14 us  [the longest x2 1.97 us: body(): lax.ppermute(give, 'side', swap)]
    all_to_all x1, blocking collectives: 14.6 us -> 13.4 us  [body(): inbox = lax.all_to_all(outbox, 'grp', 0, 0, tiled=True)]
  transfers between devices with their start and end apart: 2 -> 4, of which waited for: 2 -> 4; matrix products, arithmetic and copies ran while one was open for 0% -> 0% of each run, Pallas kernels for 0% -> 0%
where the time goes in v3:
time: 84.5 us; the launch traced here: 84.2 us
  blocking collectives  43.5 us (51%)
  waiting for transfers between devices  16.8 us (20%)
  starting transfers between devices  12.5 us (15%)
  Pallas kernels  11.3 us (13%)
    all_to_all x1, blocking collectives, body(): every = lax.all_to_all(sent, 'grp', 0, 0, tiled=True)  21 us
    all_to_all x1, waiting for transfers between devices, body(): returned = lax.all_to_all(back, ('grp', 'tp'), 0, 0, tiled=True)  13.7 us
    all_to_all x1, blocking collectives, body(): inbox = lax.all_to_all(outbox, 'grp', 0, 0, tiled=True)  13.4 us
    pallas_call x8, Pallas kernels, call(): return made(*args)  11.3 us
    all_to_all x1, blocking collectives, body(): got = lax.all_to_all(message, 'tp', 0, 0, tiled=True)  8.99 us
    all_to_all x1, starting transfers between devices, body(): returned = lax.all_to_all(back, ('grp', 'tp'), 0, 0, tiled=True)  6.16 us
    ppermute x1, starting transfers between devices, body(): lax.ppermute(inbox, 'side', swap)  3.76 us
    ppermute x2, starting transfers between devices, body(): lax.ppermute(give, 'side', swap)  2.61 us
  transfers between devices with their start and end apart: 4, of which 4 were waited for; matrix products, arithmetic and copies ran while one was open for 0% of the time, Pallas kernels for 0%

profile of v3, /device:TPU:1, one launch (start us, length us, event | category | flops | bytes accessed | tf_op | source)
XLA Modules:
  0.0 84.2 jit_solution(6930170630960325350)
XLA Ops:
  0.0 1.9 %shard_map.136 = (bf16[32,16,128]{2,1,0:T(8,128)(2,1)S(1)}, bf16[192,512]{1,0:T(8,128)(2,1)S(1)}, f32[4,128]{1,0:T(4,128)S(1)}, bf16[16,256]{1,0:T(8,128)(2,1)S(1)}, f32[1,256]{1,0:T(1,128)S(1)}) custom-call(bf16[4,4,128]{2,1,0:T(4,128)(2,1)} %q_hbm.1, bf16[4,4,128]{2,1,0:T(4,128)(2,1)} %k_hbm.1, bf16[4,4,128]{2,1,0:T(4,128)(2,1)} %v_hbm.1, ...), custom_call_target="tpu_custom_call" | custom-call | flops 1000000 | bytes 1200000 | tf_op jit(solution)/shard_map/pallas_call | solution.py:261
  1.9 21.0 %all_to_all.20.x_ref = bf16[32,16,128]{2,1,0:T(8,128)(2,1)S(1)} all-to-all(bf16[32,16,128]{2,1,0:T(8,128)(2,1)S(1)} %get-tuple-element.16), channel_id=1, replica_groups=mesh['side'=2,'grp'=32,'tp'=4] {'grp'}, dimensions={0} | all-to-all | bytes 262144 | tf_op jit(solution)/shard_map/all_to_all | solution.py:313
  22.9 0.2 shard_map.137
  23.1 2.1 %collective-permute-start = (f32[64,256]{1,0:T(8,128)S(1)}, f32[64,256]{1,0:T(8,128)S(1)}, u32[]{:S(2)}, u32[]{:S(2)}) collective-permute-start(f32[64,256]{1,0:T(8,128)S(1)} %get-tuple-element.20), channel_id=1, source_target_pairs={{0,128},{128,0},{1,129},{129,1},{2,130},{130,2},{3,131},{131,3},{4... | collective-permute-start | bytes 196616 | tf_op jit(solution)/shard_map/ppermute | solution.py:327
  25.3 0.9 %collective-permute-done.other_ref = f32[64,256]{1,0:T(8,128)S(1)} collective-permute-done((f32[64,256]{1,0:T(8,128)S(1)}, f32[64,256]{1,0:T(8,128)S(1)}, u32[]{:S(2)}, u32[]{:S(2)}) %collective-permute-start) | collective-permute-done | bytes 65568 | tf_op jit(solution)/shard_map/ppermute | solution.py:327
  26.2 0.1 shard_map.138
  26.3 9.0 %all_to_all.21.x_ref = bf16[4,80,256]{2,1,0:T(8,128)(2,1)S(1)} all-to-all(bf16[4,80,256]{2,1,0:T(8,128)(2,1)S(1)} %shard_map.138), channel_id=1, replica_groups=mesh['side'=2,'grp'=32,'tp'=4] {'tp'}, dimensions={0} | all-to-all | bytes 327680 | tf_op jit(solution)/shard_map/all_to_all | solution.py:331
  35.3 0.5 shard_map.139
  35.7 13.4 %all_to_all.22.mine_ref = bf16[32,16,256]{2,1,0:T(8,128)(2,1)S(1)} all-to-all(bf16[32,16,256]{2,1,0:T(8,128)(2,1)S(1)} %get-tuple-element.23), channel_id=1, replica_groups=mesh['side'=2,'grp'=32,'tp'=4] {'grp'}, dimensions={0} | all-to-all | bytes 524288 | tf_op jit(solution)/shard_map/all_to_all | solution.py:341
  49.2 3.8 %collective-permute-start.1 = (bf16[32,16,256]{2,1,0:T(8,128)(2,1)S(1)}, bf16[32,16,256]{2,1,0:T(8,128)(2,1)S(1)}, u32[]{:S(2)}, u32[]{:S(2)}) collective-permute-start(bf16[32,16,256]{2,1,0:T(8,128)(2,1)S(1)} %all_to_all.22.mine_ref), channel_id=1, source_target_pairs={{0,128},{128,0},{1,129},{129,1},{2,130},{130,2},{3,131},{131,3},{4... | collective-permute-start | bytes 786440 | tf_op jit(solution)/shard_map/ppermute | solution.py:347
  53.0 1.2 %collective-permute-done.1.other_ref = bf16[32,16,256]{2,1,0:T(8,128)(2,1)S(1)} collective-permute-done((bf16[32,16,256]{2,1,0:T(8,128)(2,1)S(1)}, bf16[32,16,256]{2,1,0:T(8,128)(2,1)S(1)}, u32[]{:S(2)}, u32[]{:S(2)}) %collective-permute-start.1) | collective-permute-done | bytes 262176 | tf_op jit(solution)/shard_map/ppermute | solution.py:347
  54.1 0.0 copy-start
  54.1 0.0 copy-start.1
  54.1 6.8 %shard_map.140 = (f32[16,6144]{1,0:T(8,128)S(1)}, bf16[16,6144]{1,0:T(8,128)(2,1)S(1)}) custom-call(bf16[32,16,256]{2,1,0:T(8,128)(2,1)S(1)} %all_to_all.22.mine_ref, bf16[32,16,256]{2,1,0:T(8,128)(2,1)S(1)} %collective-permute-done.1.other_ref, bf16[288,6144]{1,0:T(8,128)(2,1)} %bitcast.15, bf16[288,6144]{1,0:T(8,128)(2,1)} %bitcast.16, ...), custom_call_target="tpu_custom_call" | custom-call | flops 400000000 | bytes 11000000 | tf_op jit(solution)/shard_map/pallas_call | solution.py:261
  60.9 0.5 collective-permute-start.2
  61.3 1.1 %collective-permute-done.2.other_ref = bf16[16,6144]{1,0:T(8,128)(2,1)S(1)} collective-permute-done((bf16[16,6144]{1,0:T(8,128)(2,1)S(1)}, bf16[16,6144]{1,0:T(8,128)(2,1)S(1)}, u32[]{:S(2)}, u32[]{:S(2)}) %collective-permute-start.2) | collective-permute-done | bytes 196640 | tf_op jit(solution)/shard_map/ppermute | solution.py:359
  62.4 0.8 shard_map.141
  63.2 6.2 %all-to-all-start.3 = ((bf16[128,8,128]{2,1,0:T(8,128)(2,1)}), bf16[128,8,128]{2,1,0:T(8,128)(2,1)S(1)}, u32[]{:S(2)}, u32[]{:S(2)}) async-start(bf16[128,8,128]{2,1,0:T(8,128)(2,1)} %shard_map.141), calls=%async_computation.3 | async-start | bytes 524288 | tf_op jit(solution)/shard_map/all_to_all | solution.py:363
  69.4 0.0 copy-done
  69.4 0.0 copy-done.1
  69.4 0.2 shard_map.142.table_ref
  69.6 13.7 %all-to-all-done.3.x_ref = bf16[128,8,128]{2,1,0:T(8,128)(2,1)S(1)} async-done(((bf16[128,8,128]{2,1,0:T(8,128)(2,1)}), bf16[128,8,128]{2,1,0:T(8,128)(2,1)S(1)}, u32[]{:S(2)}, u32[]{:S(2)}) %all-to-all-start.3) | async-done | bytes 262176 | tf_op jit(solution)/shard_map/all_to_all | solution.py:363
  83.3 0.9 %shard_map.143 = bf16[16,192]{1,0:T(8,128)(2,1)} custom-call(bf16[128,8,128]{2,1,0:T(8,128)(2,1)S(1)} %all-to-all-done.3.x_ref, bf16[96,1024]{1,0:T(8,128)(2,1)S(1)} %shard_map.142.table_ref, f32[16,256]{1,0:T(8,128)S(1)} %get-tuple-element.26.own_ref), custom_call_target="tpu_custom_call" | custom-call | flops 30000000 | bytes 500000 | tf_op jit(solution)/shard_map/pallas_call | solution.py:261
Async XLA Ops:
  23.1 3.1 %collective-permute-start = (f32[64,256]{1,0:T(8,128)S(1)}, f32[64,256]{1,0:T(8,128)S(1)}, u32[]{:S(2)}, u32[]{:S(2)}) collective-permute-start(f32[64,256]{1,0:T(8,128)S(1)} %get-tuple-element.20), channel_id=1, source_target_pairs={{0,128},{128,0},{1,129},{129,1},{2,130},{130,2},{3,131},{131,3},{4... | collective-permute-start | bytes 196616 | tf_op jit(solution)/shard_map/ppermute | solution.py:327
  49.2 4.9 %collective-permute-start.1 = (bf16[32,16,256]{2,1,0:T(8,128)(2,1)S(1)}, bf16[32,16,256]{2,1,0:T(8,128)(2,1)S(1)}, u32[]{:S(2)}, u32[]{:S(2)}) collective-permute-start(bf16[32,16,256]{2,1,0:T(8,128)(2,1)S(1)} %all_to_all.22.mine_ref), channel_id=1, source_target_pairs={{0,128},{128,0},{1,129},{129,1},{2,130},{130,2},{3,131},{131,3},{4... | collective-permute-start | bytes 786440 | tf_op jit(solution)/shard_map/ppermute | solution.py:347
  54.1 15.3 %copy-start = (s32[16,2]{0,1:T(2,128)S(1)}, s32[16,2]{0,1:T(2,128)}, u32[]{:S(2)}) copy-start(s32[16,2]{0,1:T(2,128)} %param.26) | copy-start | bytes 388
  54.1 15.3 %copy-start.1 = (f32[16,2]{0,1:T(2,128)S(1)}, f32[16,2]{0,1:T(2,128)}, u32[]{:S(2)}) copy-start(f32[16,2]{0,1:T(2,128)} %param.27) | copy-start | bytes 388
  60.9 1.5 %collective-permute-start.2 = (bf16[16,6144]{1,0:T(8,128)(2,1)S(1)}, bf16[16,6144]{1,0:T(8,128)(2,1)S(1)}, u32[]{:S(2)}, u32[]{:S(2)}) collective-permute-start(bf16[16,6144]{1,0:T(8,128)(2,1)S(1)} %get-tuple-element.25), channel_id=1, source_target_pairs={{0,128},{128,0},{1,129},{129,1},{2,130},{130,2},{3,131},{131,3},{4... | collective-permute-start | bytes 589832 | tf_op jit(solution)/shard_map/ppermute | solution.py:359
  63.2 20.1 %all-to-all-start.3 = ((bf16[128,8,128]{2,1,0:T(8,128)(2,1)}), bf16[128,8,128]{2,1,0:T(8,128)(2,1)S(1)}, u32[]{:S(2)}, u32[]{:S(2)}) async-start(bf16[128,8,128]{2,1,0:T(8,128)(2,1)} %shard_map.141), calls=%async_computation.3 | async-start | bytes 524288 | tf_op jit(solution)/shard_map/all_to_all | solution.py:363

commit v4 on v3

--- a/solution.py
+++ b/solution.py
@@ -39,19 +39,28 @@
 
 
 def attention(
-    q_hbm, k_hbm, v_hbm, kv_hbm, decay_hbm, gain_hbm, w_hbm, residual_hbm, moe_hbm, routes_hbm,
-    out_ref, w_ref, gain_ref, own_ref, moe_ref,
-    q_ref, k_ref, v_ref, kv_ref, decay_ref, residual_ref, routes_ref, narrow_ref, sems,
+    q_hbm, k_hbm, v_hbm, kv_hbm, decay_hbm, gain_hbm, w_hbm, residual_hbm, moe_hbm, routes_hbm, weights_hbm,
+    out_ref, w_ref, gain_ref, own_ref, moe_ref, table_ref,
+    q_ref, k_ref, v_ref, kv_ref, decay_ref, residual_ref, routes_ref, weights_ref, narrow_ref, sems,
 ):
     sessions, heads = q_ref.shape[:2]
     width = residual_ref.shape[1]
-    pairs = [(q_hbm, q_ref), (k_hbm, k_ref), (v_hbm, v_ref), (decay_hbm, decay_ref), (gain_hbm, gain_ref)]
+    pairs = [(routes_hbm, routes_ref), (weights_hbm, weights_ref), (residual_hbm, residual_ref)]
+    pairs += [(q_hbm, q_ref), (k_hbm, k_ref), (v_hbm, v_ref), (decay_hbm, decay_ref), (gain_hbm, gain_ref)]
     pairs += [(kv_hbm.at[s], kv_ref.at[s]) for s in range(sessions)]
-    pairs += [(residual_hbm, residual_ref), (routes_hbm, routes_ref), (moe_hbm, narrow_ref), (w_hbm, w_ref)]
+    pairs += [(moe_hbm, narrow_ref), (w_hbm, w_ref)]
     copies = [pltpu.make_async_copy(source, target, sems.at[i]) for i, (source, target) in enumerate(pairs)]
     for copy in copies:
         copy.start()
-    for copy in copies[:5]:
+    for copy in copies[:3]:
+        copy.wait()
+    routes = routes_ref[...].astype(f32)
+    combiner(routes, weights_ref[...], table_ref)
+    lane = iota((1, LANES), 1)
+    own = jnp.concatenate([residual_ref[...].astype(f32), jnp.zeros((RB, LANES - width), f32)], axis=1)
+    own = jnp.where(lane == width, column(routes[0:1], RB), jnp.where(lane == width + 1, column(routes[1:2], RB), own))
+    own_ref[...] = own.astype(bf16)
+    for copy in copies[3:8]:
         copy.wait()
     query = jnp.concatenate([q_ref[s].astype(f32) for s in range(sessions)], axis=0)
     key = jnp.concatenate([k_ref[s].astype(f32) for s in range(sessions)], axis=0)
@@ -60,7 +69,7 @@
     dots = jnp.sum(query * key, axis=1, keepdims=True)
     rows = []
     for s in range(sessions):
-        copies[5 + s].wait()
+        copies[8 + s].wait()
         for h in range(heads):
             n = s * heads + h
             read = jnp.sum(turned[:, n : n + 1] * kv_ref[s, h], axis=0, keepdims=True)
@@ -71,13 +80,8 @@
     for g in range(out_ref.shape[0]):
         out_ref[g] = message
 
-    for copy in copies[5 + sessions :]:
+    for copy in copies[8 + sessions :]:
         copy.wait()
-    lane = iota((1, LANES), 1)
-    routes = routes_ref[...].astype(f32)
-    own = jnp.concatenate([residual_ref[...].astype(f32), jnp.zeros((RB, LANES - width), f32)], axis=1)
-    own = jnp.where(lane == width, column(routes[0:1], RB), jnp.where(lane == width + 1, column(routes[1:2], RB), own))
-    own_ref[...] = own.astype(bf16)
     moe_ref[...] = jnp.concatenate([narrow_ref[...], jnp.zeros((1, LANES - width), f32)], axis=1)
 
 
@@ -151,21 +155,15 @@
         out_ref[2 * e + 1] = piece
 
 
-def experts(
-    mine_ref, other_ref, gate_hbm, up_hbm, down_hbm, keep_ref, give_ref,
-    x_ref, feature_ref, gate_ref, up_ref, down_ref, sems,
-):
+def prefetch(after_ref, far_ref, near_ref, token_ref, sem):
+    copy = pltpu.make_async_copy(far_ref, near_ref, sem)
+    copy.start()
+    token_ref[...] = jnp.zeros_like(token_ref)
+    copy.wait()
+
+
+def experts(mine_ref, other_ref, gate_ref, up_ref, down_ref, keep_ref, give_ref, x_ref, feature_ref):
     groups, rows, _ = mine_ref.shape
-    pairs = []
-    for n in range(DEEP):
-        part = pl.ds(n * D // DEEP, D // DEEP)
-        pairs += [(gate_hbm.at[:, part], gate_ref.at[:, part]), (up_hbm.at[:, part], up_ref.at[:, part])]
-    for n in range(WIDE):
-        part = pl.ds(n * D // WIDE, D // WIDE)
-        pairs.append((down_hbm.at[:, part], down_ref.at[:, part]))
-    copies = [pltpu.make_async_copy(source, target, sems.at[i]) for i, (source, target) in enumerate(pairs)]
-    for copy in copies:
-        copy.start()
     side = lax.axis_index("side")
     low_lane = iota((rows, 128), 1) < 64
     for ref, at in ((mine_ref, side), (other_ref, 1 - side)):
@@ -185,16 +183,13 @@
     for n in range(DEEP):
         part = slice(n * D // DEEP, (n + 1) * D // DEEP)
         x = x_ref[:, part]
-        copies[2 * n].wait()
         gate = gate + lax.dot_general(x, gate_ref[:, part], MINOR, preferred_element_type=f32)
-        copies[2 * n + 1].wait()
         up = up + lax.dot_general(x, up_ref[:, part], MINOR, preferred_element_type=f32)
     gate, up = scale * gate, scale * up
     hidden = (gate * jax.nn.sigmoid(gate) * up).astype(bf16)
     first = side == 0
     for n in range(WIDE):
         part = slice(n * D // WIDE, (n + 1) * D // WIDE)
-        copies[2 * DEEP + n].wait()
         chunk = jnp.dot(hidden, down_ref[:, part], preferred_element_type=f32)
         keep_ref[:, part] = jnp.where(first, chunk[:rows], chunk[rows:])
         give_ref[:, part] = jnp.where(first, chunk[rows:], chunk[:rows]).astype(bf16)
@@ -212,8 +207,7 @@
             out_ref[(2 * i + 1) * 4 + t] = jnp.concatenate([b[rows], c[rows]], axis=0).astype(bf16)
 
 
-def combiner(routes_ref, weights_ref, out_ref):
-    routes, weights = routes_ref[...].astype(f32), weights_ref[...]
+def combiner(routes, weights, out_ref):
     r0, r1 = column(routes[0:1], RB).astype(jnp.int32), column(routes[1:2], RB).astype(jnp.int32)
     w0, w1 = column(weights[0:1], RB), column(weights[1:2], RB)
     place = iota((1, out_ref.shape[1]), 1)
@@ -259,6 +253,18 @@
         cost_estimate=pl.CostEstimate(flops=flops, bytes_accessed=moved, transcendentals=0),
     )
     return made(*args)
+
+
+def fetch(after, x):
+    near, token = call(
+        prefetch,
+        [pltpu.VMEM(x.shape, x.dtype), shape((8, 128), f32)],
+        [VM, HB],
+        (after, far(x)),
+        scratch=[pltpu.SemaphoreType.DMA],
+        moved=4 * x.size,
+    )
+    return pltpu.with_memory_space_constraint(near, pltpu.VMEM), token
 
 
 def shape(dims, dtype):
@@ -288,14 +294,11 @@
     turned_routes = routes.T
     swap = [(0, 1), (1, 0)]
 
-    table = call(
-        combiner, shape((6 * RB, 1024), bf16), [VM, VM], (turned_routes, route_weights.T), flops=10**6, moved=200000
-    )
     decay, narrow, w_turned = decay_rate.reshape(1, -1), moe_gain.reshape(1, -1), w_out.T
-    taken = (queries, new_keys, new_values, kv_memory, decay, attn_gain, w_turned, residual, narrow, turned_routes)
-    held = (queries, new_keys, new_values, kv_memory, decay, residual, turned_routes, narrow)
+    taken = (queries, new_keys, new_values, kv_memory, decay, attn_gain, w_turned, residual, narrow, turned_routes, route_weights.T)
+    held = (queries, new_keys, new_values, kv_memory, decay, residual, turned_routes, route_weights.T, narrow)
     taken = tuple(far(x) for x in taken)
-    sent, w_near, gain_near, own_rows, moe_near = call(
+    sent, w_near, gain_near, own_rows, moe_near, table = call(
         attention,
         [
             shape((groups, sessions * heads, HEAD_DIM), bf16),
@@ -303,10 +306,11 @@
             shape(attn_gain.shape, f32),
             shape((RB, LANES), bf16),
             shape((1, LANES), f32),
+            shape((6 * RB, 1024), bf16),
         ],
         [HB] * len(taken),
         taken,
-        scratch=[pltpu.VMEM(x.shape, x.dtype) for x in held] + [pltpu.SemaphoreType.DMA((9 + sessions,))],
+        scratch=[pltpu.VMEM(x.shape, x.dtype) for x in held] + [pltpu.SemaphoreType.DMA((10 + sessions,))],
         flops=10**6,
         moved=1200000,
     )
@@ -335,22 +339,19 @@
         [VM, VM],
         (got, moe_near),
         scratch=[pltpu.VMEM((half, LANES), f32)],
-        flops=10**7,
+        flops=3 * 10**10,
         moved=700000,
     )
     inbox = lax.all_to_all(outbox, "grp", 0, 0, tiled=True)
-    weights = [far(x) for x in (w_gate[0].T, w_up[0].T, w_down[0])]
     keep, give = call(
         experts,
         [shape((4 * CAP, D), f32), shape((4 * CAP, D), bf16)],
-        [VM, VM, HB, HB, HB],
-        (inbox, lax.ppermute(inbox, "side", swap), *weights),
-        scratch=[pltpu.VMEM((8 * CAP, D), bf16), pltpu.VMEM((8 * CAP, 128), f32)]
-        + [pltpu.VMEM(x.shape, bf16) for x in weights]
-        + [pltpu.SemaphoreType.DMA((2 * DEEP + WIDE,))],
+        [VM] * 5,
+        (inbox, lax.ppermute(inbox, "side", swap), w_gate[0].T, w_up[0].T, w_down[0]),
+        scratch=[pltpu.VMEM((8 * CAP, D), bf16), pltpu.VMEM((8 * CAP, 128), f32)],
         flops=4 * 10**8,
         moved=11000000,
-        limit=24,
+        limit=12,
     )
     back = call(
         spread,

time: 84.5 us -> 79.8 us (0.944)
  blocking collectives: 43.5 us -> 63.6 us
  waiting for transfers between devices: 16.8 us -> 3.15 us
  starting transfers between devices: 12.5 us -> 6.08 us
  Pallas kernels: 11.3 us -> 6.64 us
    all_to_all x0 -> x1, blocking collectives: none -> 19.5 us  [body(): returned = lax.all_to_all(back, ('grp', 'tp'), 0, 0, tiled=True)]
    all_to_all x1 -> x0, waiting for transfers between devices: 13.7 us -> none  [body(): returned = lax.all_to_all(back, ('grp', 'tp'), 0, 0, tiled=True)]
    all_to_all x1 -> x0, starting transfers between devices: 6.16 us -> none  [body(): returned = lax.all_to_all(back, ('grp', 'tp'), 0, 0, tiled=True)]
    pallas_call x8 -> x7, Pallas kernels: 11.3 us -> 6.64 us  [call(): return made(*args)]
  transfers between devices with their start and end apart: 4 -> 3, of which waited for: 4 -> 3; matrix products, arithmetic and copies ran while one was open for 0% -> 0% of each run, Pallas kernels for 0% -> 0%
where the time goes in v4:
time: 79.8 us; the launch traced here: 79.5 us
  blocking collectives  63.6 us (80%)
  Pallas kernels  6.64 us (8%)
  starting transfers between devices  6.08 us (8%)
  waiting for transfers between devices  3.15 us (4%)
    all_to_all x1, blocking collectives, body(): every = lax.all_to_all(sent, 'grp', 0, 0, tiled=True)  21 us
    all_to_all x1, blocking collectives, body(): returned = lax.all_to_all(back, ('grp', 'tp'), 0, 0, tiled=True)  19.5 us
    all_to_all x1, blocking collectives, body(): inbox = lax.all_to_all(outbox, 'grp', 0, 0, tiled=True)  14.1 us
    all_to_all x1, blocking collectives, body(): got = lax.all_to_all(message, 'tp', 0, 0, tiled=True)  8.99 us
    pallas_call x7, Pallas kernels, call(): return made(*args)  6.64 us
    ppermute x1, starting transfers between devices, body(): lax.ppermute(inbox, 'side', swap)  3.5 us
    ppermute x2, starting transfers between devices, body(): lax.ppermute(give, 'side', swap)  2.58 us
    ppermute x2, waiting for transfers between devices, body(): lax.ppermute(give, 'side', swap)  1.98 us
  transfers between devices with their start and end apart: 3, of which 3 were waited for; matrix products, arithmetic and copies ran while one was open for 0% of the time, Pallas kernels for 0%

profile of v4, /device:TPU:1, one launch (start us, length us, event | category | flops | bytes accessed | tf_op | source)
XLA Modules:
  0.0 79.5 jit_solution(15928641014349067388)
XLA Ops:
  0.0 1.9 %shard_map.136 = (bf16[32,16,128]{2,1,0:T(8,128)(2,1)S(1)}, bf16[192,512]{1,0:T(8,128)(2,1)S(1)}, f32[4,128]{1,0:T(4,128)S(1)}, bf16[16,256]{1,0:T(8,128)(2,1)S(...) custom-call(bf16[4,4,128]{2,1,0:T(4,128)(2,1)} %q_hbm.1, bf16[4,4,128]{2,1,0:T(4,128)(2,1)} %k_hbm.1, ...), custom_call_target="tpu_custom_call" | custom-call | flops 1000000 | bytes 1200000 | tf_op jit(solution)/shard_map/pallas_call | solution.py:255
  1.9 21.0 %all_to_all.20.x_ref = bf16[32,16,128]{2,1,0:T(8,128)(2,1)S(1)} all-to-all(bf16[32,16,128]{2,1,0:T(8,128)(2,1)S(1)} %get-tuple-element.17), channel_id=1, replica_groups=mesh['side'=2,'grp'=32,'tp'=4] {'grp'}, dimensions={0} | all-to-all | bytes 262144 | tf_op jit(solution)/shard_map/all_to_all | solution.py:317
  22.9 0.2 shard_map.137
  23.1 2.1 %collective-permute-start = (f32[64,256]{1,0:T(8,128)S(1)}, f32[64,256]{1,0:T(8,128)S(1)}, u32[]{:S(2)}, u32[]{:S(2)}) collective-permute-start(f32[64,256]{1,0:T(8,128)S(1)} %get-tuple-element.21), channel_id=1, source_target_pairs={{0,128},{128,0},{1,129},{129,1},{2,130},{130,2},{3,131},{131,3},{4... | collective-permute-start | bytes 196616 | tf_op jit(solution)/shard_map/ppermute | solution.py:331
  25.3 0.9 %collective-permute-done.other_ref = f32[64,256]{1,0:T(8,128)S(1)} collective-permute-done((f32[64,256]{1,0:T(8,128)S(1)}, f32[64,256]{1,0:T(8,128)S(1)}, u32[]{:S(2)}, u32[]{:S(2)}) %collective-permute-start) | collective-permute-done | bytes 65568 | tf_op jit(solution)/shard_map/ppermute | solution.py:331
  26.2 0.1 shard_map.138
  26.3 9.0 %all_to_all.21.x_ref = bf16[4,80,256]{2,1,0:T(8,128)(2,1)S(1)} all-to-all(bf16[4,80,256]{2,1,0:T(8,128)(2,1)S(1)} %shard_map.138), channel_id=1, replica_groups=mesh['side'=2,'grp'=32,'tp'=4] {'tp'}, dimensions={0} | all-to-all | bytes 327680 | tf_op jit(solution)/shard_map/all_to_all | solution.py:335
  35.3 0.0 copy-start
  35.3 0.0 copy-start.1
  35.3 0.0 copy-start.2
  35.3 0.5 shard_map.139
  35.7 14.1 %all_to_all.22.mine_ref = bf16[32,16,256]{2,1,0:T(8,128)(2,1)S(1)} all-to-all(bf16[32,16,256]{2,1,0:T(8,128)(2,1)S(1)} %get-tuple-element.24), channel_id=1, replica_groups=mesh['side'=2,'grp'=32,'tp'=4] {'grp'}, dimensions={0} | all-to-all | bytes 524288 | tf_op jit(solution)/shard_map/all_to_all | solution.py:345
  49.8 3.5 %collective-permute-start.1 = (bf16[32,16,256]{2,1,0:T(8,128)(2,1)S(1)}, bf16[32,16,256]{2,1,0:T(8,128)(2,1)S(1)}, u32[]{:S(2)}, u32[]{:S(2)}) collective-permute-start(bf16[32,16,256]{2,1,0:T(8,128)(2,1)S(1)} %all_to_all.22.mine_ref), channel_id=1, source_target_pairs={{0,128},{128,0},{1,129},{129,1},{2,130},{130,2},{3,131},{131,3},{4... | collective-permute-start | bytes 786440 | tf_op jit(solution)/shard_map/ppermute | solution.py:350
  53.3 1.2 %collective-permute-done.1.other_ref = bf16[32,16,256]{2,1,0:T(8,128)(2,1)S(1)} collective-permute-done((bf16[32,16,256]{2,1,0:T(8,128)(2,1)S(1)}, bf16[32,16,256]{2,1,0:T(8,128)(2,1)S(1)}, u32[]{:S(2)}, u32[]{:S(2)}) %collective-permute-start.1) | collective-permute-done | bytes 262176 | tf_op jit(solution)/shard_map/ppermute | solution.py:350
  54.5 0.0 copy-done
  54.5 0.0 copy-done.1
  54.5 0.0 copy-done.2
  54.5 3.0 %shard_map.140 = (f32[16,6144]{1,0:T(8,128)S(1)}, bf16[16,6144]{1,0:T(8,128)(2,1)S(1)}) custom-call(bf16[32,16,256]{2,1,0:T(8,128)(2,1)S(1)} %all_to_all.22.mine_ref, bf16[32,16,256]{2,1,0:T(8,128)(2,1)S(1)} %collective-permute-done.1.other_ref, bf16[288,6144]{1,0:T(8,128)(2,1)S(1)} %bitcast.12, bf16[288,6144]{1,0:T(8,128)(2,1)S(1)} %bitcast.13, ...), custom_call_target="tpu_custom_call" | custom-call | flops 400000000 | bytes 11000000 | tf_op jit(solution)/shard_map/pallas_call | solution.py:255
  57.5 0.4 collective-permute-start.2
  58.0 1.1 %collective-permute-done.2.other_ref = bf16[16,6144]{1,0:T(8,128)(2,1)S(1)} collective-permute-done((bf16[16,6144]{1,0:T(8,128)(2,1)S(1)}, bf16[16,6144]{1,0:T(8,128)(2,1)S(1)}, u32[]{:S(2)}, u32[]{:S(2)}) %collective-permute-start.2) | collective-permute-done | bytes 196640 | tf_op jit(solution)/shard_map/ppermute | solution.py:360
  59.0 0.1 shard_map.141
  59.1 19.5 %all_to_all.23.x_ref = bf16[128,8,128]{2,1,0:T(8,128)(2,1)S(1)} all-to-all(bf16[128,8,128]{2,1,0:T(8,128)(2,1)S(1)} %shard_map.141), channel_id=1, replica_groups=mesh['side'=2,'grp'=32,'tp'=4] {'grp','tp'}, dimensions={0} | all-to-all | bytes 524288 | tf_op jit(solution)/shard_map/all_to_all | solution.py:364
  78.6 0.9 %shard_map.142 = bf16[16,192]{1,0:T(8,128)(2,1)} custom-call(bf16[128,8,128]{2,1,0:T(8,128)(2,1)S(1)} %all_to_all.23.x_ref, bf16[96,1024]{1,0:T(8,128)(2,1)S(1)} %get-tuple-element.27.table_ref, f32[16,256]{1,0:T(8,128)S(1)} %get-tuple-element.28.own_ref), custom_call_target="tpu_custom_call" | custom-call | flops 30000000 | bytes 500000 | tf_op jit(solution)/shard_map/pallas_call | solution.py:255
Async XLA Ops:
  23.1 3.1 %collective-permute-start = (f32[64,256]{1,0:T(8,128)S(1)}, f32[64,256]{1,0:T(8,128)S(1)}, u32[]{:S(2)}, u32[]{:S(2)}) collective-permute-start(f32[64,256]{1,0:T(8,128)S(1)} %get-tuple-element.21), channel_id=1, source_target_pairs={{0,128},{128,0},{1,129},{129,1},{2,130},{130,2},{3,131},{131,3},{4... | collective-permute-start | bytes 196616 | tf_op jit(solution)/shard_map/ppermute | solution.py:331
  35.3 19.2 %copy-start = (bf16[1,6144,288]{1,2,0:T(8,128)(2,1)S(1)}, bf16[1,6144,288]{1,2,0:T(8,128)(2,1)}, u32[]{:S(2)}) copy-start(bf16[1,6144,288]{1,2,0:T(8,128)(2,1)} %param.23) | copy-start | bytes 10616836
  35.3 19.2 %copy-start.1 = (bf16[1,6144,288]{1,2,0:T(8,128)(2,1)S(1)}, bf16[1,6144,288]{1,2,0:T(8,128)(2,1)}, u32[]{:S(2)}) copy-start(bf16[1,6144,288]{1,2,0:T(8,128)(2,1)} %param.24) | copy-start | bytes 10616836
  35.3 19.2 %copy-start.2 = (bf16[1,288,6144]{2,1,0:T(8,128)(2,1)S(1)}, bf16[1,288,6144]{2,1,0:T(8,128)(2,1)}, u32[]{:S(2)}) copy-start(bf16[1,288,6144]{2,1,0:T(8,128)(2,1)} %param.25) | copy-start | bytes 10616836
  49.8 4.7 %collective-permute-start.1 = (bf16[32,16,256]{2,1,0:T(8,128)(2,1)S(1)}, bf16[32,16,256]{2,1,0:T(8,128)(2,1)S(1)}, u32[]{:S(2)}, u32[]{:S(2)}) collective-permute-start(bf16[32,16,256]{2,1,0:T(8,128)(2,1)S(1)} %all_to_all.22.mine_ref), channel_id=1, source_target_pairs={{0,128},{128,0},{1,129},{129,1},{2,130},{130,2},{3,131},{131,3},{4... | collective-permute-start | bytes 786440 | tf_op jit(solution)/shard_map/ppermute | solution.py:350
  57.5 1.5 %collective-permute-start.2 = (bf16[16,6144]{1,0:T(8,128)(2,1)S(1)}, bf16[16,6144]{1,0:T(8,128)(2,1)S(1)}, u32[]{:S(2)}, u32[]{:S(2)}) collective-permute-start(bf16[16,6144]{1,0:T(8,128)(2,1)S(1)} %get-tuple-element.26), channel_id=1, source_target_pairs={{0,128},{128,0},{1,129},{129,1},{2,130},{130,2},{3,131},{131,3},{4... | collective-permute-start | bytes 589832 | tf_op jit(solution)/shard_map/ppermute | solution.py:360

commit v5 on v4

--- a/solution.py
+++ b/solution.py
@@ -14,10 +14,11 @@
 RB = 16
 LANES = 256
 DEEP = 6
-WIDE = 4
+WIDE = 8
+
+STEPS = (1, 3, 2)
 
 epsilon = 1e-06
-BLOCK = ("side", "tp")
 f32, bf16 = jnp.float32, jnp.bfloat16
 VM = pl.BlockSpec(memory_space=pltpu.VMEM)
 HB = pl.BlockSpec(memory_space=pltpu.HBM)
@@ -108,27 +109,30 @@
     other_ref[...] = jnp.where(first, table[half:], table[:half])
 
 
-def gather_side(width, mine_ref, other_ref, own_ref, out_ref):
+def gather_side(width, mine_ref, other_ref, own_ref, out_ref, sum_ref):
     half = mine_ref.shape[0]
     lane = iota((1, LANES), 1)
     table = mine_ref[...] + other_ref[...]
+    sum_ref[...] = table
     squares = jnp.sum(jnp.where(lane == width, table, 0.0), axis=1, keepdims=True)
     high, low = halves(squares)
     table = jnp.where(lane == width, high, jnp.where(lane == width + 1, low, table)).astype(bf16)
-    for t in range(out_ref.shape[0]):
-        out_ref[t, :half, :] = table
-        out_ref[t, half:, :] = own_ref[...]
-
-
-def dispatch(width, x_ref, gain_ref, out_ref, own_ref, scratch_ref):
-    half = x_ref.shape[1] - RB
+    out_ref[:half, :] = table
+    out_ref[half:, :] = own_ref[...]
+
+
+def dispatch(width, sum_ref, mine_ref, a_ref, b_ref, c_ref, gain_ref, out_ref, own_ref, rest_ref, scratch_ref):
+    half = sum_ref.shape[0]
     tp, odd = lax.axis_index("tp"), lax.rem(lax.axis_index("grp"), 2)
     lane = iota((1, LANES), 1)
-    summed = x_ref[0, :half, :].astype(f32)
-    for t in range(1, 4):
-        summed = summed + x_ref[t, :half, :].astype(f32)
+    summed = sum_ref[...]
+    rest_ref[pl.ds(pl.multiple_of(tp * RB, RB), RB), :] = mine_ref[...].astype(f32)
+    for step, ref in zip(STEPS, (a_ref, b_ref, c_ref)):
+        summed = summed + ref[:half, :].astype(f32)
+        source = lax.rem(tp + 4 - step, 4)
+        rest_ref[pl.ds(pl.multiple_of(source * RB, RB), RB), :] = ref[half:, :].astype(f32)
     squares = jnp.sum(jnp.where((lane == width) | (lane == width + 1), summed, 0.0), axis=1, keepdims=True)
-    rest = jnp.concatenate([x_ref[t, half:, :].astype(f32) for t in range(4)], axis=0)
+    rest = rest_ref[...]
     hidden = jnp.where(lane < width, rest + lax.rsqrt(squares / (HEADS * HEAD_DIM) + epsilon) * summed, 0.0)
     scratch_ref[...] = hidden
     own_ref[...] = scratch_ref[pl.ds(pl.multiple_of(tp * RB, RB), RB), :]
@@ -155,44 +159,39 @@
         out_ref[2 * e + 1] = piece
 
 
-def prefetch(after_ref, far_ref, near_ref, token_ref, sem):
-    copy = pltpu.make_async_copy(far_ref, near_ref, sem)
-    copy.start()
-    token_ref[...] = jnp.zeros_like(token_ref)
-    copy.wait()
-
-
-def experts(mine_ref, other_ref, gate_ref, up_ref, down_ref, keep_ref, give_ref, x_ref, feature_ref):
-    groups, rows, _ = mine_ref.shape
-    side = lax.axis_index("side")
+def stage(in_ref, x_ref, feature_ref):
+    groups, rows, _ = in_ref.shape
     low_lane = iota((rows, 128), 1) < 64
-    for ref, at in ((mine_ref, side), (other_ref, 1 - side)):
-        start = pl.multiple_of(at * rows, rows)
-        feature = jnp.zeros((rows, 128), f32)
-        for i in range(groups // 2):
-            b_even = ref[2 * i, :, 128:].astype(f32)
-            b_odd = ref[2 * i + 1, :, :128].astype(f32)
-            feature = feature + jnp.where(low_lane, b_odd, b_even)
-            x_ref[pl.ds(start, rows), 384 * i : 384 * i + 128] = ref[2 * i, :, :128]
-            x_ref[pl.ds(start, rows), 384 * i + 128 : 384 * i + 256] = jnp.where(low_lane, b_even, b_odd).astype(bf16)
-            x_ref[pl.ds(start, rows), 384 * i + 256 : 384 * i + 384] = ref[2 * i + 1, :, 128:]
-        feature_ref[pl.ds(start, rows), :] = feature
-    scale = lax.rsqrt(jnp.sum(feature_ref[...], axis=1, keepdims=True) / D + epsilon)
-    gate = jnp.zeros((2 * rows, gate_ref.shape[0]), f32)
+    feature = jnp.zeros((rows, 128), f32)
+    for i in range(groups // 2):
+        b_even = in_ref[2 * i, :, 128:].astype(f32)
+        b_odd = in_ref[2 * i + 1, :, :128].astype(f32)
+        feature = feature + jnp.where(low_lane, b_odd, b_even)
+        x_ref[:, 384 * i : 384 * i + 128] = in_ref[2 * i, :, :128]
+        x_ref[:, 384 * i + 128 : 384 * i + 256] = jnp.where(low_lane, b_even, b_odd).astype(bf16)
+        x_ref[:, 384 * i + 256 : 384 * i + 384] = in_ref[2 * i + 1, :, 128:]
+    feature_ref[...] = feature
+
+
+def experts(x_ref, feature_ref, other_ref, gate_ref, up_ref, down_ref, keep_ref, give_ref, x2_ref, feature2_ref):
+    rows = x_ref.shape[0]
+    stage(other_ref, x2_ref, feature2_ref)
+    feature = jnp.concatenate([feature_ref[...], feature2_ref[...]], axis=0)
+    scale = lax.rsqrt(jnp.sum(jnp.transpose(feature), axis=0, keepdims=True) / D + epsilon)
+    gate = jnp.zeros((gate_ref.shape[0], 2 * rows), f32)
     up = gate
     for n in range(DEEP):
         part = slice(n * D // DEEP, (n + 1) * D // DEEP)
-        x = x_ref[:, part]
-        gate = gate + lax.dot_general(x, gate_ref[:, part], MINOR, preferred_element_type=f32)
-        up = up + lax.dot_general(x, up_ref[:, part], MINOR, preferred_element_type=f32)
+        x = jnp.concatenate([x_ref[:, part], x2_ref[:, part]], axis=0)
+        gate = gate + lax.dot_general(gate_ref[:, part], x, MINOR, preferred_element_type=f32)
+        up = up + lax.dot_general(up_ref[:, part], x, MINOR, preferred_element_type=f32)
     gate, up = scale * gate, scale * up
-    hidden = (gate * jax.nn.sigmoid(gate) * up).astype(bf16)
-    first = side == 0
+    hidden = jnp.transpose(gate * jax.nn.sigmoid(gate) * up).astype(bf16)
     for n in range(WIDE):
         part = slice(n * D // WIDE, (n + 1) * D // WIDE)
         chunk = jnp.dot(hidden, down_ref[:, part], preferred_element_type=f32)
-        keep_ref[:, part] = jnp.where(first, chunk[:rows], chunk[rows:])
-        give_ref[:, part] = jnp.where(first, chunk[rows:], chunk[:rows]).astype(bf16)
+        keep_ref[:, part] = chunk[:rows]
+        give_ref[:, part] = chunk[rows:].astype(bf16)
 
 
 def spread(keep_ref, other_ref, out_ref):
@@ -253,18 +252,6 @@
         cost_estimate=pl.CostEstimate(flops=flops, bytes_accessed=moved, transcendentals=0),
     )
     return made(*args)
-
-
-def fetch(after, x):
-    near, token = call(
-        prefetch,
-        [pltpu.VMEM(x.shape, x.dtype), shape((8, 128), f32)],
-        [VM, HB],
-        (after, far(x)),
-        scratch=[pltpu.SemaphoreType.DMA],
-        moved=4 * x.size,
-    )
-    return pltpu.with_memory_space_constraint(near, pltpu.VMEM), token
 
 
 def shape(dims, dtype):
@@ -324,31 +311,33 @@
         flops=25 * 10**6,
         moved=700000,
     )
-    message = call(
+    message, summed = call(
         functools.partial(gather_side, width),
-        shape((4, half + RB, LANES), bf16),
+        [shape((half + RB, LANES), bf16), shape((half, LANES), f32)],
         [VM] * 3,
         (mine, lax.ppermute(give, "side", swap), own_rows),
         flops=10**6,
         moved=400000,
     )
-    got = lax.all_to_all(message, "tp", 0, 0, tiled=True)
+    got = [lax.ppermute(message, "tp", [(t, (t + step) % 4) for t in range(4)]) for step in STEPS]
     outbox, own_hidden = call(
         functools.partial(dispatch, width),
         [shape((groups, 4 * CAP, LANES), bf16), shape((RB, LANES), f32)],
-        [VM, VM],
-        (got, moe_near),
-        scratch=[pltpu.VMEM((half, LANES), f32)],
+        [VM] * 6,
+        (summed, own_rows, *got, moe_near),
+        scratch=[pltpu.VMEM((half, LANES), f32)] * 2,
         flops=3 * 10**10,
         moved=700000,
     )
     inbox = lax.all_to_all(outbox, "grp", 0, 0, tiled=True)
+    staged = [shape((4 * CAP, D), bf16), shape((4 * CAP, 128), f32)]
+    x_mine, feature = call(stage, staged, [VM], (inbox,), flops=10**6, moved=500000)
     keep, give = call(
         experts,
         [shape((4 * CAP, D), f32), shape((4 * CAP, D), bf16)],
-        [VM] * 5,
-        (inbox, lax.ppermute(inbox, "side", swap), w_gate[0].T, w_up[0].T, w_down[0]),
-        scratch=[pltpu.VMEM((8 * CAP, D), bf16), pltpu.VMEM((8 * CAP, 128), f32)],
+        [VM] * 6,
+        (x_mine, feature, lax.ppermute(inbox, "side", swap), w_gate[0].T, w_up[0].T, w_down[0]),
+        scratch=[pltpu.VMEM(x.shape, x.dtype) for x in staged],
         flops=4 * 10**8,
         moved=11000000,
         limit=12,

time: 79.8 us -> 78.4 us (0.982)
  blocking collectives: 63.6 us -> 54.6 us
  starting transfers between devices: 6.08 us -> 10.6 us
  waiting for transfers between devices: 3.15 us -> 6.46 us
    all_to_all x1 -> x0, blocking collectives: 8.99 us -> none  [body(): got = lax.all_to_all(message, 'tp', 0, 0, tiled=True)]
    ppermute x0 -> x3, starting transfers between devices: none -> 4.47 us  [body(): lax.ppermute(message, 'tp', [(t, (t + step) % 4) for t in range(4)])]
    ppermute x0 -> x3, waiting for transfers between devices: none -> 3.37 us  [body(): lax.ppermute(message, 'tp', [(t, (t + step) % 4) for t in range(4)])]
    pallas_call x7 -> x8, Pallas kernels: 6.64 us -> 6.42 us  [call(): return made(*args)]
  transfers between devices with their start and end apart: 3 -> 6, of which waited for: 3 -> 5; matrix products, arithmetic and copies ran while one was open for 0% -> 0% of each run, Pallas kernels for 0% -> 0%
where the time goes in v5:
time: 78.4 us; the launch traced here: 78.2 us
  blocking collectives  54.6 us (70%)
  starting transfers between devices  10.6 us (14%)
  waiting for transfers between devices  6.46 us (8%)
  Pallas kernels  6.42 us (8%)
    all_to_all x1, blocking collectives, body(): every = lax.all_to_all(sent, 'grp', 0, 0, tiled=True)  21 us
    all_to_all x1, blocking collectives, body(): returned = lax.all_to_all(back, ('grp', 'tp'), 0, 0, tiled=True)  19.5 us
    all_to_all x1, blocking collectives, body(): inbox = lax.all_to_all(outbox, 'grp', 0, 0, tiled=True)  14.1 us
    pallas_call x8, Pallas kernels, call(): return made(*args)  6.42 us
    ppermute x3, starting transfers between devices, body(): lax.ppermute(message, 'tp', [(t, (t + step) % 4) for t in range(4)])  4.47 us
    ppermute x1, starting transfers between devices, body(): lax.ppermute(inbox, 'side', swap)  3.57 us
    ppermute x3, waiting for transfers between devices, body(): lax.ppermute(message, 'tp', [(t, (t + step) % 4) for t in range(4)])  3.37 us
    ppermute x2, starting transfers between devices, body(): lax.ppermute(give, 'side', swap)  2.58 us
  transfers between devices with their start and end apart: 6, of which 5 were waited for; matrix products, arithmetic and copies ran while one was open for 0% of the time, Pallas kernels for 0%

profile of v5, /device:TPU:1, one launch (start us, length us, event | category | flops | bytes accessed | tf_op | source)
XLA Modules:
  0.0 78.2 jit_solution(4617823201966896360)
XLA Ops:
  0.0 1.9 %shard_map.136 = (bf16[32,16,128]{2,1,0:T(8,128)(2,1)S(1)}, bf16[192,512]{1,0:T(8,128)(2,1)S(1)}, f32[4,128]{1,0:T(4,128)S(1)}, bf16[16,256]{1,0:T(8,128)(2,1)S(...) custom-call(bf16[4,4,128]{2,1,0:T(4,128)(2,1)} %q_hbm.1, bf16[4,4,128]{2,1,0:T(4,128)(2,1)} %k_hbm.1, ...), custom_call_target="tpu_custom_call" | custom-call | flops 1000000 | bytes 1200000 | tf_op jit(solution)/shard_map/pallas_call | solution.py:254
  1.9 21.0 %all_to_all.15.x_ref = bf16[32,16,128]{2,1,0:T(8,128)(2,1)S(1)} all-to-all(bf16[32,16,128]{2,1,0:T(8,128)(2,1)S(1)} %get-tuple-element.21), channel_id=1, replica_groups=mesh['side'=2,'grp'=32,'tp'=4] {'grp'}, dimensions={0} | all-to-all | bytes 262144 | tf_op jit(solution)/shard_map/all_to_all | solution.py:304
  22.9 0.2 shard_map.137
  23.1 2.1 %collective-permute-start = (f32[64,256]{1,0:T(8,128)S(1)}, f32[64,256]{1,0:T(8,128)S(1)}, u32[]{:S(2)}, u32[]{:S(2)}) collective-permute-start(f32[64,256]{1,0:T(8,128)S(1)} %get-tuple-element.25), channel_id=1, source_target_pairs={{0,128},{128,0},{1,129},{129,1},{2,130},{130,2},{3,131},{131,3},{4... | collective-permute-start | bytes 196616 | tf_op jit(solution)/shard_map/ppermute | solution.py:318
  25.3 0.9 %collective-permute-done.other_ref = f32[64,256]{1,0:T(8,128)S(1)} collective-permute-done((f32[64,256]{1,0:T(8,128)S(1)}, f32[64,256]{1,0:T(8,128)S(1)}, u32[]{:S(2)}, u32[]{:S(2)}) %collective-permute-start) | collective-permute-done | bytes 65568 | tf_op jit(solution)/shard_map/ppermute | solution.py:318
  26.2 0.1 shard_map.138
  26.3 3.0 %collective-permute-start.3 = (bf16[80,256]{1,0:T(8,128)(2,1)S(1)}, bf16[80,256]{1,0:T(8,128)(2,1)S(1)}, u32[]{:S(2)}, u32[]{:S(2)}) collective-permute-start(bf16[80,256]{1,0:T(8,128)(2,1)S(1)} %get-tuple-element.28), channel_id=1, source_target_pairs={{0,2},{1,3},{2,0},{3,1},{4,6},{5,7},{6,4},{7,5},{8,10},{9,11},{10,... | collective-permute-start | bytes 122888 | tf_op jit(solution)/shard_map/ppermute | solution.py:322
  29.3 0.8 collective-permute-start.2
  30.0 0.7 collective-permute-start.1
  30.7 0.0 collective-permute-done.3.c_ref
  30.7 1.6 %collective-permute-done.2.b_ref = bf16[80,256]{1,0:T(8,128)(2,1)S(1)} collective-permute-done((bf16[80,256]{1,0:T(8,128)(2,1)S(1)}, bf16[80,256]{1,0:T(8,128)(2,1)S(1)}, u32[]{:S(2)}, u32[]{:S(2)}) %collective-permute-start.2) | collective-permute-done | bytes 40992 | tf_op jit(solution)/shard_map/ppermute | solution.py:322
  32.3 1.8 %collective-permute-done.1.a_ref = bf16[80,256]{1,0:T(8,128)(2,1)S(1)} collective-permute-done((bf16[80,256]{1,0:T(8,128)(2,1)S(1)}, bf16[80,256]{1,0:T(8,128)(2,1)S(1)}, u32[]{:S(2)}, u32[]{:S(2)}) %collective-permute-start.1) | collective-permute-done | bytes 40992 | tf_op jit(solution)/shard_map/ppermute | solution.py:322
  34.1 0.5 shard_map.139
  34.6 14.1 %all_to_all.16.in_ref = bf16[32,16,256]{2,1,0:T(8,128)(2,1)S(1)} all-to-all(bf16[32,16,256]{2,1,0:T(8,128)(2,1)S(1)} %get-tuple-element.30), channel_id=1, replica_groups=mesh['side'=2,'grp'=32,'tp'=4] {'grp'}, dimensions={0} | all-to-all | bytes 524288 | tf_op jit(solution)/shard_map/all_to_all | solution.py:332
  48.7 3.6 %collective-permute-start.4 = (bf16[32,16,256]{2,1,0:T(8,128)(2,1)S(1)}, bf16[32,16,256]{2,1,0:T(8,128)(2,1)S(1)}, u32[]{:S(2)}, u32[]{:S(2)}) collective-permute-start(bf16[32,16,256]{2,1,0:T(8,128)(2,1)S(1)} %all_to_all.16.in_ref), channel_id=1, source_target_pairs={{0,128},{128,0},{1,129},{129,1},{2,130},{130,2},{3,131},{131,3},{4... | collective-permute-start | bytes 786440 | tf_op jit(solution)/shard_map/ppermute | solution.py:339
  52.3 1.1 %collective-permute-done.4.other_ref = bf16[32,16,256]{2,1,0:T(8,128)(2,1)S(1)} collective-permute-done((bf16[32,16,256]{2,1,0:T(8,128)(2,1)S(1)}, bf16[32,16,256]{2,1,0:T(8,128)(2,1)S(1)}, u32[]{:S(2)}, u32[]{:S(2)}) %collective-permute-start.4) | collective-permute-done | bytes 262176 | tf_op jit(solution)/shard_map/ppermute | solution.py:339
  53.4 0.0 copy-done
  53.4 0.0 copy-done.1
  53.4 2.8 %shard_map.141 = (f32[16,6144]{1,0:T(8,128)S(1)}, bf16[16,6144]{1,0:T(8,128)(2,1)S(1)}) custom-call(bf16[16,6144]{1,0:T(8,128)(2,1)S(1)} %get-tuple-element.31.x_ref, f32[16,128]{1,0:T(8,128)S(1)} %get-tuple-element.32.feature_ref, bf16[32,16,256]{2,1,0:T(8,128)(2,1)S(1)} %collective-permute-done.4.other_ref, bf16[288,6144]{1,0:T(8,128)(2,1)S(1)} %bitcast.12, ...), custom_call_target="tpu_custom_call" | custom-call | flops 400000000 | bytes 11000000 | tf_op jit(solution)/shard_map/pallas_call | solution.py:254
  56.2 0.4 collective-permute-start.5
  56.6 1.1 %collective-permute-done.5.other_ref = bf16[16,6144]{1,0:T(8,128)(2,1)S(1)} collective-permute-done((bf16[16,6144]{1,0:T(8,128)(2,1)S(1)}, bf16[16,6144]{1,0:T(8,128)(2,1)S(1)}, u32[]{:S(2)}, u32[]{:S(2)}) %collective-permute-start.5) | collective-permute-done | bytes 196640 | tf_op jit(solution)/shard_map/ppermute | solution.py:349
  57.7 0.1 shard_map.142
  57.8 19.5 %all_to_all.17.x_ref = bf16[128,8,128]{2,1,0:T(8,128)(2,1)S(1)} all-to-all(bf16[128,8,128]{2,1,0:T(8,128)(2,1)S(1)} %shard_map.142), channel_id=1, replica_groups=mesh['side'=2,'grp'=32,'tp'=4] {'grp','tp'}, dimensions={0} | all-to-all | bytes 524288 | tf_op jit(solution)/shard_map/all_to_all | solution.py:353
  77.3 0.9 %shard_map.143 = bf16[16,192]{1,0:T(8,128)(2,1)} custom-call(bf16[128,8,128]{2,1,0:T(8,128)(2,1)S(1)} %all_to_all.17.x_ref, bf16[96,1024]{1,0:T(8,128)(2,1)S(1)} %get-tuple-element.35.table_ref, f32[16,256]{1,0:T(8,128)S(1)} %get-tuple-element.36.own_ref), custom_call_target="tpu_custom_call" | custom-call | flops 30000000 | bytes 500000 | tf_op jit(solution)/shard_map/pallas_call | solution.py:254
  (5 shorter events, 0.0 us)
Async XLA Ops:
  23.1 3.1 %collective-permute-start = (f32[64,256]{1,0:T(8,128)S(1)}, f32[64,256]{1,0:T(8,128)S(1)}, u32[]{:S(2)}, u32[]{:S(2)}) collective-permute-start(f32[64,256]{1,0:T(8,128)S(1)} %get-tuple-element.25), channel_id=1, source_target_pairs={{0,128},{128,0},{1,129},{129,1},{2,130},{130,2},{3,131},{131,3},{4... | collective-permute-start | bytes 196616 | tf_op jit(solution)/shard_map/ppermute | solution.py:318
  26.3 4.5 %collective-permute-start.3 = (bf16[80,256]{1,0:T(8,128)(2,1)S(1)}, bf16[80,256]{1,0:T(8,128)(2,1)S(1)}, u32[]{:S(2)}, u32[]{:S(2)}) collective-permute-start(bf16[80,256]{1,0:T(8,128)(2,1)S(1)} %get-tuple-element.28), channel_id=1, source_target_pairs={{0,2},{1,3},{2,0},{3,1},{4,6},{5,7},{6,4},{7,5},{8,10},{9,11},{10,... | collective-permute-start | bytes 122888 | tf_op jit(solution)/shard_map/ppermute | solution.py:322
  29.3 3.0 %collective-permute-start.2 = (bf16[80,256]{1,0:T(8,128)(2,1)S(1)}, bf16[80,256]{1,0:T(8,128)(2,1)S(1)}, u32[]{:S(2)}, u32[]{:S(2)}) collective-permute-start(bf16[80,256]{1,0:T(8,128)(2,1)S(1)} %get-tuple-element.28), channel_id=1, source_target_pairs={{0,3},{1,0},{2,1},{3,2},{4,7},{5,4},{6,5},{7,6},{8,11},{9,8},{10,9... | collective-permute-start | bytes 122888 | tf_op jit(solution)/shard_map/ppermute | solution.py:322
  30.0 4.1 %collective-permute-start.1 = (bf16[80,256]{1,0:T(8,128)(2,1)S(1)}, bf16[80,256]{1,0:T(8,128)(2,1)S(1)}, u32[]{:S(2)}, u32[]{:S(2)}) collective-permute-start(bf16[80,256]{1,0:T(8,128)(2,1)S(1)} %get-tuple-element.28), channel_id=1, source_target_pairs={{0,1},{1,2},{2,3},{3,0},{4,5},{5,6},{6,7},{7,4},{8,9},{9,10},{10,1... | collective-permute-start | bytes 122888 | tf_op jit(solution)/shard_map/ppermute | solution.py:322
  34.1 19.3 %copy-start = (bf16[1,6144,288]{1,2,0:T(8,128)(2,1)S(1)}, bf16[1,6144,288]{1,2,0:T(8,128)(2,1)}, u32[]{:S(2)}) copy-start(bf16[1,6144,288]{1,2,0:T(8,128)(2,1)} %param.23) | copy-start | bytes 10616836
  34.1 19.3 %copy-start.1 = (bf16[1,6144,288]{1,2,0:T(8,128)(2,1)S(1)}, bf16[1,6144,288]{1,2,0:T(8,128)(2,1)}, u32[]{:S(2)}) copy-start(bf16[1,6144,288]{1,2,0:T(8,128)(2,1)} %param.24) | copy-start | bytes 10616836
  34.1 19.3 %copy-start.2 = (bf16[1,288,6144]{2,1,0:T(8,128)(2,1)S(1)}, bf16[1,288,6144]{2,1,0:T(8,128)(2,1)}, u32[]{:S(2)}) copy-start(bf16[1,288,6144]{2,1,0:T(8,128)(2,1)} %param.25) | copy-start | bytes 10616836
  48.7 4.7 %collective-permute-start.4 = (bf16[32,16,256]{2,1,0:T(8,128)(2,1)S(1)}, bf16[32,16,256]{2,1,0:T(8,128)(2,1)S(1)}, u32[]{:S(2)}, u32[]{:S(2)}) collective-permute-start(bf16[32,16,256]{2,1,0:T(8,128)(2,1)S(1)} %all_to_all.16.in_ref), channel_id=1, source_target_pairs={{0,128},{128,0},{1,129},{129,1},{2,130},{130,2},{3,131},{131,3},{4... | collective-permute-start | bytes 786440 | tf_op jit(solution)/shard_map/ppermute | solution.py:339
  56.2 1.5 %collective-permute-start.5 = (bf16[16,6144]{1,0:T(8,128)(2,1)S(1)}, bf16[16,6144]{1,0:T(8,128)(2,1)S(1)}, u32[]{:S(2)}, u32[]{:S(2)}) collective-permute-start(bf16[16,6144]{1,0:T(8,128)(2,1)S(1)} %get-tuple-element.34), channel_id=1, source_target_pairs={{0,128},{128,0},{1,129},{129,1},{2,130},{130,2},{3,131},{131,3},{4... | collective-permute-start | bytes 589832 | tf_op jit(solution)/shard_map/ppermute | solution.py:349

commit v6 on v5

--- a/solution.py
+++ b/solution.py
@@ -17,6 +17,7 @@
 WIDE = 8
 
 STEPS = (1, 3, 2)
+BACK = (2, 3, 1)
 
 epsilon = 1e-06
 f32, bf16 = jnp.float32, jnp.bfloat16
@@ -40,50 +41,52 @@
 
 
 def attention(
-    q_hbm, k_hbm, v_hbm, kv_hbm, decay_hbm, gain_hbm, w_hbm, residual_hbm, moe_hbm, routes_hbm, weights_hbm,
-    out_ref, w_ref, gain_ref, own_ref, moe_ref, table_ref,
-    q_ref, k_ref, v_ref, kv_ref, decay_ref, residual_ref, routes_ref, weights_ref, narrow_ref, sems,
+    q_hbm, k_hbm, v_hbm, decay_hbm, gain_hbm, kv_hbm, w_hbm, residual_hbm, moe_hbm, routes_hbm, weights_hbm,
+    out_ref, gain_ref, w_ref, residual_ref, moe_ref, routes_ref, weights_ref,
+    q_ref, k_ref, v_ref, decay_ref, kv_ref, sems,
 ):
     sessions, heads = q_ref.shape[:2]
-    width = residual_ref.shape[1]
-    pairs = [(routes_hbm, routes_ref), (weights_hbm, weights_ref), (residual_hbm, residual_ref)]
-    pairs += [(q_hbm, q_ref), (k_hbm, k_ref), (v_hbm, v_ref), (decay_hbm, decay_ref), (gain_hbm, gain_ref)]
+    pairs = [(q_hbm, q_ref), (k_hbm, k_ref), (v_hbm, v_ref), (decay_hbm, decay_ref), (gain_hbm, gain_ref)]
     pairs += [(kv_hbm.at[s], kv_ref.at[s]) for s in range(sessions)]
-    pairs += [(moe_hbm, narrow_ref), (w_hbm, w_ref)]
+    pairs += [(w_hbm, w_ref), (residual_hbm, residual_ref), (moe_hbm, moe_ref)]
+    pairs += [(routes_hbm, routes_ref), (weights_hbm, weights_ref)]
     copies = [pltpu.make_async_copy(source, target, sems.at[i]) for i, (source, target) in enumerate(pairs)]
     for copy in copies:
         copy.start()
-    for copy in copies[:3]:
-        copy.wait()
-    routes = routes_ref[...].astype(f32)
-    combiner(routes, weights_ref[...], table_ref)
-    lane = iota((1, LANES), 1)
-    own = jnp.concatenate([residual_ref[...].astype(f32), jnp.zeros((RB, LANES - width), f32)], axis=1)
-    own = jnp.where(lane == width, column(routes[0:1], RB), jnp.where(lane == width + 1, column(routes[1:2], RB), own))
-    own_ref[...] = own.astype(bf16)
-    for copy in copies[3:8]:
+    for copy in copies[:5]:
         copy.wait()
     query = jnp.concatenate([q_ref[s].astype(f32) for s in range(sessions)], axis=0)
     key = jnp.concatenate([k_ref[s].astype(f32) for s in range(sessions)], axis=0)
     value = jnp.concatenate([v_ref[s].astype(f32) for s in range(sessions)], axis=0)
-    turned = jnp.transpose(query)
     dots = jnp.sum(query * key, axis=1, keepdims=True)
+    count = sessions * heads
+    ones = jnp.where(iota((count, count * HEAD_DIM), 1) // HEAD_DIM == iota((count, count * HEAD_DIM), 0), 1.0, 0.0)
+    turned = jnp.dot(jnp.transpose(query).astype(bf16), ones.astype(bf16), preferred_element_type=f32)
     rows = []
     for s in range(sessions):
-        copies[8 + s].wait()
+        copies[5 + s].wait()
         for h in range(heads):
             n = s * heads + h
-            read = jnp.sum(turned[:, n : n + 1] * kv_ref[s, h], axis=0, keepdims=True)
+            read = jnp.sum(turned[:, n * HEAD_DIM : (n + 1) * HEAD_DIM] * kv_ref[s, h], axis=0, keepdims=True)
             rows.append(decay_ref[:, h : h + 1] * read)
     attended = jnp.concatenate(rows, axis=0) + dots * value
     gain = jnp.concatenate([gain_ref[...]] * sessions, axis=0)
     message = (attended * gain).astype(bf16)
     for g in range(out_ref.shape[0]):
         out_ref[g] = message
-
-    for copy in copies[8 + sessions :]:
+    for copy in copies[5 + sessions :]:
         copy.wait()
-    moe_ref[...] = jnp.concatenate([narrow_ref[...], jnp.zeros((1, LANES - width), f32)], axis=1)
+
+
+def prepare(after_ref, residual_ref, moe_ref, routes_ref, weights_ref, own_ref, gain_ref, table_ref):
+    width = residual_ref.shape[1]
+    routes = routes_ref[...].astype(f32)
+    lane = iota((1, LANES), 1)
+    own = jnp.concatenate([residual_ref[...].astype(f32), jnp.zeros((RB, LANES - width), f32)], axis=1)
+    own = jnp.where(lane == width, column(routes[0:1], RB), jnp.where(lane == width + 1, column(routes[1:2], RB), own))
+    own_ref[...] = own.astype(bf16)
+    gain_ref[...] = jnp.concatenate([moe_ref[...], jnp.zeros((1, LANES - width), f32)], axis=1)
+    combiner(routes, weights_ref[...], table_ref)
 
 
 def project(x_ref, w_ref, gain_ref, mine_ref, other_ref, spread_ref):
@@ -194,23 +197,37 @@
         give_ref[:, part] = chunk[rows:].astype(bf16)
 
 
-def spread(keep_ref, other_ref, out_ref):
-    for i in range(D // 384):
-        a, b, c = (
-            keep_ref[:, 128 * n : 128 * n + 128] + other_ref[:, 128 * n : 128 * n + 128].astype(f32)
-            for n in range(3 * i, 3 * i + 3)
-        )
+def spread(keep_ref, other_ref, mine_ref, a_ref, b_ref, c_ref, total_ref):
+    tp = lax.axis_index("tp")
+    for n in range(WIDE):
+        part = slice(n * D // WIDE, (n + 1) * D // WIDE)
+        total = keep_ref[:, part] + other_ref[:, part].astype(f32)
         for t in range(4):
-            rows = slice(t * CAP, (t + 1) * CAP)
-            out_ref[(2 * i) * 4 + t] = jnp.concatenate([a[rows], b[rows]], axis=0).astype(bf16)
-            out_ref[(2 * i + 1) * 4 + t] = jnp.concatenate([b[rows], c[rows]], axis=0).astype(bf16)
+            total_ref[t, :, part] = total[t * CAP : (t + 1) * CAP]
+    span = mine_ref.shape[1]
+    for step, ref in zip((0,) + BACK, (mine_ref, a_ref, b_ref, c_ref)):
+        rows = total_ref[lax.rem(tp + step, 4)]
+        piece = jnp.concatenate([rows[:, q * span : (q + 1) * span] for q in range(4)], axis=0)
+        ref[...] = piece.astype(ref.dtype)
+
+
+def reduce_parts(mine_ref, a_ref, b_ref, c_ref, out_ref):
+    total = mine_ref[...]
+    for ref in (a_ref, b_ref, c_ref):
+        total = total + ref[...].astype(f32)
+    for q in range(4):
+        rows = total[q * CAP : (q + 1) * CAP]
+        for i in range(4):
+            a, b, c = (rows[:, 384 * i + 128 * n : 384 * i + 128 * (n + 1)] for n in range(3))
+            out_ref[q * 8 + 2 * i] = jnp.concatenate([a, b], axis=0).astype(out_ref.dtype)
+            out_ref[q * 8 + 2 * i + 1] = jnp.concatenate([b, c], axis=0).astype(out_ref.dtype)
 
 
 def combiner(routes, weights, out_ref):
     r0, r1 = column(routes[0:1], RB).astype(jnp.int32), column(routes[1:2], RB).astype(jnp.int32)
     w0, w1 = column(weights[0:1], RB), column(weights[1:2], RB)
     place = iota((1, out_ref.shape[1]), 1)
-    expert = place // 64
+    expert = place // 16
     chosen = jnp.where((r0 == expert) | (r1 == expert), 1.0, 0.0)
     earlier = jnp.where(iota((RB, RB), 1) < iota((RB, RB), 0), 1.0, 0.0)
     slot = jnp.dot(earlier, chosen, preferred_element_type=f32)
@@ -282,22 +299,16 @@
     swap = [(0, 1), (1, 0)]
 
     decay, narrow, w_turned = decay_rate.reshape(1, -1), moe_gain.reshape(1, -1), w_out.T
-    taken = (queries, new_keys, new_values, kv_memory, decay, attn_gain, w_turned, residual, narrow, turned_routes, route_weights.T)
-    held = (queries, new_keys, new_values, kv_memory, decay, residual, turned_routes, route_weights.T, narrow)
-    taken = tuple(far(x) for x in taken)
-    sent, w_near, gain_near, own_rows, moe_near, table = call(
+    held = (queries, new_keys, new_values, decay)
+    passed = (w_turned, residual, narrow, turned_routes, route_weights.T)
+    taken = tuple(far(x) for x in held + (attn_gain, kv_memory) + passed)
+    sent, gain_near, w_near, *rest = call(
         attention,
-        [
-            shape((groups, sessions * heads, HEAD_DIM), bf16),
-            shape(w_turned.shape, bf16),
-            shape(attn_gain.shape, f32),
-            shape((RB, LANES), bf16),
-            shape((1, LANES), f32),
-            shape((6 * RB, 1024), bf16),
-        ],
+        [shape((groups, sessions * heads, HEAD_DIM), bf16)] + [shape(x.shape, x.dtype) for x in (attn_gain,) + passed],
         [HB] * len(taken),
         taken,
-        scratch=[pltpu.VMEM(x.shape, x.dtype) for x in held] + [pltpu.SemaphoreType.DMA((10 + sessions,))],
+        scratch=[pltpu.VMEM(x.shape, x.dtype) for x in held + (kv_memory,)]
+        + [pltpu.SemaphoreType.DMA((10 + sessions,))],
         flops=10**6,
         moved=1200000,
     )
@@ -311,12 +322,20 @@
         flops=25 * 10**6,
         moved=700000,
     )
+    own_rows, moe_near, table = call(
+        prepare,
+        [shape((RB, LANES), bf16), shape((1, LANES), f32), shape((6 * RB, 256), bf16)],
+        [VM] * 5,
+        (give, *rest),
+        flops=10**6,
+        moved=200000,
+    )
     message, summed = call(
         functools.partial(gather_side, width),
         [shape((half + RB, LANES), bf16), shape((half, LANES), f32)],
         [VM] * 3,
         (mine, lax.ppermute(give, "side", swap), own_rows),
-        flops=10**6,
+        flops=3 * 10**10,
         moved=400000,
     )
     got = [lax.ppermute(message, "tp", [(t, (t + step) % 4) for t in range(4)]) for step in STEPS]
@@ -326,7 +345,7 @@
         [VM] * 6,
         (summed, own_rows, *got, moe_near),
         scratch=[pltpu.VMEM((half, LANES), f32)] * 2,
-        flops=3 * 10**10,
+        flops=10**7,
         moved=700000,
     )
     inbox = lax.all_to_all(outbox, "grp", 0, 0, tiled=True)
@@ -342,15 +361,26 @@
         moved=11000000,
         limit=12,
     )
-    back = call(
+    piece = (4 * CAP, D // 4)
+    sums, *pieces = call(
         spread,
-        shape((groups * 4, 2 * CAP, 128), bf16),
+        [shape(piece, f32)] + [shape(piece, bf16)] * 3,
         [VM, VM],
         (keep, lax.ppermute(give, "side", swap)),
+        scratch=[pltpu.VMEM((4, CAP, D), f32)],
         flops=10**6,
         moved=900000,
     )
-    returned = lax.all_to_all(back, ("grp", "tp"), 0, 0, tiled=True)
+    pieces = [lax.ppermute(x, "tp", [(t, (t + step) % 4) for t in range(4)]) for step, x in zip(BACK, pieces)]
+    back = call(
+        reduce_parts,
+        shape((groups, 2 * CAP, 128), bf16),
+        [VM] * 4,
+        (sums, *pieces),
+        flops=10**6,
+        moved=400000,
+    )
+    returned = lax.all_to_all(back, "grp", 0, 0, tiled=True)
     return call(
         combine,
         shape((RB, width), bf16),

time: 78.4 us -> 77.4 us (0.987); the launches traced: 78.2 us -> 76.2 us
  blocking collectives: 54.6 us -> 46.4 us
  waiting for transfers between devices: 6.46 us -> 10.4 us
  starting transfers between devices: 10.6 us -> 13.1 us
    all_to_all x1, blocking collectives: 19.5 us -> 11.9 us  [body(): returned = lax.all_to_all(back, 'grp', 0, 0, tiled=True)]
    ppermute x0 -> x3, waiting for transfers between devices: none -> 4.15 us  [body(): lax.ppermute(x, 'tp', [(t, (t + step) % 4) for t in range(4)])]
    ppermute x0 -> x3, starting transfers between devices: none -> 2.32 us  [body(): lax.ppermute(x, 'tp', [(t, (t + step) % 4) for t in range(4)])]
    pallas_call x8 -> x10, Pallas kernels: 6.42 us -> 6.26 us  [call(): return made(*args)]
  transfers between devices with their start and end apart: 6 -> 9, of which waited for: 5 -> 7; matrix products, arithmetic and copies ran while one was open for 0% -> 0% of each run, Pallas kernels for 0% -> 0%
where the time goes in v6:
time: 77.4 us; the launch traced here: 76.2 us
  blocking collectives  46.4 us (60%)
  starting transfers between devices  13.1 us (17%)
  waiting for transfers between devices  10.4 us (13%)
  Pallas kernels  6.26 us (8%)
    all_to_all x1, blocking collectives, body(): every = lax.all_to_all(sent, 'grp', 0, 0, tiled=True)  21 us
    all_to_all x1, blocking collectives, body(): inbox = lax.all_to_all(outbox, 'grp', 0, 0, tiled=True)  13.4 us
    all_to_all x1, blocking collectives, body(): returned = lax.all_to_all(back, 'grp', 0, 0, tiled=True)  11.9 us
    pallas_call x10, Pallas kernels, call(): return made(*args)  6.26 us
    ppermute x3, starting transfers between devices, body(): lax.ppermute(message, 'tp', [(t, (t + step) % 4) for t in range(4)])  4.51 us
    ppermute x3, waiting for transfers between devices, body(): lax.ppermute(x, 'tp', [(t, (t + step) % 4) for t in range(4)])  4.15 us
    ppermute x1, starting transfers between devices, body(): lax.ppermute(inbox, 'side', swap)  3.68 us
    ppermute x3, waiting for transfers between devices, body(): lax.ppermute(message, 'tp', [(t, (t + step) % 4) for t in range(4)])  3.37 us
  transfers between devices with their start and end apart: 9, of which 7 were waited for; matrix products, arithmetic and copies ran while one was open for 0% of the time, Pallas kernels for 0%

profile of v6, /device:TPU:1, one launch (start us, length us, event | category | flops | bytes accessed | tf_op | source)
XLA Modules:
  0.0 76.2 jit_solution(3119157679888508824)
XLA Ops:
  0.0 1.5 %shard_map.136 = (bf16[32,16,128]{2,1,0:T(8,128)(2,1)S(1)}, f32[4,128]{1,0:T(4,128)S(1)}, bf16[192,512]{1,0:T(8,128)(2,1)S(1)}, bf16[16,192]{1,0:T(8,128)(2,1)S(...) custom-call(bf16[4,4,128]{2,1,0:T(4,128)(2,1)} %q_hbm.1, bf16[4,4,128]{2,1,0:T(4,128)(2,1)} %k_hbm.1, ...), custom_call_target="tpu_custom_call" | custom-call | flops 1000000 | bytes 1200000 | tf_op jit(solution)/shard_map/pallas_call | solution.py:271
  1.5 21.0 %all_to_all.15.x_ref = bf16[32,16,128]{2,1,0:T(8,128)(2,1)S(1)} all-to-all(bf16[32,16,128]{2,1,0:T(8,128)(2,1)S(1)} %get-tuple-element.29), channel_id=1, replica_groups=mesh['side'=2,'grp'=32,'tp'=4] {'grp'}, dimensions={0} | all-to-all | bytes 262144 | tf_op jit(solution)/shard_map/all_to_all | solution.py:315
  22.5 0.2 shard_map.137
  22.8 2.1 %collective-permute-start = (f32[64,256]{1,0:T(8,128)S(1)}, f32[64,256]{1,0:T(8,128)S(1)}, u32[]{:S(2)}, u32[]{:S(2)}) collective-permute-start(f32[64,256]{1,0:T(8,128)S(1)} %get-tuple-element.33.after_ref), channel_id=1, source_target_pairs={{0,128},{128,0},{1,129},{129,1},{2,130},{130,2},{3,131},{131,3},{4... | collective-permute-start | bytes 196616 | tf_op jit(solution)/shard_map/ppermute | solution.py:337
  24.9 0.2 shard_map.138
  25.1 0.7 collective-permute-done.other_ref
  25.9 3.0 %collective-permute-start.3 = (bf16[80,256]{1,0:T(8,128)(2,1)S(1)}, bf16[80,256]{1,0:T(8,128)(2,1)S(1)}, u32[]{:S(2)}, u32[]{:S(2)}) collective-permute-start(bf16[80,256]{1,0:T(8,128)(2,1)S(1)} %get-tuple-element.40), channel_id=1, source_target_pairs={{0,2},{1,3},{2,0},{3,1},{4,6},{5,7},{6,4},{7,5},{8,10},{9,11},{10,... | collective-permute-start | bytes 122888 | tf_op jit(solution)/shard_map/ppermute | solution.py:341
  29.0 0.8 %collective-permute-start.2 = (bf16[80,256]{1,0:T(8,128)(2,1)S(1)}, bf16[80,256]{1,0:T(8,128)(2,1)S(1)}, u32[]{:S(2)}, u32[]{:S(2)}) collective-permute-start(bf16[80,256]{1,0:T(8,128)(2,1)S(1)} %get-tuple-element.40), channel_id=1, source_target_pairs={{0,3},{1,0},{2,1},{3,2},{4,7},{5,4},{6,5},{7,6},{8,11},{9,8},{10,9... | collective-permute-start | bytes 122888 | tf_op jit(solution)/shard_map/ppermute | solution.py:341
  29.7 0.7 collective-permute-start.1
  30.4 1.6 %collective-permute-done.2.b_ref = bf16[80,256]{1,0:T(8,128)(2,1)S(1)} collective-permute-done((bf16[80,256]{1,0:T(8,128)(2,1)S(1)}, bf16[80,256]{1,0:T(8,128)(2,1)S(1)}, u32[]{:S(2)}, u32[]{:S(2)}) %collective-permute-start.2) | collective-permute-done | bytes 40992 | tf_op jit(solution)/shard_map/ppermute | solution.py:341
  32.0 1.8 %collective-permute-done.1.a_ref = bf16[80,256]{1,0:T(8,128)(2,1)S(1)} collective-permute-done((bf16[80,256]{1,0:T(8,128)(2,1)S(1)}, bf16[80,256]{1,0:T(8,128)(2,1)S(1)}, u32[]{:S(2)}, u32[]{:S(2)}) %collective-permute-start.1) | collective-permute-done | bytes 40992 | tf_op jit(solution)/shard_map/ppermute | solution.py:341
  33.8 0.5 shard_map.140
  34.3 13.4 %all_to_all.16.in_ref = bf16[32,16,256]{2,1,0:T(8,128)(2,1)S(1)} all-to-all(bf16[32,16,256]{2,1,0:T(8,128)(2,1)S(1)} %get-tuple-element.42), channel_id=1, replica_groups=mesh['side'=2,'grp'=32,'tp'=4] {'grp'}, dimensions={0} | all-to-all | bytes 524288 | tf_op jit(solution)/shard_map/all_to_all | solution.py:351
  47.7 3.7 %collective-permute-start.4 = (bf16[32,16,256]{2,1,0:T(8,128)(2,1)S(1)}, bf16[32,16,256]{2,1,0:T(8,128)(2,1)S(1)}, u32[]{:S(2)}, u32[]{:S(2)}) collective-permute-start(bf16[32,16,256]{2,1,0:T(8,128)(2,1)S(1)} %all_to_all.16.in_ref), channel_id=1, source_target_pairs={{0,128},{128,0},{1,129},{129,1},{2,130},{130,2},{3,131},{131,3},{4... | collective-permute-start | bytes 786440 | tf_op jit(solution)/shard_map/ppermute | solution.py:358
  51.4 1.1 %collective-permute-done.4.other_ref = bf16[32,16,256]{2,1,0:T(8,128)(2,1)S(1)} collective-permute-done((bf16[32,16,256]{2,1,0:T(8,128)(2,1)S(1)}, bf16[32,16,256]{2,1,0:T(8,128)(2,1)S(1)}, u32[]{:S(2)}, u32[]{:S(2)}) %collective-permute-start.4) | collective-permute-done | bytes 262176 | tf_op jit(solution)/shard_map/ppermute | solution.py:358
  52.6 2.8 %shard_map.142 = (f32[16,6144]{1,0:T(8,128)S(1)}, bf16[16,6144]{1,0:T(8,128)(2,1)S(1)}) custom-call(bf16[16,6144]{1,0:T(8,128)(2,1)S(1)} %get-tuple-element.43.x_ref, f32[16,128]{1,0:T(8,128)S(1)} %get-tuple-element.44.feature_ref, bf16[32,16,256]{2,1,0:T(8,128)(2,1)S(1)} %collective-permute-done.4.other_ref, bf16[288,6144]{1,0:T(8,128)(2,1)S(1)} %bitcast.12, ...), custom_call_target="tpu_custom_call" | custom-call | flops 400000000 | bytes 11000000 | tf_op jit(solution)/shard_map/pallas_call | solution.py:271
  55.3 0.4 collective-permute-start.5
  55.8 1.1 %collective-permute-done.5.other_ref = bf16[16,6144]{1,0:T(8,128)(2,1)S(1)} collective-permute-done((bf16[16,6144]{1,0:T(8,128)(2,1)S(1)}, bf16[16,6144]{1,0:T(8,128)(2,1)S(1)}, u32[]{:S(2)}, u32[]{:S(2)}) %collective-permute-start.5) | collective-permute-done | bytes 196640 | tf_op jit(solution)/shard_map/ppermute | solution.py:369
  56.9 0.8 %collective-permute-start.6 = (bf16[16,1536]{1,0:T(8,128)(2,1)S(1)}, bf16[16,1536]{1,0:T(8,128)(2,1)S(1)}, u32[]{:S(2)}, u32[]{:S(2)}) collective-permute-start(bf16[16,1536]{1,0:T(8,128)(2,1)S(1)} %get-tuple-element.48), channel_id=1, source_target_pairs={{0,2},{1,3},{2,0},{3,1},{4,6},{5,7},{6,4},{7,5},{8,10},{9,11},{10,... | collective-permute-start | bytes 147464 | tf_op jit(solution)/shard_map/ppermute | solution.py:374
  57.7 1.5 %collective-permute-start.7 = (bf16[16,1536]{1,0:T(8,128)(2,1)S(1)}, bf16[16,1536]{1,0:T(8,128)(2,1)S(1)}, u32[]{:S(2)}, u32[]{:S(2)}) collective-permute-start(bf16[16,1536]{1,0:T(8,128)(2,1)S(1)} %get-tuple-element.49), channel_id=1, source_target_pairs={{0,3},{1,0},{2,1},{3,2},{4,7},{5,4},{6,5},{7,6},{8,11},{9,8},{10,9... | collective-permute-start | bytes 147464 | tf_op jit(solution)/shard_map/ppermute | solution.py:374
  59.2 2.2 %collective-permute-done.6.a_ref = bf16[16,1536]{1,0:T(8,128)(2,1)S(1)} collective-permute-done((bf16[16,1536]{1,0:T(8,128)(2,1)S(1)}, bf16[16,1536]{1,0:T(8,128)(2,1)S(1)}, u32[]{:S(2)}, u32[]{:S(2)}) %collective-permute-start.6) | collective-permute-done | bytes 49184 | tf_op jit(solution)/shard_map/ppermute | solution.py:374
  61.5 1.9 %collective-permute-done.8.c_ref = bf16[16,1536]{1,0:T(8,128)(2,1)S(1)} collective-permute-done((bf16[16,1536]{1,0:T(8,128)(2,1)S(1)}, bf16[16,1536]{1,0:T(8,128)(2,1)S(1)}, u32[]{:S(2)}, u32[]{:S(2)}) %collective-permute-start.8) | collective-permute-done | bytes 49184 | tf_op jit(solution)/shard_map/ppermute | solution.py:374
  63.4 11.9 %all_to_all.17.x_ref = bf16[32,8,128]{2,1,0:T(8,128)(2,1)S(1)} all-to-all(bf16[32,8,128]{2,1,0:T(8,128)(2,1)S(1)} %shard_map.144), channel_id=1, replica_groups=mesh['side'=2,'grp'=32,'tp'=4] {'grp'}, dimensions={0} | all-to-all | bytes 131072 | tf_op jit(solution)/shard_map/all_to_all | solution.py:383
  75.3 0.8 %shard_map.145 = bf16[16,192]{1,0:T(8,128)(2,1)} custom-call(bf16[32,8,128]{2,1,0:T(8,128)(2,1)S(1)} %all_to_all.17.x_ref, bf16[96,256]{1,0:T(8,128)(2,1)S(1)} %get-tuple-element.51.table_ref, f32[16,256]{1,0:T(8,128)S(1)} %get-tuple-element.52.own_ref), custom_call_target="tpu_custom_call" | custom-call | flops 30000000 | bytes 500000 | tf_op jit(solution)/shard_map/pallas_call | solution.py:271
  (13 shorter events, 0.3 us)
Async XLA Ops:
  22.8 3.0 %collective-permute-start = (f32[64,256]{1,0:T(8,128)S(1)}, f32[64,256]{1,0:T(8,128)S(1)}, u32[]{:S(2)}, u32[]{:S(2)}) collective-permute-start(f32[64,256]{1,0:T(8,128)S(1)} %get-tuple-element.33.after_ref), channel_id=1, source_target_pairs={{0,128},{128,0},{1,129},{129,1},{2,130},{130,2},{3,131},{131,3},{4... | collective-permute-start | bytes 196616 | tf_op jit(solution)/shard_map/ppermute | solution.py:337
  25.8 26.7 %copy-start = (bf16[1,6144,288]{1,2,0:T(8,128)(2,1)S(1)}, bf16[1,6144,288]{1,2,0:T(8,128)(2,1)}, u32[]{:S(2)}) copy-start(bf16[1,6144,288]{1,2,0:T(8,128)(2,1)} %param.23) | copy-start | bytes 10616836
  25.8 26.7 %copy-start.1 = (bf16[1,6144,288]{1,2,0:T(8,128)(2,1)S(1)}, bf16[1,6144,288]{1,2,0:T(8,128)(2,1)}, u32[]{:S(2)}) copy-start(bf16[1,6144,288]{1,2,0:T(8,128)(2,1)} %param.24) | copy-start | bytes 10616836
  25.8 26.7 %copy-start.2 = (bf16[1,288,6144]{2,1,0:T(8,128)(2,1)S(1)}, bf16[1,288,6144]{2,1,0:T(8,128)(2,1)}, u32[]{:S(2)}) copy-start(bf16[1,288,6144]{2,1,0:T(8,128)(2,1)} %param.25) | copy-start | bytes 10616836
  25.9 4.5 %collective-permute-start.3 = (bf16[80,256]{1,0:T(8,128)(2,1)S(1)}, bf16[80,256]{1,0:T(8,128)(2,1)S(1)}, u32[]{:S(2)}, u32[]{:S(2)}) collective-permute-start(bf16[80,256]{1,0:T(8,128)(2,1)S(1)} %get-tuple-element.40), channel_id=1, source_target_pairs={{0,2},{1,3},{2,0},{3,1},{4,6},{5,7},{6,4},{7,5},{8,10},{9,11},{10,... | collective-permute-start | bytes 122888 | tf_op jit(solution)/shard_map/ppermute | solution.py:341
  29.0 3.0 %collective-permute-start.2 = (bf16[80,256]{1,0:T(8,128)(2,1)S(1)}, bf16[80,256]{1,0:T(8,128)(2,1)S(1)}, u32[]{:S(2)}, u32[]{:S(2)}) collective-permute-start(bf16[80,256]{1,0:T(8,128)(2,1)S(1)} %get-tuple-element.40), channel_id=1, source_target_pairs={{0,3},{1,0},{2,1},{3,2},{4,7},{5,4},{6,5},{7,6},{8,11},{9,8},{10,9... | collective-permute-start | bytes 122888 | tf_op jit(solution)/shard_map/ppermute | solution.py:341
  29.7 4.1 %collective-permute-start.1 = (bf16[80,256]{1,0:T(8,128)(2,1)S(1)}, bf16[80,256]{1,0:T(8,128)(2,1)S(1)}, u32[]{:S(2)}, u32[]{:S(2)}) collective-permute-start(bf16[80,256]{1,0:T(8,128)(2,1)S(1)} %get-tuple-element.40), channel_id=1, source_target_pairs={{0,1},{1,2},{2,3},{3,0},{4,5},{5,6},{6,7},{7,4},{8,9},{9,10},{10,1... | collective-permute-start | bytes 122888 | tf_op jit(solution)/shard_map/ppermute | solution.py:341
  47.7 4.8 %collective-permute-start.4 = (bf16[32,16,256]{2,1,0:T(8,128)(2,1)S(1)}, bf16[32,16,256]{2,1,0:T(8,128)(2,1)S(1)}, u32[]{:S(2)}, u32[]{:S(2)}) collective-permute-start(bf16[32,16,256]{2,1,0:T(8,128)(2,1)S(1)} %all_to_all.16.in_ref), channel_id=1, source_target_pairs={{0,128},{128,0},{1,129},{129,1},{2,130},{130,2},{3,131},{131,3},{4... | collective-permute-start | bytes 786440 | tf_op jit(solution)/shard_map/ppermute | solution.py:358
  55.3 1.5 %collective-permute-start.5 = (bf16[16,6144]{1,0:T(8,128)(2,1)S(1)}, bf16[16,6144]{1,0:T(8,128)(2,1)S(1)}, u32[]{:S(2)}, u32[]{:S(2)}) collective-permute-start(bf16[16,6144]{1,0:T(8,128)(2,1)S(1)} %get-tuple-element.46), channel_id=1, source_target_pairs={{0,128},{128,0},{1,129},{129,1},{2,130},{130,2},{3,131},{131,3},{4... | collective-permute-start | bytes 589832 | tf_op jit(solution)/shard_map/ppermute | solution.py:369
  56.9 4.5 %collective-permute-start.6 = (bf16[16,1536]{1,0:T(8,128)(2,1)S(1)}, bf16[16,1536]{1,0:T(8,128)(2,1)S(1)}, u32[]{:S(2)}, u32[]{:S(2)}) collective-permute-start(bf16[16,1536]{1,0:T(8,128)(2,1)S(1)} %get-tuple-element.48), channel_id=1, source_target_pairs={{0,2},{1,3},{2,0},{3,1},{4,6},{5,7},{6,4},{7,5},{8,10},{9,11},{10,... | collective-permute-start | bytes 147464 | tf_op jit(solution)/shard_map/ppermute | solution.py:374
  57.7 3.7 %collective-permute-start.7 = (bf16[16,1536]{1,0:T(8,128)(2,1)S(1)}, bf16[16,1536]{1,0:T(8,128)(2,1)S(1)}, u32[]{:S(2)}, u32[]{:S(2)}) collective-permute-start(bf16[16,1536]{1,0:T(8,128)(2,1)S(1)} %get-tuple-element.49), channel_id=1, source_target_pairs={{0,3},{1,0},{2,1},{3,2},{4,7},{5,4},{6,5},{7,6},{8,11},{9,8},{10,9... | collective-permute-start | bytes 147464 | tf_op jit(solution)/shard_map/ppermute | solution.py:374
  59.2 4.2 %collective-permute-start.8 = (bf16[16,1536]{1,0:T(8,128)(2,1)S(1)}, bf16[16,1536]{1,0:T(8,128)(2,1)S(1)}, u32[]{:S(2)}, u32[]{:S(2)}) collective-permute-start(bf16[16,1536]{1,0:T(8,128)(2,1)S(1)} %get-tuple-element.50), channel_id=1, source_target_pairs={{0,1},{1,2},{2,3},{3,0},{4,5},{5,6},{6,7},{7,4},{8,9},{9,10},{10,1... | collective-permute-start | bytes 147464 | tf_op jit(solution)/shard_map/ppermute | solution.py:374

commit v7 on v6

--- a/solution.py
+++ b/solution.py
@@ -17,7 +17,6 @@
 WIDE = 8
 
 STEPS = (1, 3, 2)
-BACK = (2, 3, 1)
 
 epsilon = 1e-06
 f32, bf16 = jnp.float32, jnp.bfloat16
@@ -95,7 +94,7 @@
     total = x_ref.shape[0] * x_ref.shape[1]
     sessions = total // heads
     half = sessions // 2
-    spread_ref[...] = x_ref[...].reshape(total, HEAD_DIM).astype(f32)
+    spread_ref[:total] = x_ref[...].reshape(total, HEAD_DIM).astype(f32)
     lane = iota((1, LANES), 1)
     squares = jnp.zeros((sessions, 1), f32)
     parts = []
@@ -197,37 +196,23 @@
         give_ref[:, part] = chunk[rows:].astype(bf16)
 
 
-def spread(keep_ref, other_ref, mine_ref, a_ref, b_ref, c_ref, total_ref):
-    tp = lax.axis_index("tp")
-    for n in range(WIDE):
-        part = slice(n * D // WIDE, (n + 1) * D // WIDE)
-        total = keep_ref[:, part] + other_ref[:, part].astype(f32)
+def spread(keep_ref, other_ref, out_ref):
+    for i in range(D // 384):
+        a, b, c = (
+            keep_ref[:, 128 * n : 128 * n + 128] + other_ref[:, 128 * n : 128 * n + 128].astype(f32)
+            for n in range(3 * i, 3 * i + 3)
+        )
         for t in range(4):
-            total_ref[t, :, part] = total[t * CAP : (t + 1) * CAP]
-    span = mine_ref.shape[1]
-    for step, ref in zip((0,) + BACK, (mine_ref, a_ref, b_ref, c_ref)):
-        rows = total_ref[lax.rem(tp + step, 4)]
-        piece = jnp.concatenate([rows[:, q * span : (q + 1) * span] for q in range(4)], axis=0)
-        ref[...] = piece.astype(ref.dtype)
-
-
-def reduce_parts(mine_ref, a_ref, b_ref, c_ref, out_ref):
-    total = mine_ref[...]
-    for ref in (a_ref, b_ref, c_ref):
-        total = total + ref[...].astype(f32)
-    for q in range(4):
-        rows = total[q * CAP : (q + 1) * CAP]
-        for i in range(4):
-            a, b, c = (rows[:, 384 * i + 128 * n : 384 * i + 128 * (n + 1)] for n in range(3))
-            out_ref[q * 8 + 2 * i] = jnp.concatenate([a, b], axis=0).astype(out_ref.dtype)
-            out_ref[q * 8 + 2 * i + 1] = jnp.concatenate([b, c], axis=0).astype(out_ref.dtype)
+            rows = slice(t * CAP, (t + 1) * CAP)
+            out_ref[(2 * i) * 4 + t] = jnp.concatenate([a[rows], b[rows]], axis=0).astype(bf16)
+            out_ref[(2 * i + 1) * 4 + t] = jnp.concatenate([b[rows], c[rows]], axis=0).astype(bf16)
 
 
 def combiner(routes, weights, out_ref):
     r0, r1 = column(routes[0:1], RB).astype(jnp.int32), column(routes[1:2], RB).astype(jnp.int32)
     w0, w1 = column(weights[0:1], RB), column(weights[1:2], RB)
     place = iota((1, out_ref.shape[1]), 1)
-    expert = place // 16
+    expert = place // 64
     chosen = jnp.where((r0 == expert) | (r1 == expert), 1.0, 0.0)
     earlier = jnp.where(iota((RB, RB), 1) < iota((RB, RB), 0), 1.0, 0.0)
     slot = jnp.dot(earlier, chosen, preferred_element_type=f32)
@@ -318,13 +303,13 @@
         [shape((half, LANES), f32)] * 2,
         [VM] * 3,
         (every, w_near, gain_near),
-        scratch=[pltpu.VMEM((groups * sessions * heads, HEAD_DIM), f32)],
+        scratch=[pltpu.VMEM((groups * sessions * heads + 8, HEAD_DIM), f32)],
         flops=25 * 10**6,
         moved=700000,
     )
     own_rows, moe_near, table = call(
         prepare,
-        [shape((RB, LANES), bf16), shape((1, LANES), f32), shape((6 * RB, 256), bf16)],
+        [shape((RB, LANES), bf16), shape((1, LANES), f32), shape((6 * RB, 1024), bf16)],
         [VM] * 5,
         (give, *rest),
         flops=10**6,
@@ -361,26 +346,15 @@
         moved=11000000,
         limit=12,
     )
-    piece = (4 * CAP, D // 4)
-    sums, *pieces = call(
+    back = call(
         spread,
-        [shape(piece, f32)] + [shape(piece, bf16)] * 3,
+        shape((groups * 4, 2 * CAP, 128), bf16),
         [VM, VM],
         (keep, lax.ppermute(give, "side", swap)),
-        scratch=[pltpu.VMEM((4, CAP, D), f32)],
         flops=10**6,
         moved=900000,
     )
-    pieces = [lax.ppermute(x, "tp", [(t, (t + step) % 4) for t in range(4)]) for step, x in zip(BACK, pieces)]
-    back = call(
-        reduce_parts,
-        shape((groups, 2 * CAP, 128), bf16),
-        [VM] * 4,
-        (sums, *pieces),
-        flops=10**6,
-        moved=400000,
-    )
-    returned = lax.all_to_all(back, "grp", 0, 0, tiled=True)
+    returned = lax.all_to_all(back, ("grp", "tp"), 0, 0, tiled=True)
     return call(
         combine,
         shape((RB, width), bf16),

time: 77.4 us -> 77.4 us (level); the launches traced: 76.2 us -> 77.2 us
  blocking collectives: 46.4 us -> 53.8 us
  waiting for transfers between devices: 10.4 us -> 6.21 us
  starting transfers between devices: 13.1 us -> 10.8 us
    all_to_all x1, blocking collectives: 11.9 us -> 19.4 us  [body(): returned = lax.all_to_all(back, ('grp', 'tp'), 0, 0, tiled=True)]
    ppermute x3 -> x0, waiting for transfers between devices: 4.15 us -> none  [body(): lax.ppermute(x, 'tp', [(t, (t + step) % 4) for t in range(4)])]
    ppermute x3 -> x0, starting transfers between devices: 2.32 us -> none  [body(): lax.ppermute(x, 'tp', [(t, (t + step) % 4) for t in range(4)])]
    pallas_call x10 -> x9, Pallas kernels: 6.26 us -> 6.31 us  [call(): return made(*args)]
  transfers between devices with their start and end apart: 9 -> 6, of which waited for: 7 -> 5; matrix products, arithmetic and copies ran while one was open for 0% -> 0% of each run, Pallas kernels for 0% -> 0%
where the time goes in v7:
time: 77.4 us; the launch traced here: 77.2 us
  blocking collectives  53.8 us (70%)
  starting transfers between devices  10.8 us (14%)
  Pallas kernels  6.31 us (8%)
  waiting for transfers between devices  6.21 us (8%)
    all_to_all x1, blocking collectives, body(): every = lax.all_to_all(sent, 'grp', 0, 0, tiled=True)  21 us
    all_to_all x1, blocking collectives, body(): returned = lax.all_to_all(back, ('grp', 'tp'), 0, 0, tiled=True)  19.4 us
    all_to_all x1, blocking collectives, body(): inbox = lax.all_to_all(outbox, 'grp', 0, 0, tiled=True)  13.4 us
    pallas_call x9, Pallas kernels, call(): return made(*args)  6.31 us
    ppermute x3, starting transfers between devices, body(): lax.ppermute(message, 'tp', [(t, (t + step) % 4) for t in range(4)])  4.51 us
    ppermute x1, starting transfers between devices, body(): lax.ppermute(inbox, 'side', swap)  3.68 us
    ppermute x3, waiting for transfers between devices, body(): lax.ppermute(message, 'tp', [(t, (t + step) % 4) for t in range(4)])  3.37 us
    ppermute x2, starting transfers between devices, body(): lax.ppermute(give, 'side', swap)  2.58 us
  transfers between devices with their start and end apart: 6, of which 5 were waited for; matrix products, arithmetic and copies ran while one was open for 0% of the time, Pallas kernels for 0%

profile of v7, /device:TPU:1, one launch (start us, length us, event | category | flops | bytes accessed | tf_op | source)
XLA Modules:
  0.0 77.2 jit_solution(5590107924426048088)
XLA Ops:
  0.0 1.5 %shard_map.136 = (bf16[32,16,128]{2,1,0:T(8,128)(2,1)S(1)}, f32[4,128]{1,0:T(4,128)S(1)}, bf16[192,512]{1,0:T(8,128)(2,1)S(1)}, bf16[16,192]{1,0:T(8,128)(2,1)S(...) custom-call(bf16[4,4,128]{2,1,0:T(4,128)(2,1)} %q_hbm.1, bf16[4,4,128]{2,1,0:T(4,128)(2,1)} %k_hbm.1, ...), custom_call_target="tpu_custom_call" | custom-call | flops 1000000 | bytes 1200000 | tf_op jit(solution)/shard_map/pallas_call | solution.py:256
  1.5 21.0 %all_to_all.15.x_ref = bf16[32,16,128]{2,1,0:T(8,128)(2,1)S(1)} all-to-all(bf16[32,16,128]{2,1,0:T(8,128)(2,1)S(1)} %get-tuple-element.25), channel_id=1, replica_groups=mesh['side'=2,'grp'=32,'tp'=4] {'grp'}, dimensions={0} | all-to-all | bytes 262144 | tf_op jit(solution)/shard_map/all_to_all | solution.py:300
  22.5 0.2 shard_map.137
  22.8 2.1 %collective-permute-start = (f32[64,256]{1,0:T(8,128)S(1)}, f32[64,256]{1,0:T(8,128)S(1)}, u32[]{:S(2)}, u32[]{:S(2)}) collective-permute-start(f32[64,256]{1,0:T(8,128)S(1)} %get-tuple-element.29.after_ref), channel_id=1, source_target_pairs={{0,128},{128,0},{1,129},{129,1},{2,130},{130,2},{3,131},{131,3},{4... | collective-permute-start | bytes 196616 | tf_op jit(solution)/shard_map/ppermute | solution.py:322
  24.9 0.2 shard_map.138
  25.2 0.7 collective-permute-done.other_ref
  25.8 0.1 shard_map.139
  25.9 3.0 %collective-permute-start.3 = (bf16[80,256]{1,0:T(8,128)(2,1)S(1)}, bf16[80,256]{1,0:T(8,128)(2,1)S(1)}, u32[]{:S(2)}, u32[]{:S(2)}) collective-permute-start(bf16[80,256]{1,0:T(8,128)(2,1)S(1)} %get-tuple-element.36), channel_id=1, source_target_pairs={{0,2},{1,3},{2,0},{3,1},{4,6},{5,7},{6,4},{7,5},{8,10},{9,11},{10,... | collective-permute-start | bytes 122888 | tf_op jit(solution)/shard_map/ppermute | solution.py:326
  29.0 0.8 %collective-permute-start.2 = (bf16[80,256]{1,0:T(8,128)(2,1)S(1)}, bf16[80,256]{1,0:T(8,128)(2,1)S(1)}, u32[]{:S(2)}, u32[]{:S(2)}) collective-permute-start(bf16[80,256]{1,0:T(8,128)(2,1)S(1)} %get-tuple-element.36), channel_id=1, source_target_pairs={{0,3},{1,0},{2,1},{3,2},{4,7},{5,4},{6,5},{7,6},{8,11},{9,8},{10,9... | collective-permute-start | bytes 122888 | tf_op jit(solution)/shard_map/ppermute | solution.py:326
  29.7 0.7 collective-permute-start.1
  30.4 0.0 collective-permute-done.3.c_ref
  30.4 1.6 %collective-permute-done.2.b_ref = bf16[80,256]{1,0:T(8,128)(2,1)S(1)} collective-permute-done((bf16[80,256]{1,0:T(8,128)(2,1)S(1)}, bf16[80,256]{1,0:T(8,128)(2,1)S(1)}, u32[]{:S(2)}, u32[]{:S(2)}) %collective-permute-start.2) | collective-permute-done | bytes 40992 | tf_op jit(solution)/shard_map/ppermute | solution.py:326
  32.0 1.8 %collective-permute-done.1.a_ref = bf16[80,256]{1,0:T(8,128)(2,1)S(1)} collective-permute-done((bf16[80,256]{1,0:T(8,128)(2,1)S(1)}, bf16[80,256]{1,0:T(8,128)(2,1)S(1)}, u32[]{:S(2)}, u32[]{:S(2)}) %collective-permute-start.1) | collective-permute-done | bytes 40992 | tf_op jit(solution)/shard_map/ppermute | solution.py:326
  33.8 0.5 shard_map.140
  34.3 13.4 %all_to_all.16.in_ref = bf16[32,16,256]{2,1,0:T(8,128)(2,1)S(1)} all-to-all(bf16[32,16,256]{2,1,0:T(8,128)(2,1)S(1)} %get-tuple-element.38), channel_id=1, replica_groups=mesh['side'=2,'grp'=32,'tp'=4] {'grp'}, dimensions={0} | all-to-all | bytes 524288 | tf_op jit(solution)/shard_map/all_to_all | solution.py:336
  47.7 3.7 %collective-permute-start.4 = (bf16[32,16,256]{2,1,0:T(8,128)(2,1)S(1)}, bf16[32,16,256]{2,1,0:T(8,128)(2,1)S(1)}, u32[]{:S(2)}, u32[]{:S(2)}) collective-permute-start(bf16[32,16,256]{2,1,0:T(8,128)(2,1)S(1)} %all_to_all.16.in_ref), channel_id=1, source_target_pairs={{0,128},{128,0},{1,129},{129,1},{2,130},{130,2},{3,131},{131,3},{4... | collective-permute-start | bytes 786440 | tf_op jit(solution)/shard_map/ppermute | solution.py:343
  51.4 1.1 %collective-permute-done.4.other_ref = bf16[32,16,256]{2,1,0:T(8,128)(2,1)S(1)} collective-permute-done((bf16[32,16,256]{2,1,0:T(8,128)(2,1)S(1)}, bf16[32,16,256]{2,1,0:T(8,128)(2,1)S(1)}, u32[]{:S(2)}, u32[]{:S(2)}) %collective-permute-start.4) | collective-permute-done | bytes 262176 | tf_op jit(solution)/shard_map/ppermute | solution.py:343
  52.6 0.0 copy-done
  52.6 2.8 %shard_map.142 = (f32[16,6144]{1,0:T(8,128)S(1)}, bf16[16,6144]{1,0:T(8,128)(2,1)S(1)}) custom-call(bf16[16,6144]{1,0:T(8,128)(2,1)S(1)} %get-tuple-element.39.x_ref, f32[16,128]{1,0:T(8,128)S(1)} %get-tuple-element.40.feature_ref, bf16[32,16,256]{2,1,0:T(8,128)(2,1)S(1)} %collective-permute-done.4.other_ref, bf16[288,6144]{1,0:T(8,128)(2,1)S(1)} %bitcast.12, ...), custom_call_target="tpu_custom_call" | custom-call | flops 400000000 | bytes 11000000 | tf_op jit(solution)/shard_map/pallas_call | solution.py:256
  55.3 0.4 collective-permute-start.5
  55.8 1.1 %collective-permute-done.5.other_ref = bf16[16,6144]{1,0:T(8,128)(2,1)S(1)} collective-permute-done((bf16[16,6144]{1,0:T(8,128)(2,1)S(1)}, bf16[16,6144]{1,0:T(8,128)(2,1)S(1)}, u32[]{:S(2)}, u32[]{:S(2)}) %collective-permute-start.5) | collective-permute-done | bytes 196640 | tf_op jit(solution)/shard_map/ppermute | solution.py:353
  56.8 0.1 shard_map.143
  56.9 19.4 %all_to_all.17.x_ref = bf16[128,8,128]{2,1,0:T(8,128)(2,1)S(1)} all-to-all(bf16[128,8,128]{2,1,0:T(8,128)(2,1)S(1)} %shard_map.143), channel_id=1, replica_groups=mesh['side'=2,'grp'=32,'tp'=4] {'grp','tp'}, dimensions={0} | all-to-all | bytes 524288 | tf_op jit(solution)/shard_map/all_to_all | solution.py:357
  76.3 0.9 %shard_map.144 = bf16[16,192]{1,0:T(8,128)(2,1)} custom-call(bf16[128,8,128]{2,1,0:T(8,128)(2,1)S(1)} %all_to_all.17.x_ref, bf16[96,1024]{1,0:T(8,128)(2,1)S(1)} %get-tuple-element.43.table_ref, f32[16,256]{1,0:T(8,128)S(1)} %get-tuple-element.44.own_ref), custom_call_target="tpu_custom_call" | custom-call | flops 30000000 | bytes 500000 | tf_op jit(solution)/shard_map/pallas_call | solution.py:256
  (6 shorter events, 0.1 us)
Async XLA Ops:
  22.8 3.0 %collective-permute-start = (f32[64,256]{1,0:T(8,128)S(1)}, f32[64,256]{1,0:T(8,128)S(1)}, u32[]{:S(2)}, u32[]{:S(2)}) collective-permute-start(f32[64,256]{1,0:T(8,128)S(1)} %get-tuple-element.29.after_ref), channel_id=1, source_target_pairs={{0,128},{128,0},{1,129},{129,1},{2,130},{130,2},{3,131},{131,3},{4... | collective-permute-start | bytes 196616 | tf_op jit(solution)/shard_map/ppermute | solution.py:322
  25.8 26.7 %copy-start = (bf16[1,6144,288]{1,2,0:T(8,128)(2,1)S(1)}, bf16[1,6144,288]{1,2,0:T(8,128)(2,1)}, u32[]{:S(2)}) copy-start(bf16[1,6144,288]{1,2,0:T(8,128)(2,1)} %param.23) | copy-start | bytes 10616836
  25.8 26.7 %copy-start.1 = (bf16[1,6144,288]{1,2,0:T(8,128)(2,1)S(1)}, bf16[1,6144,288]{1,2,0:T(8,128)(2,1)}, u32[]{:S(2)}) copy-start(bf16[1,6144,288]{1,2,0:T(8,128)(2,1)} %param.24) | copy-start | bytes 10616836
  25.8 26.7 %copy-start.2 = (bf16[1,288,6144]{2,1,0:T(8,128)(2,1)S(1)}, bf16[1,288,6144]{2,1,0:T(8,128)(2,1)}, u32[]{:S(2)}) copy-start(bf16[1,288,6144]{2,1,0:T(8,128)(2,1)} %param.25) | copy-start | bytes 10616836
  25.9 4.5 %collective-permute-start.3 = (bf16[80,256]{1,0:T(8,128)(2,1)S(1)}, bf16[80,256]{1,0:T(8,128)(2,1)S(1)}, u32[]{:S(2)}, u32[]{:S(2)}) collective-permute-start(bf16[80,256]{1,0:T(8,128)(2,1)S(1)} %get-tuple-element.36), channel_id=1, source_target_pairs={{0,2},{1,3},{2,0},{3,1},{4,6},{5,7},{6,4},{7,5},{8,10},{9,11},{10,... | collective-permute-start | bytes 122888 | tf_op jit(solution)/shard_map/ppermute | solution.py:326
  29.0 3.0 %collective-permute-start.2 = (bf16[80,256]{1,0:T(8,128)(2,1)S(1)}, bf16[80,256]{1,0:T(8,128)(2,1)S(1)}, u32[]{:S(2)}, u32[]{:S(2)}) collective-permute-start(bf16[80,256]{1,0:T(8,128)(2,1)S(1)} %get-tuple-element.36), channel_id=1, source_target_pairs={{0,3},{1,0},{2,1},{3,2},{4,7},{5,4},{6,5},{7,6},{8,11},{9,8},{10,9... | collective-permute-start | bytes 122888 | tf_op jit(solution)/shard_map/ppermute | solution.py:326
  29.7 4.1 %collective-permute-start.1 = (bf16[80,256]{1,0:T(8,128)(2,1)S(1)}, bf16[80,256]{1,0:T(8,128)(2,1)S(1)}, u32[]{:S(2)}, u32[]{:S(2)}) collective-permute-start(bf16[80,256]{1,0:T(8,128)(2,1)S(1)} %get-tuple-element.36), channel_id=1, source_target_pairs={{0,1},{1,2},{2,3},{3,0},{4,5},{5,6},{6,7},{7,4},{8,9},{9,10},{10,1... | collective-permute-start | bytes 122888 | tf_op jit(solution)/shard_map/ppermute | solution.py:326
  47.7 4.8 %collective-permute-start.4 = (bf16[32,16,256]{2,1,0:T(8,128)(2,1)S(1)}, bf16[32,16,256]{2,1,0:T(8,128)(2,1)S(1)}, u32[]{:S(2)}, u32[]{:S(2)}) collective-permute-start(bf16[32,16,256]{2,1,0:T(8,128)(2,1)S(1)} %all_to_all.16.in_ref), channel_id=1, source_target_pairs={{0,128},{128,0},{1,129},{129,1},{2,130},{130,2},{3,131},{131,3},{4... | collective-permute-start | bytes 786440 | tf_op jit(solution)/shard_map/ppermute | solution.py:343
  55.3 1.5 %collective-permute-start.5 = (bf16[16,6144]{1,0:T(8,128)(2,1)S(1)}, bf16[16,6144]{1,0:T(8,128)(2,1)S(1)}, u32[]{:S(2)}, u32[]{:S(2)}) collective-permute-start(bf16[16,6144]{1,0:T(8,128)(2,1)S(1)} %get-tuple-element.42), channel_id=1, source_target_pairs={{0,128},{128,0},{1,129},{129,1},{2,130},{130,2},{3,131},{131,3},{4... | collective-permute-start | bytes 589832 | tf_op jit(solution)/shard_map/ppermute | solution.py:353

commit v8 on v7

--- a/solution.py
+++ b/solution.py
@@ -13,7 +13,7 @@
 CAP = 4
 RB = 16
 LANES = 256
-DEEP = 6
+DEEP = 1
 WIDE = 8
 
 STEPS = (1, 3, 2)
@@ -161,7 +161,7 @@
         out_ref[2 * e + 1] = piece
 
 
-def stage(in_ref, x_ref, feature_ref):
+def stage(in_ref, x_ref):
     groups, rows, _ = in_ref.shape
     low_lane = iota((rows, 128), 1) < 64
     feature = jnp.zeros((rows, 128), f32)
@@ -172,13 +172,14 @@
         x_ref[:, 384 * i : 384 * i + 128] = in_ref[2 * i, :, :128]
         x_ref[:, 384 * i + 128 : 384 * i + 256] = jnp.where(low_lane, b_even, b_odd).astype(bf16)
         x_ref[:, 384 * i + 256 : 384 * i + 384] = in_ref[2 * i + 1, :, 128:]
-    feature_ref[...] = feature
-
-
-def experts(x_ref, feature_ref, other_ref, gate_ref, up_ref, down_ref, keep_ref, give_ref, x2_ref, feature2_ref):
+    high, low = halves(jnp.sum(feature, axis=1, keepdims=True))
+    lane = iota((1, 128), 1)
+    x_ref[:, D:] = jnp.where(lane == 0, high, jnp.where(lane == 1, low, 0.0)).astype(bf16)
+
+
+def experts(x_ref, x2_ref, gate_ref, up_ref, down_ref, keep_ref, give_ref):
     rows = x_ref.shape[0]
-    stage(other_ref, x2_ref, feature2_ref)
-    feature = jnp.concatenate([feature_ref[...], feature2_ref[...]], axis=0)
+    feature = jnp.concatenate([x_ref[:, D:], x2_ref[:, D:]], axis=0).astype(f32)
     scale = lax.rsqrt(jnp.sum(jnp.transpose(feature), axis=0, keepdims=True) / D + epsilon)
     gate = jnp.zeros((gate_ref.shape[0], 2 * rows), f32)
     up = gate
@@ -334,14 +335,12 @@
         moved=700000,
     )
     inbox = lax.all_to_all(outbox, "grp", 0, 0, tiled=True)
-    staged = [shape((4 * CAP, D), bf16), shape((4 * CAP, 128), f32)]
-    x_mine, feature = call(stage, staged, [VM], (inbox,), flops=10**6, moved=500000)
+    x_mine = call(stage, shape((4 * CAP, D + 128), bf16), [VM], (inbox,), flops=10**6, moved=500000)
     keep, give = call(
         experts,
         [shape((4 * CAP, D), f32), shape((4 * CAP, D), bf16)],
-        [VM] * 6,
-        (x_mine, feature, lax.ppermute(inbox, "side", swap), w_gate[0].T, w_up[0].T, w_down[0]),
-        scratch=[pltpu.VMEM(x.shape, x.dtype) for x in staged],
+        [VM] * 5,
+        (x_mine, lax.ppermute(x_mine, "side", swap), w_gate[0].T, w_up[0].T, w_down[0]),
         flops=4 * 10**8,
         moved=11000000,
         limit=12,

time: 77.4 us -> 77.4 us (level)
  no operation moved by 1% of the time
where the time goes in v8:
time: 77.4 us; the launch traced here: 77.2 us
  blocking collectives  53.8 us (70%)
  starting transfers between devices  10.8 us (14%)
  Pallas kernels  6.35 us (8%)
  waiting for transfers between devices  6.17 us (8%)
    all_to_all x1, blocking collectives, body(): every = lax.all_to_all(sent, 'grp', 0, 0, tiled=True)  21 us
    all_to_all x1, blocking collectives, body(): returned = lax.all_to_all(back, ('grp', 'tp'), 0, 0, tiled=True)  19.4 us
    all_to_all x1, blocking collectives, body(): inbox = lax.all_to_all(outbox, 'grp', 0, 0, tiled=True)  13.4 us
    pallas_call x9, Pallas kernels, call(): return made(*args)  6.35 us
    ppermute x3, starting transfers between devices, body(): lax.ppermute(message, 'tp', [(t, (t + step) % 4) for t in range(4)])  4.51 us
    ppermute x1, starting transfers between devices, body(): lax.ppermute(x_mine, 'side', swap)  3.72 us
    ppermute x3, waiting for transfers between devices, body(): lax.ppermute(message, 'tp', [(t, (t + step) % 4) for t in range(4)])  3.37 us
    ppermute x2, starting transfers between devices, body(): lax.ppermute(give, 'side', swap)  2.58 us
  transfers between devices with their start and end apart: 6, of which 5 were waited for; matrix products, arithmetic and copies ran while one was open for 0% of the time, Pallas kernels for 0%

profile of v8, /device:TPU:1, one launch (start us, length us, event | category | flops | bytes accessed | tf_op | source)
XLA Modules:
  0.0 77.2 jit_solution(1374491582476895140)
XLA Ops:
  0.0 1.5 %shard_map.136 = (bf16[32,16,128]{2,1,0:T(8,128)(2,1)S(1)}, f32[4,128]{1,0:T(4,128)S(1)}, bf16[192,512]{1,0:T(8,128)(2,1)S(1)}, bf16[16,192]{1,0:T(8,128)(2,1)S(...) custom-call(bf16[4,4,128]{2,1,0:T(4,128)(2,1)} %q_hbm.1, bf16[4,4,128]{2,1,0:T(4,128)(2,1)} %k_hbm.1, ...), custom_call_target="tpu_custom_call" | custom-call | flops 1000000 | bytes 1200000 | tf_op jit(solution)/shard_map/pallas_call | solution.py:257
  1.5 21.0 %all_to_all.15.x_ref = bf16[32,16,128]{2,1,0:T(8,128)(2,1)S(1)} all-to-all(bf16[32,16,128]{2,1,0:T(8,128)(2,1)S(1)} %get-tuple-element.23), channel_id=1, replica_groups=mesh['side'=2,'grp'=32,'tp'=4] {'grp'}, dimensions={0} | all-to-all | bytes 262144 | tf_op jit(solution)/shard_map/all_to_all | solution.py:301
  22.5 0.2 shard_map.137
  22.8 2.1 %collective-permute-start = (f32[64,256]{1,0:T(8,128)S(1)}, f32[64,256]{1,0:T(8,128)S(1)}, u32[]{:S(2)}, u32[]{:S(2)}) collective-permute-start(f32[64,256]{1,0:T(8,128)S(1)} %get-tuple-element.27.after_ref), channel_id=1, source_target_pairs={{0,128},{128,0},{1,129},{129,1},{2,130},{130,2},{3,131},{131,3},{4... | collective-permute-start | bytes 196616 | tf_op jit(solution)/shard_map/ppermute | solution.py:323
  24.9 0.2 shard_map.138
  25.2 0.7 collective-permute-done.other_ref
  25.8 0.1 shard_map.139
  25.9 3.0 %collective-permute-start.3 = (bf16[80,256]{1,0:T(8,128)(2,1)S(1)}, bf16[80,256]{1,0:T(8,128)(2,1)S(1)}, u32[]{:S(2)}, u32[]{:S(2)}) collective-permute-start(bf16[80,256]{1,0:T(8,128)(2,1)S(1)} %get-tuple-element.34), channel_id=1, source_target_pairs={{0,2},{1,3},{2,0},{3,1},{4,6},{5,7},{6,4},{7,5},{8,10},{9,11},{10,... | collective-permute-start | bytes 122888 | tf_op jit(solution)/shard_map/ppermute | solution.py:327
  29.0 0.8 %collective-permute-start.2 = (bf16[80,256]{1,0:T(8,128)(2,1)S(1)}, bf16[80,256]{1,0:T(8,128)(2,1)S(1)}, u32[]{:S(2)}, u32[]{:S(2)}) collective-permute-start(bf16[80,256]{1,0:T(8,128)(2,1)S(1)} %get-tuple-element.34), channel_id=1, source_target_pairs={{0,3},{1,0},{2,1},{3,2},{4,7},{5,4},{6,5},{7,6},{8,11},{9,8},{10,9... | collective-permute-start | bytes 122888 | tf_op jit(solution)/shard_map/ppermute | solution.py:327
  29.7 0.7 collective-permute-start.1
  30.4 0.0 collective-permute-done.3.c_ref
  30.4 1.6 %collective-permute-done.2.b_ref = bf16[80,256]{1,0:T(8,128)(2,1)S(1)} collective-permute-done((bf16[80,256]{1,0:T(8,128)(2,1)S(1)}, bf16[80,256]{1,0:T(8,128)(2,1)S(1)}, u32[]{:S(2)}, u32[]{:S(2)}) %collective-permute-start.2) | collective-permute-done | bytes 40992 | tf_op jit(solution)/shard_map/ppermute | solution.py:327
  32.0 1.8 %collective-permute-done.1.a_ref = bf16[80,256]{1,0:T(8,128)(2,1)S(1)} collective-permute-done((bf16[80,256]{1,0:T(8,128)(2,1)S(1)}, bf16[80,256]{1,0:T(8,128)(2,1)S(1)}, u32[]{:S(2)}, u32[]{:S(2)}) %collective-permute-start.1) | collective-permute-done | bytes 40992 | tf_op jit(solution)/shard_map/ppermute | solution.py:327
  33.8 0.5 shard_map.140
  34.3 13.4 %all_to_all.16.in_ref = bf16[32,16,256]{2,1,0:T(8,128)(2,1)S(1)} all-to-all(bf16[32,16,256]{2,1,0:T(8,128)(2,1)S(1)} %get-tuple-element.36), channel_id=1, replica_groups=mesh['side'=2,'grp'=32,'tp'=4] {'grp'}, dimensions={0} | all-to-all | bytes 524288 | tf_op jit(solution)/shard_map/all_to_all | solution.py:337
  47.7 0.1 shard_map.141.x_ref
  47.8 3.7 %collective-permute-start.4 = (bf16[16,6272]{1,0:T(8,128)(2,1)S(1)}, bf16[16,6272]{1,0:T(8,128)(2,1)S(1)}, u32[]{:S(2)}, u32[]{:S(2)}) collective-permute-start(bf16[16,6272]{1,0:T(8,128)(2,1)S(1)} %shard_map.141.x_ref), channel_id=1, source_target_pairs={{0,128},{128,0},{1,129},{129,1},{2,130},{130,2},{3,131},{131,3},{4... | collective-permute-start | bytes 602120 | tf_op jit(solution)/shard_map/ppermute | solution.py:343
  51.5 1.1 %collective-permute-done.4.x2_ref = bf16[16,6272]{1,0:T(8,128)(2,1)S(1)} collective-permute-done((bf16[16,6272]{1,0:T(8,128)(2,1)S(1)}, bf16[16,6272]{1,0:T(8,128)(2,1)S(1)}, u32[]{:S(2)}, u32[]{:S(2)}) %collective-permute-start.4) | collective-permute-done | bytes 200736 | tf_op jit(solution)/shard_map/ppermute | solution.py:343
  52.6 2.7 %shard_map.142 = (f32[16,6144]{1,0:T(8,128)S(1)}, bf16[16,6144]{1,0:T(8,128)(2,1)S(1)}) custom-call(bf16[16,6272]{1,0:T(8,128)(2,1)S(1)} %shard_map.141.x_ref, bf16[16,6272]{1,0:T(8,128)(2,1)S(1)} %collective-permute-done.4.x2_ref, bf16[288,6144]{1,0:T(8,128)(2,1)S(1)} %bitcast.12, bf16[288,6144]{1,0:T(8,128)(2,1)S(1)} %bitcast.13, ...), custom_call_target="tpu_custom_call" | custom-call | flops 400000000 | bytes 11000000 | tf_op jit(solution)/shard_map/pallas_call | solution.py:257
  55.4 0.4 collective-permute-start.5
  55.8 1.1 %collective-permute-done.5.other_ref = bf16[16,6144]{1,0:T(8,128)(2,1)S(1)} collective-permute-done((bf16[16,6144]{1,0:T(8,128)(2,1)S(1)}, bf16[16,6144]{1,0:T(8,128)(2,1)S(1)}, u32[]{:S(2)}, u32[]{:S(2)}) %collective-permute-start.5) | collective-permute-done | bytes 196640 | tf_op jit(solution)/shard_map/ppermute | solution.py:352
  56.9 0.1 shard_map.143
  56.9 19.4 %all_to_all.17.x_ref = bf16[128,8,128]{2,1,0:T(8,128)(2,1)S(1)} all-to-all(bf16[128,8,128]{2,1,0:T(8,128)(2,1)S(1)} %shard_map.143), channel_id=1, replica_groups=mesh['side'=2,'grp'=32,'tp'=4] {'grp','tp'}, dimensions={0} | all-to-all | bytes 524288 | tf_op jit(solution)/shard_map/all_to_all | solution.py:356
  76.3 0.9 %shard_map.144 = bf16[16,192]{1,0:T(8,128)(2,1)} custom-call(bf16[128,8,128]{2,1,0:T(8,128)(2,1)S(1)} %all_to_all.17.x_ref, bf16[96,1024]{1,0:T(8,128)(2,1)S(1)} %get-tuple-element.39.table_ref, f32[16,256]{1,0:T(8,128)S(1)} %get-tuple-element.40.own_ref), custom_call_target="tpu_custom_call" | custom-call | flops 30000000 | bytes 500000 | tf_op jit(solution)/shard_map/pallas_call | solution.py:257
  (6 shorter events, 0.0 us)
Async XLA Ops:
  22.8 3.0 %collective-permute-start = (f32[64,256]{1,0:T(8,128)S(1)}, f32[64,256]{1,0:T(8,128)S(1)}, u32[]{:S(2)}, u32[]{:S(2)}) collective-permute-start(f32[64,256]{1,0:T(8,128)S(1)} %get-tuple-element.27.after_ref), channel_id=1, source_target_pairs={{0,128},{128,0},{1,129},{129,1},{2,130},{130,2},{3,131},{131,3},{4... | collective-permute-start | bytes 196616 | tf_op jit(solution)/shard_map/ppermute | solution.py:323
  25.8 26.8 %copy-start = (bf16[1,6144,288]{1,2,0:T(8,128)(2,1)S(1)}, bf16[1,6144,288]{1,2,0:T(8,128)(2,1)}, u32[]{:S(2)}) copy-start(bf16[1,6144,288]{1,2,0:T(8,128)(2,1)} %param.23) | copy-start | bytes 10616836
  25.8 26.8 %copy-start.1 = (bf16[1,6144,288]{1,2,0:T(8,128)(2,1)S(1)}, bf16[1,6144,288]{1,2,0:T(8,128)(2,1)}, u32[]{:S(2)}) copy-start(bf16[1,6144,288]{1,2,0:T(8,128)(2,1)} %param.24) | copy-start | bytes 10616836
  25.8 26.8 %copy-start.2 = (bf16[1,288,6144]{2,1,0:T(8,128)(2,1)S(1)}, bf16[1,288,6144]{2,1,0:T(8,128)(2,1)}, u32[]{:S(2)}) copy-start(bf16[1,288,6144]{2,1,0:T(8,128)(2,1)} %param.25) | copy-start | bytes 10616836
  25.9 4.5 %collective-permute-start.3 = (bf16[80,256]{1,0:T(8,128)(2,1)S(1)}, bf16[80,256]{1,0:T(8,128)(2,1)S(1)}, u32[]{:S(2)}, u32[]{:S(2)}) collective-permute-start(bf16[80,256]{1,0:T(8,128)(2,1)S(1)} %get-tuple-element.34), channel_id=1, source_target_pairs={{0,2},{1,3},{2,0},{3,1},{4,6},{5,7},{6,4},{7,5},{8,10},{9,11},{10,... | collective-permute-start | bytes 122888 | tf_op jit(solution)/shard_map/ppermute | solution.py:327
  29.0 3.0 %collective-permute-start.2 = (bf16[80,256]{1,0:T(8,128)(2,1)S(1)}, bf16[80,256]{1,0:T(8,128)(2,1)S(1)}, u32[]{:S(2)}, u32[]{:S(2)}) collective-permute-start(bf16[80,256]{1,0:T(8,128)(2,1)S(1)} %get-tuple-element.34), channel_id=1, source_target_pairs={{0,3},{1,0},{2,1},{3,2},{4,7},{5,4},{6,5},{7,6},{8,11},{9,8},{10,9... | collective-permute-start | bytes 122888 | tf_op jit(solution)/shard_map/ppermute | solution.py:327
  29.7 4.1 %collective-permute-start.1 = (bf16[80,256]{1,0:T(8,128)(2,1)S(1)}, bf16[80,256]{1,0:T(8,128)(2,1)S(1)}, u32[]{:S(2)}, u32[]{:S(2)}) collective-permute-start(bf16[80,256]{1,0:T(8,128)(2,1)S(1)} %get-tuple-element.34), channel_id=1, source_target_pairs={{0,1},{1,2},{2,3},{3,0},{4,5},{5,6},{6,7},{7,4},{8,9},{9,10},{10,1... | collective-permute-start | bytes 122888 | tf_op jit(solution)/shard_map/ppermute | solution.py:327
  47.8 4.8 %collective-permute-start.4 = (bf16[16,6272]{1,0:T(8,128)(2,1)S(1)}, bf16[16,6272]{1,0:T(8,128)(2,1)S(1)}, u32[]{:S(2)}, u32[]{:S(2)}) collective-permute-start(bf16[16,6272]{1,0:T(8,128)(2,1)S(1)} %shard_map.141.x_ref), channel_id=1, source_target_pairs={{0,128},{128,0},{1,129},{129,1},{2,130},{130,2},{3,131},{131,3},{4... | collective-permute-start | bytes 602120 | tf_op jit(solution)/shard_map/ppermute | solution.py:343
  55.4 1.5 %collective-permute-start.5 = (bf16[16,6144]{1,0:T(8,128)(2,1)S(1)}, bf16[16,6144]{1,0:T(8,128)(2,1)S(1)}, u32[]{:S(2)}, u32[]{:S(2)}) collective-permute-start(bf16[16,6144]{1,0:T(8,128)(2,1)S(1)} %get-tuple-element.38), channel_id=1, source_target_pairs={{0,128},{128,0},{1,129},{129,1},{2,130},{130,2},{3,131},{131,3},{4... | collective-permute-start | bytes 589832 | tf_op jit(solution)/shard_map/ppermute | solution.py:352

commit v9 on v8

--- a/solution.py
+++ b/solution.py
@@ -153,8 +153,8 @@
     slot = jnp.dot(earlier, chosen.astype(bf16), preferred_element_type=f32)
     block = iota((half, 1), 0) // RB
     here = (slot == (place % CAP).astype(f32)) & (block == place // CAP % 4)
-    table = jnp.transpose(jnp.where(here, chosen, 0.0)).astype(bf16)
-    routed = jnp.dot(table, rows, preferred_element_type=f32).astype(bf16)
+    table = jnp.where(here, chosen, 0.0).astype(bf16)
+    routed = lax.dot_general(table, rows, (((0,), (0,)), ((), ())), preferred_element_type=f32).astype(bf16)
     for e in range(EXPERTS):
         piece = routed[e * 4 * CAP : (e + 1) * 4 * CAP]
         out_ref[2 * e] = piece

time: 77.4 us -> 77.4 us (level)
  no operation moved by 1% of the time
where the time goes in v9:
time: 77.4 us; the launch traced here: 77.2 us
  blocking collectives  53.8 us (70%)
  starting transfers between devices  10.8 us (14%)
  Pallas kernels  6.33 us (8%)
  waiting for transfers between devices  6.17 us (8%)
    all_to_all x1, blocking collectives, body(): every = lax.all_to_all(sent, 'grp', 0, 0, tiled=True)  21 us
    all_to_all x1, blocking collectives, body(): returned = lax.all_to_all(back, ('grp', 'tp'), 0, 0, tiled=True)  19.4 us
    all_to_all x1, blocking collectives, body(): inbox = lax.all_to_all(outbox, 'grp', 0, 0, tiled=True)  13.4 us
    pallas_call x9, Pallas kernels, call(): return made(*args)  6.33 us
    ppermute x3, starting transfers between devices, body(): lax.ppermute(message, 'tp', [(t, (t + step) % 4) for t in range(4)])  4.51 us
    ppermute x1, starting transfers between devices, body(): lax.ppermute(x_mine, 'side', swap)  3.72 us
    ppermute x3, waiting for transfers between devices, body(): lax.ppermute(message, 'tp', [(t, (t + step) % 4) for t in range(4)])  3.37 us
    ppermute x2, starting transfers between devices, body(): lax.ppermute(give, 'side', swap)  2.58 us
  transfers between devices with their start and end apart: 6, of which 5 were waited for; matrix products, arithmetic and copies ran while one was open for 0% of the time, Pallas kernels for 0%

profile of v9, /device:TPU:1, one launch (start us, length us, event | category | flops | bytes accessed | tf_op | source)
XLA Modules:
  0.0 77.2 jit_solution(7706259048720659910)
XLA Ops:
  0.0 1.5 %shard_map.136 = (bf16[32,16,128]{2,1,0:T(8,128)(2,1)S(1)}, f32[4,128]{1,0:T(4,128)S(1)}, bf16[192,512]{1,0:T(8,128)(2,1)S(1)}, bf16[16,192]{1,0:T(8,128)(2,1)S(...) custom-call(bf16[4,4,128]{2,1,0:T(4,128)(2,1)} %q_hbm.1, bf16[4,4,128]{2,1,0:T(4,128)(2,1)} %k_hbm.1, ...), custom_call_target="tpu_custom_call" | custom-call | flops 1000000 | bytes 1200000 | tf_op jit(solution)/shard_map/pallas_call | solution.py:257
  1.5 21.0 %all_to_all.15.x_ref = bf16[32,16,128]{2,1,0:T(8,128)(2,1)S(1)} all-to-all(bf16[32,16,128]{2,1,0:T(8,128)(2,1)S(1)} %get-tuple-element.23), channel_id=1, replica_groups=mesh['side'=2,'grp'=32,'tp'=4] {'grp'}, dimensions={0} | all-to-all | bytes 262144 | tf_op jit(solution)/shard_map/all_to_all | solution.py:301
  22.5 0.2 shard_map.137
  22.8 2.1 %collective-permute-start = (f32[64,256]{1,0:T(8,128)S(1)}, f32[64,256]{1,0:T(8,128)S(1)}, u32[]{:S(2)}, u32[]{:S(2)}) collective-permute-start(f32[64,256]{1,0:T(8,128)S(1)} %get-tuple-element.27.after_ref), channel_id=1, source_target_pairs={{0,128},{128,0},{1,129},{129,1},{2,130},{130,2},{3,131},{131,3},{4... | collective-permute-start | bytes 196616 | tf_op jit(solution)/shard_map/ppermute | solution.py:323
  24.9 0.2 shard_map.138
  25.2 0.7 collective-permute-done.other_ref
  25.8 0.1 shard_map.139
  25.9 3.0 %collective-permute-start.3 = (bf16[80,256]{1,0:T(8,128)(2,1)S(1)}, bf16[80,256]{1,0:T(8,128)(2,1)S(1)}, u32[]{:S(2)}, u32[]{:S(2)}) collective-permute-start(bf16[80,256]{1,0:T(8,128)(2,1)S(1)} %get-tuple-element.34), channel_id=1, source_target_pairs={{0,2},{1,3},{2,0},{3,1},{4,6},{5,7},{6,4},{7,5},{8,10},{9,11},{10,... | collective-permute-start | bytes 122888 | tf_op jit(solution)/shard_map/ppermute | solution.py:327
  29.0 0.8 %collective-permute-start.2 = (bf16[80,256]{1,0:T(8,128)(2,1)S(1)}, bf16[80,256]{1,0:T(8,128)(2,1)S(1)}, u32[]{:S(2)}, u32[]{:S(2)}) collective-permute-start(bf16[80,256]{1,0:T(8,128)(2,1)S(1)} %get-tuple-element.34), channel_id=1, source_target_pairs={{0,3},{1,0},{2,1},{3,2},{4,7},{5,4},{6,5},{7,6},{8,11},{9,8},{10,9... | collective-permute-start | bytes 122888 | tf_op jit(solution)/shard_map/ppermute | solution.py:327
  29.7 0.7 collective-permute-start.1
  30.4 0.0 collective-permute-done.3.c_ref
  30.4 1.6 %collective-permute-done.2.b_ref = bf16[80,256]{1,0:T(8,128)(2,1)S(1)} collective-permute-done((bf16[80,256]{1,0:T(8,128)(2,1)S(1)}, bf16[80,256]{1,0:T(8,128)(2,1)S(1)}, u32[]{:S(2)}, u32[]{:S(2)}) %collective-permute-start.2) | collective-permute-done | bytes 40992 | tf_op jit(solution)/shard_map/ppermute | solution.py:327
  32.0 1.8 %collective-permute-done.1.a_ref = bf16[80,256]{1,0:T(8,128)(2,1)S(1)} collective-permute-done((bf16[80,256]{1,0:T(8,128)(2,1)S(1)}, bf16[80,256]{1,0:T(8,128)(2,1)S(1)}, u32[]{:S(2)}, u32[]{:S(2)}) %collective-permute-start.1) | collective-permute-done | bytes 40992 | tf_op jit(solution)/shard_map/ppermute | solution.py:327
  33.8 0.5 shard_map.140
  34.3 13.4 %all_to_all.16.in_ref = bf16[32,16,256]{2,1,0:T(8,128)(2,1)S(1)} all-to-all(bf16[32,16,256]{2,1,0:T(8,128)(2,1)S(1)} %get-tuple-element.36), channel_id=1, replica_groups=mesh['side'=2,'grp'=32,'tp'=4] {'grp'}, dimensions={0} | all-to-all | bytes 524288 | tf_op jit(solution)/shard_map/all_to_all | solution.py:337
  47.7 0.1 shard_map.141.x_ref
  47.8 3.7 %collective-permute-start.4 = (bf16[16,6272]{1,0:T(8,128)(2,1)S(1)}, bf16[16,6272]{1,0:T(8,128)(2,1)S(1)}, u32[]{:S(2)}, u32[]{:S(2)}) collective-permute-start(bf16[16,6272]{1,0:T(8,128)(2,1)S(1)} %shard_map.141.x_ref), channel_id=1, source_target_pairs={{0,128},{128,0},{1,129},{129,1},{2,130},{130,2},{3,131},{131,3},{4... | collective-permute-start | bytes 602120 | tf_op jit(solution)/shard_map/ppermute | solution.py:343
  51.5 1.1 %collective-permute-done.4.x2_ref = bf16[16,6272]{1,0:T(8,128)(2,1)S(1)} collective-permute-done((bf16[16,6272]{1,0:T(8,128)(2,1)S(1)}, bf16[16,6272]{1,0:T(8,128)(2,1)S(1)}, u32[]{:S(2)}, u32[]{:S(2)}) %collective-permute-start.4) | collective-permute-done | bytes 200736 | tf_op jit(solution)/shard_map/ppermute | solution.py:343
  52.6 2.7 %shard_map.142 = (f32[16,6144]{1,0:T(8,128)S(1)}, bf16[16,6144]{1,0:T(8,128)(2,1)S(1)}) custom-call(bf16[16,6272]{1,0:T(8,128)(2,1)S(1)} %shard_map.141.x_ref, bf16[16,6272]{1,0:T(8,128)(2,1)S(1)} %collective-permute-done.4.x2_ref, bf16[288,6144]{1,0:T(8,128)(2,1)S(1)} %bitcast.12, bf16[288,6144]{1,0:T(8,128)(2,1)S(1)} %bitcast.13, ...), custom_call_target="tpu_custom_call" | custom-call | flops 400000000 | bytes 11000000 | tf_op jit(solution)/shard_map/pallas_call | solution.py:257
  55.3 0.4 collective-permute-start.5
  55.8 1.1 %collective-permute-done.5.other_ref = bf16[16,6144]{1,0:T(8,128)(2,1)S(1)} collective-permute-done((bf16[16,6144]{1,0:T(8,128)(2,1)S(1)}, bf16[16,6144]{1,0:T(8,128)(2,1)S(1)}, u32[]{:S(2)}, u32[]{:S(2)}) %collective-permute-start.5) | collective-permute-done | bytes 196640 | tf_op jit(solution)/shard_map/ppermute | solution.py:352
  56.8 0.1 shard_map.143
  56.9 19.4 %all_to_all.17.x_ref = bf16[128,8,128]{2,1,0:T(8,128)(2,1)S(1)} all-to-all(bf16[128,8,128]{2,1,0:T(8,128)(2,1)S(1)} %shard_map.143), channel_id=1, replica_groups=mesh['side'=2,'grp'=32,'tp'=4] {'grp','tp'}, dimensions={0} | all-to-all | bytes 524288 | tf_op jit(solution)/shard_map/all_to_all | solution.py:356
  76.3 0.9 %shard_map.144 = bf16[16,192]{1,0:T(8,128)(2,1)} custom-call(bf16[128,8,128]{2,1,0:T(8,128)(2,1)S(1)} %all_to_all.17.x_ref, bf16[96,1024]{1,0:T(8,128)(2,1)S(1)} %get-tuple-element.39.table_ref, f32[16,256]{1,0:T(8,128)S(1)} %get-tuple-element.40.own_ref), custom_call_target="tpu_custom_call" | custom-call | flops 30000000 | bytes 500000 | tf_op jit(solution)/shard_map/pallas_call | solution.py:257
  (6 shorter events, 0.0 us)
Async XLA Ops:
  22.8 3.0 %collective-permute-start = (f32[64,256]{1,0:T(8,128)S(1)}, f32[64,256]{1,0:T(8,128)S(1)}, u32[]{:S(2)}, u32[]{:S(2)}) collective-permute-start(f32[64,256]{1,0:T(8,128)S(1)} %get-tuple-element.27.after_ref), channel_id=1, source_target_pairs={{0,128},{128,0},{1,129},{129,1},{2,130},{130,2},{3,131},{131,3},{4... | collective-permute-start | bytes 196616 | tf_op jit(solution)/shard_map/ppermute | solution.py:323
  25.8 26.8 %copy-start = (bf16[1,6144,288]{1,2,0:T(8,128)(2,1)S(1)}, bf16[1,6144,288]{1,2,0:T(8,128)(2,1)}, u32[]{:S(2)}) copy-start(bf16[1,6144,288]{1,2,0:T(8,128)(2,1)} %param.23) | copy-start | bytes 10616836
  25.8 26.8 %copy-start.1 = (bf16[1,6144,288]{1,2,0:T(8,128)(2,1)S(1)}, bf16[1,6144,288]{1,2,0:T(8,128)(2,1)}, u32[]{:S(2)}) copy-start(bf16[1,6144,288]{1,2,0:T(8,128)(2,1)} %param.24) | copy-start | bytes 10616836
  25.8 26.8 %copy-start.2 = (bf16[1,288,6144]{2,1,0:T(8,128)(2,1)S(1)}, bf16[1,288,6144]{2,1,0:T(8,128)(2,1)}, u32[]{:S(2)}) copy-start(bf16[1,288,6144]{2,1,0:T(8,128)(2,1)} %param.25) | copy-start | bytes 10616836
  25.9 4.5 %collective-permute-start.3 = (bf16[80,256]{1,0:T(8,128)(2,1)S(1)}, bf16[80,256]{1,0:T(8,128)(2,1)S(1)}, u32[]{:S(2)}, u32[]{:S(2)}) collective-permute-start(bf16[80,256]{1,0:T(8,128)(2,1)S(1)} %get-tuple-element.34), channel_id=1, source_target_pairs={{0,2},{1,3},{2,0},{3,1},{4,6},{5,7},{6,4},{7,5},{8,10},{9,11},{10,... | collective-permute-start | bytes 122888 | tf_op jit(solution)/shard_map/ppermute | solution.py:327
  29.0 3.0 %collective-permute-start.2 = (bf16[80,256]{1,0:T(8,128)(2,1)S(1)}, bf16[80,256]{1,0:T(8,128)(2,1)S(1)}, u32[]{:S(2)}, u32[]{:S(2)}) collective-permute-start(bf16[80,256]{1,0:T(8,128)(2,1)S(1)} %get-tuple-element.34), channel_id=1, source_target_pairs={{0,3},{1,0},{2,1},{3,2},{4,7},{5,4},{6,5},{7,6},{8,11},{9,8},{10,9... | collective-permute-start | bytes 122888 | tf_op jit(solution)/shard_map/ppermute | solution.py:327
  29.7 4.1 %collective-permute-start.1 = (bf16[80,256]{1,0:T(8,128)(2,1)S(1)}, bf16[80,256]{1,0:T(8,128)(2,1)S(1)}, u32[]{:S(2)}, u32[]{:S(2)}) collective-permute-start(bf16[80,256]{1,0:T(8,128)(2,1)S(1)} %get-tuple-element.34), channel_id=1, source_target_pairs={{0,1},{1,2},{2,3},{3,0},{4,5},{5,6},{6,7},{7,4},{8,9},{9,10},{10,1... | collective-permute-start | bytes 122888 | tf_op jit(solution)/shard_map/ppermute | solution.py:327
  47.8 4.8 %collective-permute-start.4 = (bf16[16,6272]{1,0:T(8,128)(2,1)S(1)}, bf16[16,6272]{1,0:T(8,128)(2,1)S(1)}, u32[]{:S(2)}, u32[]{:S(2)}) collective-permute-start(bf16[16,6272]{1,0:T(8,128)(2,1)S(1)} %shard_map.141.x_ref), channel_id=1, source_target_pairs={{0,128},{128,0},{1,129},{129,1},{2,130},{130,2},{3,131},{131,3},{4... | collective-permute-start | bytes 602120 | tf_op jit(solution)/shard_map/ppermute | solution.py:343
  55.3 1.5 %collective-permute-start.5 = (bf16[16,6144]{1,0:T(8,128)(2,1)S(1)}, bf16[16,6144]{1,0:T(8,128)(2,1)S(1)}, u32[]{:S(2)}, u32[]{:S(2)}) collective-permute-start(bf16[16,6144]{1,0:T(8,128)(2,1)S(1)} %get-tuple-element.38), channel_id=1, source_target_pairs={{0,128},{128,0},{1,129},{129,1},{2,130},{130,2},{3,131},{131,3},{4... | collective-permute-start | bytes 589832 | tf_op jit(solution)/shard_map/ppermute | solution.py:352
